TPU v7x, 1024 devices: a whole 4x4x32 slice. The times are simulated.
1024 devices in a mesh: replica: 64 (over z_lo, x), mp: 16 (over y, z_hi, core).
Axes of the slice: x: 4, y: 4, z: 32 (z_hi: 2, z_lo: 16; z = z_hi * 16 + z_lo), core: 2. Of those that a mesh axis runs over, the one named last changes fastest.
Arguments:
- local_weights: bfloat16 [64, 256, 28672], P('replica', None, 'mp'), may hold values from -16 to 16
- outer_base: float32 [256, 28672], P(None, 'mp'), may hold values from -6 to 6
- outer_momentum: float32 [256, 28672], P(None, 'mp'), may hold values from -6 to 6
- tokens: bfloat16 [65536, 8192], P('replica', 'mp'), may hold values from -6 to 6
- key_value_weight: bfloat16 [8192, 2048], P('mp'), may hold values from -0.09375 to 0.09375
Outputs:
- updated_base: float32 [256, 28672], P('replica', 'mp')
- updated_momentum: float32 [256, 28672], P('replica', 'mp')
- synced_weights: bfloat16 [256, 28672], P(None, 'mp')
- keys_values: bfloat16 [65536, 2048], P('replica', 'mp')
All inputs are finite; a program needn't handle non-finite values.
Results may differ from a plain program's by a relative error of at most 0.017.
Values may be sent and summed in bfloat16 or wider, within the bound.
No kernel may reach another device: no remote copies, remote signals or barrier semaphores. Data moves between devices by JAX's collectives and lax.ppermute only.
A program may use at most 64 MiB of HBM per device.

v0:
```python
import jax
import jax.numpy as jnp
from jax import lax
from jax.sharding import PartitionSpec as P


def nesterov_step(summed, base_part, momentum_part, groups):
    anchor = lax.optimization_barrier(base_part.astype(jnp.bfloat16)).astype(jnp.float32)
    outer_grad = anchor - summed / groups
    new_momentum = 0.9 * momentum_part + outer_grad
    new_base = base_part - 0.7 * (outer_grad + 0.9 * new_momentum)
    return (new_base, new_momentum)


def shards(local_weights, outer_base, outer_momentum, tokens, key_value_weight):
    local_terms = local_weights[0].astype(jnp.float32)
    groups = lax.axis_size("replica")
    partial_value = jnp.dot(tokens, key_value_weight, preferred_element_type=jnp.float32).astype(
        jnp.bfloat16
    )
    keys_values = (
        lax.psum_scatter(partial_value, "mp", scatter_dimension=1, tiled=True)
        .astype(jnp.float32)
        .astype(jnp.bfloat16)
    )
    summed = lax.psum(local_terms, "replica")
    full_base, full_momentum = nesterov_step(summed, outer_base, outer_momentum, groups)
    synced_weights = full_base.astype(jnp.bfloat16)
    row_count = full_base.shape[0] // groups
    row_start = lax.axis_index("replica") * row_count
    updated_base = lax.dynamic_slice_in_dim(full_base, row_start, row_count, 0)
    updated_momentum = lax.dynamic_slice_in_dim(full_momentum, row_start, row_count, 0)
    return (updated_base, updated_momentum, synced_weights, keys_values)


def solution(mesh):
    return jax.shard_map(
        shards,
        mesh=mesh,
        in_specs=(
            P("replica", None, "mp"),
            P(None, "mp"),
            P(None, "mp"),
            P("replica", "mp"),
            P("mp", None),
        ),
        out_specs=(P("replica", "mp"), P("replica", "mp"), P(None, "mp"), P("replica", "mp")),
        check_vma=False,
    )
```

profile of v0, /device:TPU:8, one launch (start us, length us, event | category | flops | bytes accessed | tf_op | source)
XLA Modules:
  0.0 1585.7 jit_solution(10988806426096170562)
XLA Ops:
  8.0 0.0 copy-start
  8.0 0.0 copy-start.1
  8.0 0.0 all-reduce.2.cloned.1.call-start
  8.1 2.7 bitcast_convert_fusion
  10.7 0.0 all-reduce.2.cloned.1.call-update
  10.8 0.0 reduce-scatter.4.cloned.1.call-start
  10.8 0.0 copy-done
  10.8 0.0 copy-done.1
  10.8 4.3 convolution_convert_fusion
  15.2 6.4 copy.9
  21.5 0.0 reduce-scatter.4.cloned.1.call-update
  21.6 1.6 convert_element_type.20
  23.2 1548.6 %all-reduce.2.cloned.1.call-done = f32[256,1792]{1,0:T(8,128)} async-done(((f32[256,1792]{1,0:T(8,128)}), f32[256,1792]{1,0:T(8,128)}) %all-reduce.2.cloned.1.call-update) | async-done | bytes 1835024 | tf_op jit(solution)/shard_map/psum | solution.py:26
  1571.7 4.1 fusion
  1575.8 0.6 constant_dynamic-slice_fusion
  1576.5 0.0 reduce-scatter.4.cloned.1.call-done
  1576.5 1.8 copy.10
Async XLA Ops:
  8.0 2.8 copy-start
  8.0 2.8 copy-start.1
  8.0 1563.7 %all-reduce.2.cloned.1.call-start = ((), (), s32[]{:S(2)}) async-start(), calls=%async_computation.1 | async-start | bytes 3670016 | tf_op jit(solution)/shard_map/psum | solution.py:26
  10.8 1565.7 %reduce-scatter.4.cloned.1.call-start = ((), (), s32[]{:S(2)}) async-start(), calls=%async_computation.2 | async-start | bytes 4456448
Sparse Core Ops, SparseCore 0:
  12.4 1559.3 all-reduce.1
Sparse Core Ops, SparseCore 1:
  21.6 263.9 reduce-scatter.3
where the time goes:
time: 1590 us
  waiting for transfers between devices  1550 us (97%)
    psum x1, waiting for transfers between devices, shards(): summed = lax.psum(local_terms, 'replica')  1550 us
  transfers between devices with their start and end apart: 2, of which 1 were waited for; matrix products, arithmetic and copies ran while one was open for 1% of the time, Pallas kernels for 0%

commit v1 on v0

v1 whole, which is shorter than its diff:
```python
import jax
import jax.numpy as jnp
from jax import lax
from jax.experimental import pallas as pl
from jax.experimental.pallas import tpu as pltpu
from jax.sharding import Mesh, PartitionSpec as P

SIZES = (4, 4, 4, 4, 2, 2)
NAMES = ("zo", "zi", "x", "y", "h", "c")
LANES = 128
CHUNKS = 2

bf16 = jnp.bfloat16
f32 = jnp.float32


def shift(axis, size, step):
    return [(i, (i + step) % size) for i in range(size)]


def column(block, h, c):
    return pl.multiple_of((block * 4 + h * 2 + c) * LANES, LANES)


def pack_kernel(blocks, place_ref, weight_ref, packed_ref):
    h, c = place_ref[0], place_ref[1]
    for block in range(blocks):
        for k, side in enumerate((h, 1 - h)):
            to = (2 * block + k) * LANES
            packed_ref[:, to : to + LANES] = weight_ref[:, pl.ds(column(block, side, 1 - c), LANES)]


def project_kernel(blocks, place_ref, own_ref, sibling_ref, weight_ref, packed_ref, out_ref):
    h, c = place_ref[0], place_ref[1]
    own, sibling = own_ref[...], sibling_ref[...]
    for block in range(blocks):
        mine = jnp.concatenate(
            [weight_ref[:, pl.ds(column(block, side, c), LANES)] for side in (h, 1 - h)], axis=1
        )
        width = 2 * LANES
        total = jnp.dot(own, mine, preferred_element_type=f32)
        total += jnp.dot(
            sibling, packed_ref[:, block * width : (block + 1) * width], preferred_element_type=f32
        )
        out_ref[block] = total.astype(bf16)


def pack(place, weight, blocks):
    depth, width = weight.shape
    return pl.pallas_call(
        lambda *refs: pack_kernel(blocks, *refs),
        out_shape=jax.ShapeDtypeStruct((depth, width // 2), bf16),
        grid_spec=pltpu.PrefetchScalarGridSpec(
            num_scalar_prefetch=1,
            grid=(2,),
            in_specs=[pl.BlockSpec((depth // 2, width), lambda i, _: (i, 0))],
            out_specs=pl.BlockSpec((depth // 2, width // 2), lambda i, _: (i, 0)),
        ),
        cost_estimate=pl.CostEstimate(flops=0, bytes_accessed=weight.size * 3, transcendentals=0),
        compiler_params=pltpu.CompilerParams(vmem_limit_bytes=32 << 20),
    )(place, weight)


def project(place, own, sibling, weight, packed, blocks, chunk, rows):
    depth, width = weight.shape
    tile = min(rows, 256)
    first = chunk * (rows // tile)
    return pl.pallas_call(
        lambda *refs: project_kernel(blocks, *refs),
        out_shape=jax.ShapeDtypeStruct((blocks, rows, 2 * LANES), bf16),
        grid_spec=pltpu.PrefetchScalarGridSpec(
            num_scalar_prefetch=1,
            grid=(rows // tile,),
            in_specs=[
                pl.BlockSpec((tile, depth), lambda i, _: (first + i, 0)),
                pl.BlockSpec((tile, depth), lambda i, _: (first + i, 0)),
                pl.BlockSpec((depth, width), lambda i, _: (0, 0)),
                pl.BlockSpec((depth, width // 2), lambda i, _: (0, 0)),
            ],
            out_specs=pl.BlockSpec((blocks, tile, 2 * LANES), lambda i, _: (0, i, 0)),
        ),
        cost_estimate=pl.CostEstimate(
            flops=2 * rows * depth * width, bytes_accessed=rows * depth * 8 + weight.size * 3, transcendentals=0
        ),
        compiler_params=pltpu.CompilerParams(vmem_limit_bytes=32 << 20),
    )(place, own, sibling, weight, packed)


def after(array, *earlier):
    return lax.optimization_barrier((array, *earlier))[0]


def one_hot(source, count):
    return (source[:, None] == jnp.arange(count, dtype=jnp.int32)[None, :]).astype(bf16)


def select_rows(source, array):
    return jnp.dot(one_hot(source, array.shape[0]), array, preferred_element_type=f32).astype(bf16)


def gather_small(array, axis, size):
    copies = jnp.broadcast_to(array, (size, *array.shape))
    return lax.all_to_all(copies, axis, split_axis=0, concat_axis=0, tiled=True)


def shards(local_weights, base, momentum, tokens, weight):
    sizes = dict(zip(NAMES, SIZES))
    zo, zi, x, h, c = (lax.axis_index(a) for a in ("zo", "zi", "x", "h", "c"))
    n_zo, n_zi, n_x, n_y = (sizes[a] for a in ("zo", "zi", "x", "y"))
    swap = [(0, 1), (1, 0)]
    terms = local_weights[0]

    place = jnp.stack([h, c]).astype(jnp.int32)
    sibling = lax.ppermute(tokens, "c", swap)
    packed = pack(place, weight, n_y)
    terms = after(terms, packed)
    packed = lax.ppermute(packed, "c", swap)

    groups = n_zo * n_zi * n_x
    rows, width = base.shape
    own = rows // groups
    per_x = rows // n_x
    at = jnp.arange(per_x, dtype=jnp.int32)
    in_zi, in_zo, in_own = at // (n_zo * own), (at // own) % n_zo, at % own

    def rows_of(at_x):
        return ((in_zo * n_zi + in_zi) * n_x + at_x) * own + in_own

    received = []
    for step in range(1, n_x):
        sent = select_rows(rows_of((x + step) % n_x), terms)
        received.append(lax.ppermute(sent, "x", shift("x", n_x, step)))

    count = tokens.shape[0] // CHUNKS

    def over_y(chunk, *earlier):
        part = project(place, tokens, sibling, weight, packed, n_y, chunk, count)
        part = after(part, *earlier)
        part = lax.all_to_all(part, "y", split_axis=0, concat_axis=0, tiled=True)
        total = part.astype(f32).sum(axis=0)
        return lax.optimization_barrier((total[:, :LANES], total[:, LANES:].astype(bf16)))

    mine0, other0 = over_y(0)
    other0_there = lax.ppermute(other0, "h", swap)

    anchor = select_rows(rows_of(x), base.astype(bf16)).astype(f32)
    total = select_rows(rows_of(x), terms).astype(f32) - n_x * anchor
    received = [after(piece, other0) for piece in received]
    for piece in received:
        total += piece.astype(f32)
    part = lax.all_to_all(total.astype(bf16), "zi", split_axis=0, concat_axis=0, tiled=True)
    part = part.reshape(n_zi, n_zo * own, width)

    mine1, other1 = over_y(1, part)
    other1_there = lax.ppermute(other1, "h", swap)

    start = ((zo * n_zi + zi) * n_x + x) * own
    r = jnp.arange(rows, dtype=jnp.int32)
    from_x, from_zi, from_zo = (r // own) % n_x, (r // (own * n_x)) % n_zi, r // (own * n_x * n_zi)
    where = (from_zi * n_zo + from_zo) * own + r % own + ((x - from_x) % n_x) * per_x

    def finish(part):
        part = part.reshape(n_zi, n_zo * own, width)
        total = part.astype(f32).sum(axis=0).astype(bf16).reshape(n_zo, own, width)
        part = lax.all_to_all(total, "zo", split_axis=0, concat_axis=0, tiled=True)
        outer_grad = -part.astype(f32).sum(axis=0) / groups
        own_base = lax.dynamic_slice_in_dim(base, start, own, 0)
        own_momentum = lax.dynamic_slice_in_dim(momentum, start, own, 0)
        new_momentum = 0.9 * own_momentum + outer_grad
        new_base = own_base - 0.7 * (outer_grad + 0.9 * new_momentum)
        gathered = gather_small(new_base.astype(bf16), "zo", n_zo).reshape(n_zo * own, width)
        gathered = gather_small(gathered, "zi", n_zi).reshape(per_x, width)
        pieces = [gathered] + [lax.ppermute(gathered, "x", shift("x", n_x, step)) for step in range(1, n_x)]
        return gathered, new_base, new_momentum, select_rows(where, jnp.concatenate(pieces, axis=0))

    once = 1 + (h >> 4)
    part = after(part, other0, other1).reshape(per_x, width)
    empty = (part, jnp.zeros((own, width), f32), jnp.zeros((own, width), f32), jnp.zeros((rows, width), bf16))
    _, new_base, new_momentum, synced = lax.fori_loop(0, once, lambda _, carry: finish(carry[0]), empty)

    results = []
    for mine, there in ((mine0, other0_there), (mine1, other1_there)):
        there = after(there, new_base, synced)
        results.append((mine + there.astype(f32)).astype(bf16))
    keys_values = jnp.concatenate(results, axis=0)
    return new_base, new_momentum, synced, keys_values


def solution(mesh):
    fine = Mesh(mesh.devices.reshape(SIZES), NAMES)
    replica, mp = NAMES[:3], NAMES[3:]
    return jax.shard_map(
        shards,
        mesh=fine,
        in_specs=(
            P(replica, None, mp),
            P(None, mp),
            P(None, mp),
            P(replica, mp),
            P(mp, None),
        ),
        out_specs=(P(replica, mp), P(replica, mp), P(None, mp), P(replica, mp)),
        check_vma=False,
    )
```

time: 1590 us -> 212 us (0.13)
  waiting for transfers between devices: 1550 us -> 13.8 us
  blocking collectives: 0 us -> 84.8 us
  starting transfers between devices: 0.08 us -> 76.7 us
    psum x1 -> x0, waiting for transfers between devices: 1550 us -> none  [shards(): summed = lax.psum(local_terms, 'replica')]
    all_to_all x0 -> x3, blocking collectives: none -> 84.8 us  [the longest x1 53.1 us: finish(): part = lax.all_to_all(total, 'zo', split_axis=0, concat_axis=0, tiled=True)]
    ppermute x0 -> x10, starting transfers between devices: none -> 55.3 us  [the longest x1 18.8 us: shards(): other0_there = lax.ppermute(other0, 'h', swap)]
    all_to_all x0 -> x3, starting transfers between devices: none -> 21.4 us  [the longest x2 18 us: over_y(): part = lax.all_to_all(part, 'y', split_axis=0, concat_axis=0, tiled=True)]
  transfers between devices with their start and end apart: 2 -> 13, of which waited for: 1 -> 4; matrix products, arithmetic and copies ran while one was open for 1% -> 8% of each run, Pallas kernels for 0% -> 3%
where the time goes in v1:
time: 212 us; the launch traced here: 211 us
  blocking collectives  84.8 us (40%)
  starting transfers between devices  76.7 us (36%)
  waiting for transfers between devices  13.8 us (7%)
  matrix products  11 us (5%)
  local copies, waits for them, and re-layouts  10 us (5%)
  Pallas kernels  8.67 us (4%)
  other arithmetic  5.28 us (2%)
    all_to_all x1, blocking collectives, finish(): part = lax.all_to_all(total, 'zo', split_axis=0, concat_axis=0, tiled=True)  53.1 us
    all_to_all x2, blocking collectives, gather_small(): return lax.all_to_all(copies, axis, split_axis=0, concat_axis=0, tiled=True)  31.7 us
    ppermute x1, starting transfers between devices, shards(): other0_there = lax.ppermute(other0, 'h', swap)  18.8 us
    all_to_all x2, starting transfers between devices, over_y(): part = lax.all_to_all(part, 'y', split_axis=0, concat_axis=0, tiled=True)  18 us
    ppermute x3, starting transfers between devices, shards(): received.append(lax.ppermute(sent, 'x', shift('x', n_x, step)))  13.1 us
    ppermute x1, starting transfers between devices, shards(): other1_there = lax.ppermute(other1, 'h', swap)  11.1 us
    dot_general x6, matrix products, select_rows(): jnp.dot(one_hot(source, array.shape[0]), array, preferred_element_type=f32)  11 us
    ppermute x3, starting transfers between devices, finish(): lax.ppermute(gathered, 'x', shift('x', n_x, step))  7.91 us
  transfers between devices with their start and end apart: 13, of which 4 were waited for; matrix products, arithmetic and copies ran while one was open for 8% of the time, Pallas kernels for 3%

profile of v1, /device:TPU:8, one launch (start us, length us, event | category | flops | bytes accessed | tf_op | source)
XLA Modules:
  0.0 211.3 jit_solution(6917573796273841612)
XLA Ops:
  0.6 0.0 copy-start
  0.7 0.1 pad_add_fusion.refs_0_
  0.7 1.7 copy-done.1
  2.4 1.7 shard_map.84
  4.1 1.9 collective-permute-start.5
  6.0 0.0 copy-done.4
  6.1 2.4 %collective-permute-start.4 = (bf16[1024,512]{1,0:T(8,128)(2,1)S(1)}, bf16[1024,512]{1,0:T(8,128)(2,1)}, u32[]{:S(2)}, u32[]{:S(2)}) collective-permute-start(bf16[1024,512]{1,0:T(8,128)(2,1)S(1)} %copy-done.4), channel_id=1, source_target_pairs={{0,1},{1,0},{2,3},{3,2},{4,5},{5,4},{6,7},{7,6},{8,9},{9,8},{10,11... | collective-permute-start | bytes 3145736 | tf_op jit(solution)/shard_map/ppermute | solution.py:114
  8.5 2.2 %convolution_convert_fusion.3 = bf16[64,1792]{1,0:T(8,128)(2,1)} fusion(bf16[256,1792]{1,0:T(8,128)(2,1)} %bitcast.15, s32[64]{0:T(128)S(1)} %multiply_add_fusion.3), kind=kOutput, calls=%fused_computation.50 | convolution fusion | flops 58851328 | bytes 1147136 | tf_op jit(solution)/shard_map/dot_general | solution.py:98
  10.7 3.4 %collective-permute-start.3 = (bf16[64,1792]{1,0:T(8,128)(2,1)}, bf16[64,1792]{1,0:T(8,128)(2,1)}, u32[]{:S(2)}, u32[]{:S(2)}) collective-permute-start(bf16[64,1792]{1,0:T(8,128)(2,1)} %convolution_convert_fusion.3), channel_id=1, source_target_pairs={{0,16},{16,32},{32,48},{48,0},{1,17},{17,33},{33,49},{49,1},{2,18}... | collective-permute-start | bytes 688136 | tf_op jit(solution)/shard_map/ppermute | solution.py:132
  14.1 2.2 %convolution_convert_fusion.2 = bf16[64,1792]{1,0:T(8,128)(2,1)} fusion(bf16[256,1792]{1,0:T(8,128)(2,1)} %bitcast.16, s32[64]{0:T(128)S(1)} %get-tuple-element.194), kind=kOutput, calls=%fused_computation.49 | convolution fusion | flops 58851328 | bytes 1147136 | tf_op jit(solution)/shard_map/dot_general | solution.py:98
  16.3 4.6 %collective-permute-start.6 = (bf16[64,1792]{1,0:T(8,128)(2,1)}, bf16[64,1792]{1,0:T(8,128)(2,1)}, u32[]{:S(2)}, u32[]{:S(2)}) collective-permute-start(bf16[64,1792]{1,0:T(8,128)(2,1)} %convolution_convert_fusion.2), channel_id=1, source_target_pairs={{0,32},{16,48},{32,0},{48,16},{1,33},{17,49},{33,1},{49,17},{2,34}... | collective-permute-start | bytes 688136 | tf_op jit(solution)/shard_map/ppermute | solution.py:132
  21.0 0.0 collective-permute-done.5.refs_4_
  21.0 0.0 collective-permute-done.4.refs_2_
  21.0 0.0 copy-start.2
  21.0 1.6 copy-done.2
  22.6 3.5 %shard_map.85 = bf16[4,512,256]{2,1,0:T(8,128)(2,1)S(1)} custom-call(s32[2]{0:T(128)S(1)} %pad_add_fusion.refs_0_, bf16[1024,512]{1,0:T(8,128)(2,1)S(1)} %copy-done.4, bf16[1024,512]{1,0:T(8,128)(2,1)} %collective-permute-done.4.refs_2_, bf16[512,2048]{1,0:T(8,128)(2,1)S(1)} %copy-done.2, bf16[512,1024]{1,0:T(8,128)(2,1)} %collective-permute-done.5.refs_4_), custom_call_target="tpu_custom_call" | custom-call | flops 1073741824 | bytes 5242880 | tf_op jit(solution)/shard_map/pallas_call | solution.py:68
  26.1 0.0 copy-start.6
  26.1 1.0 copy-done.6
  27.0 13.1 %all-to-all-start.3 = ((bf16[4,512,256]{2,1,0:T(8,128)(2,1)}), bf16[4,512,256]{2,1,0:T(8,128)(2,1)}, u32[]{:S(2)}, u32[]{:S(2)}) async-start(bf16[4,512,256]{2,1,0:T(8,128)(2,1)} %copy-done.6), calls=%async_computation.3 | async-start | bytes 2097152 | tf_op jit(solution)/shard_map/all_to_all | solution.py:139
  40.2 2.3 %convolution_convert_fusion.1 = bf16[64,1792]{1,0:T(8,128)(2,1)} fusion(bf16[256,1792]{1,0:T(8,128)(2,1)} %bitcast.17, s32[64]{0:T(128)S(1)} %get-tuple-element.193), kind=kOutput, calls=%fused_computation.48 | convolution fusion | flops 58851328 | bytes 1147136 | tf_op jit(solution)/shard_map/dot_general | solution.py:98
  42.5 5.1 %collective-permute-start.7 = (bf16[64,1792]{1,0:T(8,128)(2,1)}, bf16[64,1792]{1,0:T(8,128)(2,1)}, u32[]{:S(2)}, u32[]{:S(2)}) collective-permute-start(bf16[64,1792]{1,0:T(8,128)(2,1)} %convolution_convert_fusion.1), channel_id=1, source_target_pairs={{0,48},{16,0},{32,16},{48,32},{1,49},{17,1},{33,17},{49,33},{2,50}... | collective-permute-start | bytes 688136 | tf_op jit(solution)/shard_map/ppermute | solution.py:132
  47.6 1.5 fusion.27
  49.1 0.0 copy-done.7
  49.1 0.3 fusion.26
  49.5 4.9 %all-to-all-done.3 = bf16[4,512,256]{2,1,0:T(8,128)(2,1)} async-done(((bf16[4,512,256]{2,1,0:T(8,128)(2,1)}), bf16[4,512,256]{2,1,0:T(8,128)(2,1)}, u32[]{:S(2)}, u32[]{:S(2)}) %all-to-all-start.3) | async-done | bytes 1048608 | tf_op jit(solution)/shard_map/all_to_all | solution.py:139
  54.3 1.4 convert_reduce_fusion.2
  55.8 0.0 copy-start.8
  55.8 0.0 collective-permute-done.3
  55.8 0.0 collective-permute-done.6
  55.8 0.0 collective-permute-done.7
  55.8 2.1 add_convert_fusion
  57.9 0.0 copy-done.8
  57.9 3.4 %all-to-all-start.4 = ((bf16[4,16,1792]{2,1,0:T(8,128)(2,1)}), bf16[4,16,1792]{2,1,0:T(8,128)(2,1)S(1)}, u32[]{:S(2)}, u32[]{:S(2)}) async-start(bf16[4,16,1792]{2,1,0:T(8,128)(2,1)} %bitcast.26), calls=%async_computation.4 | async-start | bytes 458752 | tf_op jit(solution)/shard_map/all_to_all | solution.py:151
  61.3 0.0 copy-start.3
  61.3 1.6 copy-done.3
  62.9 3.5 %shard_map.86 = bf16[4,512,256]{2,1,0:T(8,128)(2,1)S(1)} custom-call(s32[2]{0:T(128)S(1)} %pad_add_fusion.refs_0_, bf16[1024,512]{1,0:T(8,128)(2,1)S(1)} %copy-done.4, bf16[1024,512]{1,0:T(8,128)(2,1)} %collective-permute-done.4.refs_2_, bf16[512,2048]{1,0:T(8,128)(2,1)S(1)} %copy-done.3, bf16[512,1024]{1,0:T(8,128)(2,1)} %collective-permute-done.5.refs_4_), custom_call_target="tpu_custom_call" | custom-call | flops 1073741824 | bytes 5242880 | tf_op jit(solution)/shard_map/pallas_call | solution.py:68
  66.4 0.0 copy-start.5
  66.4 1.0 copy-done.5
  67.4 1.6 all-to-all-done.4
  69.0 4.9 %all-to-all-start.5 = ((bf16[4,512,256]{2,1,0:T(8,128)(2,1)}), bf16[4,512,256]{2,1,0:T(8,128)(2,1)S(1)}, u32[]{:S(2)}, u32[]{:S(2)}) async-start(bf16[4,512,256]{2,1,0:T(8,128)(2,1)} %copy-done.5), calls=%async_computation.5 | async-start | bytes 2097152 | tf_op jit(solution)/shard_map/all_to_all | solution.py:139
  74.0 0.8 constant_dynamic-slice_fusion
  74.8 18.8 %collective-permute-start.8 = (bf16[512,128]{1,0:T(8,128)(2,1)S(1)}, bf16[512,128]{1,0:T(8,128)(2,1)S(1)}, u32[]{:S(2)}, u32[]{:S(2)}) collective-permute-start(bf16[512,128]{1,0:T(8,128)(2,1)S(1)} %slice.25), channel_id=1, source_target_pairs={{0,2},{2,0},{1,3},{3,1},{4,6},{6,4},{5,7},{7,5},{8,10},{10,8},{9,1... | collective-permute-start | bytes 393224 | tf_op jit(solution)/shard_map/ppermute | solution.py:144
  93.7 0.0 all-to-all-done.5
  93.7 0.1 convert_reduce_fusion.1
  93.9 11.1 %collective-permute-start.9 = (bf16[512,128]{1,0:T(8,128)(2,1)S(1)}, bf16[512,128]{1,0:T(8,128)(2,1)S(1)}, u32[]{:S(2)}, u32[]{:S(2)}) collective-permute-start(bf16[512,128]{1,0:T(8,128)(2,1)S(1)} %slice.24), channel_id=1, source_target_pairs={{0,2},{2,0},{1,3},{3,1},{4,6},{6,4},{5,7},{7,5},{8,10},{10,8},{9,1... | collective-permute-start | bytes 393224 | tf_op jit(solution)/shard_map/ppermute | solution.py:155
  105.0 0.0 collective-permute-done.8
  105.0 1.0 broadcast_in_dim.12
  106.0 0.6 broadcast.410
  106.6 0.6 broadcast.410.clone
  107.2 103.2 %while.19 = (s32[]{:T(128)}, bf16[64,1792]{1,0:T(8,128)(2,1)S(1)}, f32[4,1792]{1,0:T(4,128)}, f32[4,1792]{1,0:T(4,128)}, bf16[256,1792]{1,0:T(8,128)(2,1)}, /*in...) while((s32[]{:T(128)}, bf16[64,1792]{1,0:T(8,128)(2,1)S(1)}, ...), condition=%wide.region_5.6_spmd.clone, body=%wide.region_2.5_spmd.clone.sunk | while | flops 239292416 | bytes 6396139 | solution.py:179
  107.3 53.1 %all_to_all.49 = bf16[4,4,1792]{2,1,0:T(4,128)(2,1)S(1)} all-to-all(bf16[4,4,1792]{2,1,0:T(4,128)(2,1)S(1)} %reshape.107), channel_id=1, replica_groups=mesh['zo'=4,'zi'=4,'x'=4,'y'=4,'h'=2,'c'=2] {'zo'}, dimensions={0} | all-to-all | bytes 114688 | tf_op jit(solution)/shard_map/while/body/all_to_all | solution.py:165
  160.4 0.6 fusion.47
  161.1 19.8 %all_to_all.50 = bf16[4,4,1792]{2,1,0:T(4,128)(2,1)S(1)} all-to-all(bf16[4,4,1792]{2,1,0:T(4,128)(2,1)S(1)} %broadcast_in_dim.32), channel_id=1, replica_groups=mesh['zo'=4,'zi'=4,'x'=4,'y'=4,'h'=2,'c'=2] {'zo'}, dimensions={0} | all-to-all | bytes 114688 | tf_op jit(solution)/shard_map/while/body/all_to_all | solution.py:103
  180.9 11.9 %all_to_all.51 = bf16[4,16,1792]{2,1,0:T(8,128)(2,1)S(1)} all-to-all(bf16[4,16,1792]{2,1,0:T(8,128)(2,1)S(1)} %broadcast_in_dim.33), channel_id=1, replica_groups=mesh['zo'=4,'zi'=4,'x'=4,'y'=4,'h'=2,'c'=2] {'zi'}, dimensions={0} | all-to-all | bytes 458752 | tf_op jit(solution)/shard_map/while/body/all_to_all | solution.py:103
  192.8 3.2 %collective-permute-start = (bf16[64,1792]{1,0:T(8,128)(2,1)S(1)}, bf16[64,1792]{1,0:T(8,128)(2,1)S(1)}, u32[]{:S(2)}, u32[]{:S(2)}) collective-permute-start(bf16[64,1792]{1,0:T(8,128)(2,1)S(1)} %bitcast.21), channel_id=1, source_target_pairs={{0,48},{16,0},{32,16},{48,32},{1,49},{17,1},{33,17},{49,33},{2,50}... | collective-permute-start | bytes 688136 | tf_op jit(solution)/shard_map/while/body/ppermute | solution.py:173
  196.0 2.5 %collective-permute-start.1 = (bf16[64,1792]{1,0:T(8,128)(2,1)S(1)}, bf16[64,1792]{1,0:T(8,128)(2,1)}, u32[]{:S(2)}, u32[]{:S(2)}) collective-permute-start(bf16[64,1792]{1,0:T(8,128)(2,1)S(1)} %bitcast.22), channel_id=1, source_target_pairs={{0,32},{16,48},{32,0},{48,16},{1,33},{17,49},{33,1},{49,17},{2,34}... | collective-permute-start | bytes 688136 | tf_op jit(solution)/shard_map/while/body/ppermute | solution.py:173
  198.5 2.2 %collective-permute-start.2 = (bf16[64,1792]{1,0:T(8,128)(2,1)S(1)}, bf16[64,1792]{1,0:T(8,128)(2,1)}, u32[]{:S(2)}, u32[]{:S(2)}) collective-permute-start(bf16[64,1792]{1,0:T(8,128)(2,1)S(1)} %bitcast.23), channel_id=1, source_target_pairs={{0,16},{16,32},{32,48},{48,0},{1,17},{17,33},{33,49},{49,1},{2,18}... | collective-permute-start | bytes 688136 | tf_op jit(solution)/shard_map/while/body/ppermute | solution.py:173
  200.7 0.0 collective-permute-done
  200.7 4.8 %collective-permute-done.1 = bf16[64,1792]{1,0:T(8,128)(2,1)} collective-permute-done((bf16[64,1792]{1,0:T(8,128)(2,1)S(1)}, bf16[64,1792]{1,0:T(8,128)(2,1)}, u32[]{:S(2)}, u32[]{:S(2)}) %collective-permute-start.1) | collective-permute-done | bytes 229408 | tf_op jit(solution)/shard_map/while/body/ppermute | solution.py:173
  205.6 2.4 %collective-permute-done.2 = bf16[64,1792]{1,0:T(8,128)(2,1)} collective-permute-done((bf16[64,1792]{1,0:T(8,128)(2,1)S(1)}, bf16[64,1792]{1,0:T(8,128)(2,1)}, u32[]{:S(2)}, u32[]{:S(2)}) %collective-permute-start.2) | collective-permute-done | bytes 229408 | tf_op jit(solution)/shard_map/while/body/ppermute | solution.py:173
  208.0 2.4 %convolution_convert_fusion.7 = bf16[256,1792]{1,0:T(8,128)(2,1)} fusion(bf16[64,1792]{1,0:T(8,128)(2,1)S(1)} %collective-permute-done, bf16[64,1792]{1,0:T(8,128)(2,1)} %collective-permute-done.1, bf16[64,1792]{1,0:T(8,128)(2,1)} %collective-permute-done.2, bf16[64,1792]{1,0:T(8,128)(2,1)S(1)} %bitcast.24, s32[256]{0:T(256)S(1)} %fusion.48), kind=kOutput, calls=%fused_computation.1.clone.1 | convolution fusion | flops 239075328 | bytes 1836032 | tf_op jit(solution)/shard_map/while/body/dot_general | solution.py:98
  210.5 0.0 collective-permute-done.9
  210.5 0.0 slice-done.1
  210.5 0.7 pad_maximum_fusion
  (24 shorter events, 0.3 us)
Async XLA Ops:
  0.6 74.2 %copy-start = (f32[256,1792]{1,0:T(8,128)S(1)}, f32[256,1792]{1,0:T(8,128)}, u32[]{:S(2)}) copy-start(f32[256,1792]{1,0:T(8,128)} %param.9) | copy-start | bytes 5505028
  0.7 1.7 copy-start.1
  2.4 3.6 %copy-start.4 = (bf16[1024,512]{1,0:T(8,128)(2,1)S(1)}, bf16[1024,512]{1,0:T(8,128)(2,1)}, u32[]{:S(2)}) copy-start(bf16[1024,512]{1,0:T(8,128)(2,1)} %refs_1_.5) | copy-start | bytes 3145732
  4.1 16.8 %collective-permute-start.5 = (bf16[512,1024]{1,0:T(8,128)(2,1)}, bf16[512,1024]{1,0:T(8,128)(2,1)}, u32[]{:S(2)}, u32[]{:S(2)}) collective-permute-start(bf16[512,1024]{1,0:T(8,128)(2,1)} %shard_map.84), channel_id=1, source_target_pairs={{0,1},{1,0},{2,3},{3,2},{4,5},{5,4},{6,7},{7,6},{8,9},{9,8},{10,11... | collective-permute-start | bytes 3145736 | tf_op jit(solution)/shard_map/ppermute | solution.py:117
  6.1 14.9 %collective-permute-start.4 = (bf16[1024,512]{1,0:T(8,128)(2,1)S(1)}, bf16[1024,512]{1,0:T(8,128)(2,1)}, u32[]{:S(2)}, u32[]{:S(2)}) collective-permute-start(bf16[1024,512]{1,0:T(8,128)(2,1)S(1)} %copy-done.4), channel_id=1, source_target_pairs={{0,1},{1,0},{2,3},{3,2},{4,5},{5,4},{6,7},{7,6},{8,9},{9,8},{10,11... | collective-permute-start | bytes 3145736 | tf_op jit(solution)/shard_map/ppermute | solution.py:114
  10.7 45.1 %collective-permute-start.3 = (bf16[64,1792]{1,0:T(8,128)(2,1)}, bf16[64,1792]{1,0:T(8,128)(2,1)}, u32[]{:S(2)}, u32[]{:S(2)}) collective-permute-start(bf16[64,1792]{1,0:T(8,128)(2,1)} %convolution_convert_fusion.3), channel_id=1, source_target_pairs={{0,16},{16,32},{32,48},{48,0},{1,17},{17,33},{33,49},{49,1},{2,18}... | collective-permute-start | bytes 688136 | tf_op jit(solution)/shard_map/ppermute | solution.py:132
  16.3 39.5 %collective-permute-start.6 = (bf16[64,1792]{1,0:T(8,128)(2,1)}, bf16[64,1792]{1,0:T(8,128)(2,1)}, u32[]{:S(2)}, u32[]{:S(2)}) collective-permute-start(bf16[64,1792]{1,0:T(8,128)(2,1)} %convolution_convert_fusion.2), channel_id=1, source_target_pairs={{0,32},{16,48},{32,0},{48,16},{1,33},{17,49},{33,1},{49,17},{2,34}... | collective-permute-start | bytes 688136 | tf_op jit(solution)/shard_map/ppermute | solution.py:132
  21.0 1.6 copy-start.2
  26.1 1.0 copy-start.6
  27.0 27.3 %all-to-all-start.3 = ((bf16[4,512,256]{2,1,0:T(8,128)(2,1)}), bf16[4,512,256]{2,1,0:T(8,128)(2,1)}, u32[]{:S(2)}, u32[]{:S(2)}) async-start(bf16[4,512,256]{2,1,0:T(8,128)(2,1)} %copy-done.6), calls=%async_computation.3 | async-start | bytes 2097152 | tf_op jit(solution)/shard_map/all_to_all | solution.py:139
  40.1 9.0 %copy-start.7 = (f32[256,1792]{1,0:T(8,128)S(1)}, f32[256,1792]{1,0:T(8,128)}, u32[]{:S(2)}) copy-start(f32[256,1792]{1,0:T(8,128)} %param.8) | copy-start | bytes 5505028
  42.5 13.3 %collective-permute-start.7 = (bf16[64,1792]{1,0:T(8,128)(2,1)}, bf16[64,1792]{1,0:T(8,128)(2,1)}, u32[]{:S(2)}, u32[]{:S(2)}) collective-permute-start(bf16[64,1792]{1,0:T(8,128)(2,1)} %convolution_convert_fusion.1), channel_id=1, source_target_pairs={{0,48},{16,0},{32,16},{48,32},{1,49},{17,1},{33,17},{49,33},{2,50}... | collective-permute-start | bytes 688136 | tf_op jit(solution)/shard_map/ppermute | solution.py:132
  55.8 2.2 %copy-start.8 = (f32[512,256]{1,0:T(8,128)}, f32[512,256]{1,0:T(8,128)S(1)}, u32[]{:S(2)}) copy-start(f32[512,256]{1,0:T(8,128)S(1)} %convert_reduce_fusion.2) | copy-start | bytes 1572868
  57.9 11.1 %all-to-all-start.4 = ((bf16[4,16,1792]{2,1,0:T(8,128)(2,1)}), bf16[4,16,1792]{2,1,0:T(8,128)(2,1)S(1)}, u32[]{:S(2)}, u32[]{:S(2)}) async-start(bf16[4,16,1792]{2,1,0:T(8,128)(2,1)} %bitcast.26), calls=%async_computation.4 | async-start | bytes 458752 | tf_op jit(solution)/shard_map/all_to_all | solution.py:151
  61.3 1.6 copy-start.3
  66.4 1.0 copy-start.5
  69.0 24.7 %all-to-all-start.5 = ((bf16[4,512,256]{2,1,0:T(8,128)(2,1)}), bf16[4,512,256]{2,1,0:T(8,128)(2,1)S(1)}, u32[]{:S(2)}, u32[]{:S(2)}) async-start(bf16[4,512,256]{2,1,0:T(8,128)(2,1)} %copy-done.5), calls=%async_computation.5 | async-start | bytes 2097152 | tf_op jit(solution)/shard_map/all_to_all | solution.py:139
  74.8 30.1 %collective-permute-start.8 = (bf16[512,128]{1,0:T(8,128)(2,1)S(1)}, bf16[512,128]{1,0:T(8,128)(2,1)S(1)}, u32[]{:S(2)}, u32[]{:S(2)}) collective-permute-start(bf16[512,128]{1,0:T(8,128)(2,1)S(1)} %slice.25), channel_id=1, source_target_pairs={{0,2},{2,0},{1,3},{3,1},{4,6},{6,4},{5,7},{7,5},{8,10},{10,8},{9,1... | collective-permute-start | bytes 393224 | tf_op jit(solution)/shard_map/ppermute | solution.py:144
  93.8 13.3 %copy-start.9 = (f32[512,256]{1,0:T(8,128)}, f32[512,256]{1,0:T(8,128)S(1)}, u32[]{:S(2)}) copy-start(f32[512,256]{1,0:T(8,128)S(1)} %convert_reduce_fusion.1) | copy-start | bytes 1572868
  93.9 116.6 %collective-permute-start.9 = (bf16[512,128]{1,0:T(8,128)(2,1)S(1)}, bf16[512,128]{1,0:T(8,128)(2,1)S(1)}, u32[]{:S(2)}, u32[]{:S(2)}) collective-permute-start(bf16[512,128]{1,0:T(8,128)(2,1)S(1)} %slice.24), channel_id=1, source_target_pairs={{0,2},{2,0},{1,3},{3,1},{4,6},{6,4},{5,7},{7,5},{8,10},{10,8},{9,1... | collective-permute-start | bytes 393224 | tf_op jit(solution)/shard_map/ppermute | solution.py:155
  107.2 103.2 %slice-start = ((f32[512,256]{1,0:T(8,128)}), f32[512,128]{1,0:T(8,128)S(1)}, s32[]{:S(2)}) async-start(f32[512,256]{1,0:T(8,128)} %copy-done.8), calls=%async_computation.6 | async-start | bytes 524288 | tf_op jit(solution)/shard_map/slice | solution.py:141
  107.2 103.3 %slice-start.1 = ((f32[512,256]{1,0:T(8,128)}), f32[512,128]{1,0:T(8,128)S(1)}, s32[]{:S(2)}) async-start(f32[512,256]{1,0:T(8,128)} %copy-done.9), calls=%async_computation.7 | async-start | bytes 524288 | tf_op jit(solution)/shard_map/slice | solution.py:141
  192.8 7.9 %collective-permute-start = (bf16[64,1792]{1,0:T(8,128)(2,1)S(1)}, bf16[64,1792]{1,0:T(8,128)(2,1)S(1)}, u32[]{:S(2)}, u32[]{:S(2)}) collective-permute-start(bf16[64,1792]{1,0:T(8,128)(2,1)S(1)} %bitcast.21), channel_id=1, source_target_pairs={{0,48},{16,0},{32,16},{48,32},{1,49},{17,1},{33,17},{49,33},{2,50}... | collective-permute-start | bytes 688136 | tf_op jit(solution)/shard_map/while/body/ppermute | solution.py:173
  196.0 9.5 %collective-permute-start.1 = (bf16[64,1792]{1,0:T(8,128)(2,1)S(1)}, bf16[64,1792]{1,0:T(8,128)(2,1)}, u32[]{:S(2)}, u32[]{:S(2)}) collective-permute-start(bf16[64,1792]{1,0:T(8,128)(2,1)S(1)} %bitcast.22), channel_id=1, source_target_pairs={{0,32},{16,48},{32,0},{48,16},{1,33},{17,49},{33,1},{49,17},{2,34}... | collective-permute-start | bytes 688136 | tf_op jit(solution)/shard_map/while/body/ppermute | solution.py:173
  198.5 9.5 %collective-permute-start.2 = (bf16[64,1792]{1,0:T(8,128)(2,1)S(1)}, bf16[64,1792]{1,0:T(8,128)(2,1)}, u32[]{:S(2)}, u32[]{:S(2)}) collective-permute-start(bf16[64,1792]{1,0:T(8,128)(2,1)S(1)} %bitcast.23), channel_id=1, source_target_pairs={{0,16},{16,32},{32,48},{48,0},{1,17},{17,33},{33,49},{49,1},{2,18}... | collective-permute-start | bytes 688136 | tf_op jit(solution)/shard_map/while/body/ppermute | solution.py:173

commit v2 on v0

v2 whole, which is shorter than its diff:
```python
import jax
import jax.numpy as jnp
from jax import lax
from jax.experimental import pallas as pl
from jax.experimental.pallas import tpu as pltpu
from jax.sharding import Mesh, PartitionSpec as P

SIZES = (4, 4, 4, 4, 2, 2)
NAMES = ("zo", "zi", "x", "y", "h", "c")
LANES = 128

bf16 = jnp.bfloat16
f32 = jnp.float32
VMEM = 20 << 20


def column(y, h, c):
    return y * 4 + h * 2 + c


def pack_kernel(place_ref, near_ref, far_ref, packed_ref):
    packed_ref[:, :LANES] = near_ref[...]
    packed_ref[:, LANES:] = far_ref[...]


def pack(place, weight, n_y):
    depth, width = weight.shape
    return pl.pallas_call(
        pack_kernel,
        out_shape=jax.ShapeDtypeStruct((depth, width // 2), bf16),
        grid_spec=pltpu.PrefetchScalarGridSpec(
            num_scalar_prefetch=1,
            grid=(n_y,),
            in_specs=[
                pl.BlockSpec((depth, LANES), lambda y, p: (0, column((y + p[2]) % n_y, p[0], 1 - p[1]))),
                pl.BlockSpec((depth, LANES), lambda y, p: (0, column((y + p[2]) % n_y, 1 - p[0], 1 - p[1]))),
            ],
            out_specs=pl.BlockSpec((depth, 2 * LANES), lambda y, _: (0, y)),
        ),
        cost_estimate=pl.CostEstimate(flops=0, bytes_accessed=weight.size * 2, transcendentals=0),
        compiler_params=pltpu.CompilerParams(vmem_limit_bytes=VMEM),
    )(place, weight, weight)


def project_kernel(place_ref, own_ref, sibling_ref, near_ref, far_ref, packed_ref, *out_refs):
    mine = jnp.concatenate([near_ref[...], far_ref[...]], axis=1)
    total = jnp.dot(own_ref[...], mine, preferred_element_type=f32)
    total += jnp.dot(sibling_ref[...], packed_ref[...], preferred_element_type=f32)
    total = total.astype(bf16)
    for step, out_ref in enumerate(out_refs):

        @pl.when(pl.program_id(0) == step)
        def _(out_ref=out_ref):
            out_ref[...] = total


def project(place, own, sibling, weight, packed, n_y):
    rows, depth = own.shape
    width = weight.shape[1]
    return pl.pallas_call(
        project_kernel,
        out_shape=[jax.ShapeDtypeStruct((rows, 2 * LANES), bf16)] * n_y,
        grid_spec=pltpu.PrefetchScalarGridSpec(
            num_scalar_prefetch=1,
            grid=(n_y,),
            in_specs=[
                pl.BlockSpec((rows, depth), lambda y, _: (0, 0)),
                pl.BlockSpec((rows, depth), lambda y, _: (0, 0)),
                pl.BlockSpec((depth, LANES), lambda y, p: (0, column((y + p[2]) % n_y, p[0], p[1]))),
                pl.BlockSpec((depth, LANES), lambda y, p: (0, column((y + p[2]) % n_y, 1 - p[0], p[1]))),
                pl.BlockSpec((depth, 2 * LANES), lambda y, _: (0, y)),
            ],
            out_specs=[pl.BlockSpec((rows, 2 * LANES), lambda y, _: (0, 0))] * n_y,
        ),
        cost_estimate=pl.CostEstimate(
            flops=2 * rows * depth * width, bytes_accessed=rows * (4 * depth + width) + weight.size * 2, transcendentals=0
        ),
        compiler_params=pltpu.CompilerParams(vmem_limit_bytes=VMEM),
    )(place, own, sibling, weight, weight, packed)


def after(array, *earlier):
    return lax.optimization_barrier((array, *earlier))[0]


def shift(axis, size, step):
    return [(i, (i + step) % size) for i in range(size)]


def exchange(array, axis):
    return lax.all_to_all(array, axis, split_axis=0, concat_axis=0, tiled=True)


def gather_small(array, axis, size):
    return exchange(jnp.broadcast_to(array, (size, *array.shape)), axis)


def shards(local_weights, base, momentum, tokens, weight):
    sizes = dict(zip(NAMES, SIZES))
    zo, zi, x, y, h, c = (lax.axis_index(a) for a in NAMES)
    n_zo, n_zi, n_x, n_y = (sizes[a] for a in ("zo", "zi", "x", "y"))
    swap = [(0, 1), (1, 0)]
    groups = n_zo * n_zi * n_x
    rows, width = base.shape
    own = rows // groups
    per_x, per_zi = rows // n_x, rows // (n_x * n_zi)

    terms = exchange(local_weights[0].reshape(n_x, per_x, width), "x")

    place = jnp.stack([h, c, y]).astype(jnp.int32)
    sibling = lax.ppermute(tokens, "c", swap)
    packed = lax.ppermute(pack(place, weight, n_y), "c", swap)
    part = project(place, tokens, sibling, weight, packed, n_y)

    terms = after(terms, *part)
    anchor = lax.dynamic_slice_in_dim(base, x * per_x, per_x, 0).astype(bf16).astype(f32)
    total = (terms.astype(f32).sum(axis=0) - n_x * anchor).astype(bf16)

    pieces = [lax.ppermute(part[step], "y", shift("y", n_y, step)) for step in range(1, n_y)]

    def over_z(total):
        terms = exchange(total.reshape(n_zi, per_zi, width), "zi")
        total = terms.astype(f32).sum(axis=0).astype(bf16)
        terms = exchange(total.reshape(n_zo, own, width), "zo")
        outer_grad = (-terms.astype(f32).sum(axis=0) / groups).astype(bf16)
        gathered = gather_small(outer_grad, "zo", n_zo).reshape(per_zi, width)
        return gather_small(gathered, "zi", n_zi).reshape(per_x, width)

    outer_grad = lax.fori_loop(0, 1 + (h >> 4), lambda _, value: over_z(value), total)

    pieces = lax.optimization_barrier((outer_grad, *pieces))[1:]
    total = part[0].astype(f32)
    for piece in pieces:
        total += piece.astype(f32)
    mine, other = total[:, :LANES], total[:, LANES:].astype(bf16)
    mine, other = lax.optimization_barrier((mine, other))
    outer_grad = after(outer_grad, other)
    there = lax.ppermute(other, "h", swap)
    outer_grad = lax.all_gather(outer_grad, "x", axis=0, tiled=True).astype(f32)

    def step(outer_grad, base, momentum):
        new_momentum = 0.9 * momentum + outer_grad
        return base - 0.7 * (outer_grad + 0.9 * new_momentum), new_momentum

    synced = step(outer_grad, base, momentum)[0].astype(bf16)
    start = ((zo * n_zi + zi) * n_x + x) * own
    new_base, new_momentum = step(
        *(lax.dynamic_slice_in_dim(a, start, own, 0) for a in (outer_grad, base, momentum))
    )
    there = after(there, synced, new_base)
    keys_values = (mine + there.astype(f32)).astype(bf16)
    return new_base, new_momentum, synced, keys_values


def solution(mesh):
    fine = Mesh(mesh.devices.reshape(SIZES), NAMES)
    replica, mp = NAMES[:3], NAMES[3:]
    return jax.shard_map(
        shards,
        mesh=fine,
        in_specs=(
            P(replica, None, mp),
            P(None, mp),
            P(None, mp),
            P(replica, mp),
            P(mp, None),
        ),
        out_specs=(P(replica, mp), P(replica, mp), P(None, mp), P(replica, mp)),
        check_vma=False,
    )
```

time: 1590 us -> 183 us (0.12)
  the two profiles are of different devices: /device:TPU:8 before, /device:TPU:33 now
where the time goes in v2:
time: 183 us; the launch traced here: 182 us
  blocking collectives  81 us (44%)
  waiting for transfers between devices  47 us (26%)
  starting transfers between devices  37.1 us (20%)
  Pallas kernels  8.16 us (4%)
  other arithmetic  5.72 us (3%)
  local copies, waits for them, and re-layouts  2.44 us (1%)
    all_to_all x3, blocking collectives, exchange(): return lax.all_to_all(array, axis, split_axis=0, concat_axis=0, tiled=True)  68.9 us
    ppermute x1, waiting for transfers between devices, shards(): there = lax.ppermute(other, 'h', swap)  41.9 us
    all_gather x1, blocking collectives, shards(): outer_grad = lax.all_gather(outer_grad, 'x', axis=0, tiled=True).astype(f32)  12 us
    ppermute x1, starting transfers between devices, shards(): there = lax.ppermute(other, 'h', swap)  11.7 us
    ppermute x3, starting transfers between devices, shards(): lax.ppermute(part[step], 'y', shift('y', n_y, step))  10.7 us
    all_to_all x2, starting transfers between devices, exchange(): return lax.all_to_all(array, axis, split_axis=0, concat_axis=0, tiled=True)  10.2 us
    pallas_call x1, Pallas kernels, project(): pl.pallas_call(project_kernel, out_shape=[jax.ShapeDtypeStruct((rows, 2 *...  6.8 us
    all_to_all x2, waiting for transfers between devices, exchange(): return lax.all_to_all(array, axis, split_axis=0, concat_axis=0, tiled=True)  5.09 us
  transfers between devices with their start and end apart: 8, of which 2 were waited for; matrix products, arithmetic and copies ran while one was open for 3% of the time, Pallas kernels for 4%

profile of v2, /device:TPU:33, one launch (start us, length us, event | category | flops | bytes accessed | tf_op | source)
XLA Modules:
  0.0 182.2 jit_solution(12031225485732997298)
XLA Ops:
  0.6 0.1 pad_add_fusion.place_ref
  0.7 0.0 copy-start
  0.7 1.6 copy-done
  2.3 0.0 copy-start.1
  2.3 1.4 shard_map.84
  3.7 2.6 %collective-permute-start.1 = (bf16[512,1024]{1,0:T(8,128)(2,1)S(1)}, bf16[512,1024]{1,0:T(8,128)(2,1)}, u32[]{:S(2)}, u32[]{:S(2)}) collective-permute-start(bf16[512,1024]{1,0:T(8,128)(2,1)S(1)} %shard_map.84), channel_id=1, source_target_pairs={{0,1},{1,0},{2,3},{3,2},{4,5},{5,4},{6,7},{7,6},{8,9},{9,8},{10,11... | collective-permute-start | bytes 3145736 | tf_op jit(solution)/shard_map/ppermute | solution.py:112
  6.3 1.9 %collective-permute-start = (bf16[1024,512]{1,0:T(8,128)(2,1)}, bf16[1024,512]{1,0:T(8,128)(2,1)}, u32[]{:S(2)}, u32[]{:S(2)}) collective-permute-start(bf16[1024,512]{1,0:T(8,128)(2,1)} %own_ref.1), channel_id=1, source_target_pairs={{0,1},{1,0},{2,3},{3,2},{4,5},{5,4},{6,7},{7,6},{8,9},{9,8},{10,11... | collective-permute-start | bytes 3145736 | tf_op jit(solution)/shard_map/ppermute | solution.py:111
  8.2 4.2 %all-to-all-start.4 = ((bf16[4,64,1792]{2,1,0:T(8,128)(2,1)}), bf16[4,64,1792]{2,1,0:T(8,128)(2,1)}, u32[]{:S(2)}, u32[]{:S(2)}) async-start(bf16[4,64,1792]{2,1,0:T(8,128)(2,1)} %bitcast.12), calls=%async_computation.4 | async-start | bytes 1835008 | tf_op jit(solution)/shard_map/all_to_all | solution.py:91
  12.5 0.0 collective-permute-done.1.packed_ref
  12.5 0.0 collective-permute-done.sibling_ref
  12.5 0.0 copy-done.1
  12.5 6.8 %shard_map.85 = (bf16[1024,256]{1,0:T(8,128)(2,1)S(1)}, bf16[1024,256]{1,0:T(8,128)(2,1)}, bf16[1024,256]{1,0:T(8,128)(2,1)}, bf16[1024,256]{1,0:T(8,128)(2,1)S(1)}) custom-call(s32[3]{0:T(128)S(1)} %pad_add_fusion.place_ref, bf16[1024,512]{1,0:T(8,128)(2,1)} %own_ref.1, bf16[1024,512]{1,0:T(8,128)(2,1)} %collective-permute-done.sibling_ref, ...), custom_call_target="tpu_custom_call" | custom-call | flops 2147483648 | bytes 6291456 | tf_op jit(solution)/shard_map/pallas_call | solution.py:60
  19.3 3.2 %collective-permute-start.2 = (bf16[1024,256]{1,0:T(8,128)(2,1)}, bf16[1024,256]{1,0:T(8,128)(2,1)S(1)}, u32[]{:S(2)}, u32[]{:S(2)}) collective-permute-start(bf16[1024,256]{1,0:T(8,128)(2,1)} %get-tuple-element.61), channel_id=1, source_target_pairs={{0,4},{4,8},{8,12},{12,0},{1,5},{5,9},{9,13},{13,1},{2,6},{6,10},{... | collective-permute-start | bytes 1572872 | tf_op jit(solution)/shard_map/ppermute | solution.py:119
  22.5 4.5 %collective-permute-start.3 = (bf16[1024,256]{1,0:T(8,128)(2,1)}, bf16[1024,256]{1,0:T(8,128)(2,1)S(1)}, u32[]{:S(2)}, u32[]{:S(2)}) collective-permute-start(bf16[1024,256]{1,0:T(8,128)(2,1)} %get-tuple-element.62), channel_id=1, source_target_pairs={{0,8},{4,12},{8,0},{12,4},{1,9},{5,13},{9,1},{13,5},{2,10},{6,14},... | collective-permute-start | bytes 1572872 | tf_op jit(solution)/shard_map/ppermute | solution.py:119
  27.0 3.0 %collective-permute-start.4 = (bf16[1024,256]{1,0:T(8,128)(2,1)S(1)}, bf16[1024,256]{1,0:T(8,128)(2,1)S(1)}, u32[]{:S(2)}, u32[]{:S(2)}) collective-permute-start(bf16[1024,256]{1,0:T(8,128)(2,1)S(1)} %get-tuple-element.63), channel_id=1, source_target_pairs={{0,12},{4,0},{8,4},{12,8},{1,13},{5,1},{9,5},{13,9},{2,14},{6,2},{... | collective-permute-start | bytes 1572872 | tf_op jit(solution)/shard_map/ppermute | solution.py:119
  30.0 0.0 all-to-all-done.4
  30.0 1.4 convert_reduce_fusion.1
  31.4 1.1 subtract_convert_fusion.1
  32.4 80.8 %while.12 = (s32[]{:T(128)}, bf16[64,1792]{1,0:T(8,128)(2,1)S(1)}, s32[]{:T(128)}, s32[]{:T(128)}, bf16[]{:T(256)}) while((s32[]{:T(128)}, bf16[64,1792]{1,0:T(8,128)(2,1)S(1)}, s32[]{:T(128)}, s32[]{:T(128)}, bf16[]{:T(256)}) %tuple.41), condition=%wide.region_4.0_spmd, body=%wide.region_1.0_spmd.sunk | while | flops 157698 | bytes 2379871 | solution.py:129
  32.5 18.0 %all_to_all.41 = bf16[4,16,1792]{2,1,0:T(8,128)(2,1)S(1)} all-to-all(bf16[4,16,1792]{2,1,0:T(8,128)(2,1)S(1)} %bitcast.10), channel_id=1, replica_groups=mesh['zo'=4,'zi'=4,'x'=4,'y'=4,'h'=2,'c'=2] {'zi'}, dimensions={0} | all-to-all | bytes 458752 | tf_op jit(solution)/shard_map/while/body/all_to_all | solution.py:91
  50.5 30.2 %all_to_all.42 = bf16[4,4,1792]{2,1,0:T(4,128)(2,1)S(1)} all-to-all(bf16[4,4,1792]{2,1,0:T(4,128)(2,1)S(1)} %reshape.34), channel_id=1, replica_groups=mesh['zo'=4,'zi'=4,'x'=4,'y'=4,'h'=2,'c'=2] {'zo'}, dimensions={0} | all-to-all | bytes 114688 | tf_op jit(solution)/shard_map/while/body/all_to_all | solution.py:91
  80.8 20.8 %all_to_all.43 = bf16[4,4,1792]{2,1,0:T(4,128)(2,1)S(1)} all-to-all(bf16[4,4,1792]{2,1,0:T(4,128)(2,1)S(1)} %broadcast_in_dim.14), channel_id=1, replica_groups=mesh['zo'=4,'zi'=4,'x'=4,'y'=4,'h'=2,'c'=2] {'zo'}, dimensions={0} | all-to-all | bytes 114688 | tf_op jit(solution)/shard_map/while/body/all_to_all | solution.py:91
  101.6 0.7 broadcast_in_dim.15
  102.3 5.9 %all-to-all-start.3 = ((bf16[4,16,1792]{2,1,0:T(8,128)(2,1)}), bf16[4,16,1792]{2,1,0:T(8,128)(2,1)S(1)}, u32[]{:S(2)}, u32[]{:S(2)}) async-start(bf16[4,16,1792]{2,1,0:T(8,128)(2,1)} %broadcast_in_dim.15), calls=%async_computation.3 | async-start | bytes 458752 | tf_op jit(solution)/shard_map/while/body/all_to_all | solution.py:91
  108.2 5.1 %all-to-all-done.3 = bf16[4,16,1792]{2,1,0:T(8,128)(2,1)S(1)} async-done(((bf16[4,16,1792]{2,1,0:T(8,128)(2,1)}), bf16[4,16,1792]{2,1,0:T(8,128)(2,1)S(1)}, u32[]{:S(2)}, u32[]{:S(2)}) %all-to-all-start.3) | async-done | bytes 229408 | tf_op jit(solution)/shard_map/while/body/all_to_all | solution.py:91
  113.3 0.0 collective-permute-done.2
  113.3 0.0 collective-permute-done.3
  113.3 0.0 collective-permute-done.4
  113.3 0.0 copy-start.3
  113.3 0.2 convert_add_fusion
  113.6 0.0 copy-start.2
  113.7 11.7 %collective-permute-start.5 = (bf16[1024,128]{1,0:T(8,128)(2,1)S(1)}, bf16[1024,128]{1,0:T(8,128)(2,1)S(1)}, u32[]{:S(2)}, u32[]{:S(2)}) collective-permute-start(bf16[1024,128]{1,0:T(8,128)(2,1)S(1)} %slice.12), channel_id=1, source_target_pairs={{0,2},{2,0},{1,3},{3,1},{4,6},{6,4},{5,7},{7,5},{8,10},{10,8},{9,1... | collective-permute-start | bytes 786440 | tf_op jit(solution)/shard_map/ppermute | solution.py:138
  125.4 12.0 %all_gather.3 = bf16[256,1792]{1,0:T(8,128)(2,1)S(1)} all-gather(bf16[64,1792]{1,0:T(8,128)(2,1)S(1)} %get-tuple-element.70), channel_id=1, replica_groups=mesh['zo'=4,'zi'=4,'x'=4,'y'=4,'h'=2,'c'=2] {'x'}, dimensions={0}, use_global_device_ids=true | all-gather | bytes 1146880 | tf_op jit(solution)/shard_map/all_gather | solution.py:139
  137.4 0.0 copy-done.3
  137.4 0.0 copy-done.2
  137.4 1.4 subtract_convert_fusion
  138.8 0.1 convert_element_type.59
  138.9 0.7 multiply_subtract_fusion
  139.6 41.9 %collective-permute-done.5 = bf16[1024,128]{1,0:T(8,128)(2,1)S(1)} collective-permute-done((bf16[1024,128]{1,0:T(8,128)(2,1)S(1)}, bf16[1024,128]{1,0:T(8,128)(2,1)S(1)}, u32[]{:S(2)}, u32[]{:S(2)}) %collective-permute-start.5) | collective-permute-done | bytes 262176 | tf_op jit(solution)/shard_map/ppermute | solution.py:138
  181.4 0.8 add_convert_fusion
  (8 shorter events, 0.2 us)
Async XLA Ops:
  0.7 1.6 copy-start
  2.3 10.2 %copy-start.1 = (bf16[512,2048]{1,0:T(8,128)(2,1)S(1)}, bf16[512,2048]{1,0:T(8,128)(2,1)}, u32[]{:S(2)}) copy-start(bf16[512,2048]{1,0:T(8,128)(2,1)} %far_ref.3) | copy-start | bytes 6291460
  3.7 8.8 %collective-permute-start.1 = (bf16[512,1024]{1,0:T(8,128)(2,1)S(1)}, bf16[512,1024]{1,0:T(8,128)(2,1)}, u32[]{:S(2)}, u32[]{:S(2)}) collective-permute-start(bf16[512,1024]{1,0:T(8,128)(2,1)S(1)} %shard_map.84), channel_id=1, source_target_pairs={{0,1},{1,0},{2,3},{3,2},{4,5},{5,4},{6,7},{7,6},{8,9},{9,8},{10,11... | collective-permute-start | bytes 3145736 | tf_op jit(solution)/shard_map/ppermute | solution.py:112
  6.3 6.2 %collective-permute-start = (bf16[1024,512]{1,0:T(8,128)(2,1)}, bf16[1024,512]{1,0:T(8,128)(2,1)}, u32[]{:S(2)}, u32[]{:S(2)}) collective-permute-start(bf16[1024,512]{1,0:T(8,128)(2,1)} %own_ref.1), channel_id=1, source_target_pairs={{0,1},{1,0},{2,3},{3,2},{4,5},{5,4},{6,7},{7,6},{8,9},{9,8},{10,11... | collective-permute-start | bytes 3145736 | tf_op jit(solution)/shard_map/ppermute | solution.py:111
  8.2 21.8 %all-to-all-start.4 = ((bf16[4,64,1792]{2,1,0:T(8,128)(2,1)}), bf16[4,64,1792]{2,1,0:T(8,128)(2,1)}, u32[]{:S(2)}, u32[]{:S(2)}) async-start(bf16[4,64,1792]{2,1,0:T(8,128)(2,1)} %bitcast.12), calls=%async_computation.4 | async-start | bytes 1835008 | tf_op jit(solution)/shard_map/all_to_all | solution.py:91
  19.3 94.0 %collective-permute-start.2 = (bf16[1024,256]{1,0:T(8,128)(2,1)}, bf16[1024,256]{1,0:T(8,128)(2,1)S(1)}, u32[]{:S(2)}, u32[]{:S(2)}) collective-permute-start(bf16[1024,256]{1,0:T(8,128)(2,1)} %get-tuple-element.61), channel_id=1, source_target_pairs={{0,4},{4,8},{8,12},{12,0},{1,5},{5,9},{9,13},{13,1},{2,6},{6,10},{... | collective-permute-start | bytes 1572872 | tf_op jit(solution)/shard_map/ppermute | solution.py:119
  22.5 90.8 %collective-permute-start.3 = (bf16[1024,256]{1,0:T(8,128)(2,1)}, bf16[1024,256]{1,0:T(8,128)(2,1)S(1)}, u32[]{:S(2)}, u32[]{:S(2)}) collective-permute-start(bf16[1024,256]{1,0:T(8,128)(2,1)} %get-tuple-element.62), channel_id=1, source_target_pairs={{0,8},{4,12},{8,0},{12,4},{1,9},{5,13},{9,1},{13,5},{2,10},{6,14},... | collective-permute-start | bytes 1572872 | tf_op jit(solution)/shard_map/ppermute | solution.py:119
  27.0 86.3 %collective-permute-start.4 = (bf16[1024,256]{1,0:T(8,128)(2,1)S(1)}, bf16[1024,256]{1,0:T(8,128)(2,1)S(1)}, u32[]{:S(2)}, u32[]{:S(2)}) collective-permute-start(bf16[1024,256]{1,0:T(8,128)(2,1)S(1)} %get-tuple-element.63), channel_id=1, source_target_pairs={{0,12},{4,0},{8,4},{12,8},{1,13},{5,1},{9,5},{13,9},{2,14},{6,2},{... | collective-permute-start | bytes 1572872 | tf_op jit(solution)/shard_map/ppermute | solution.py:119
  102.3 11.0 %all-to-all-start.3 = ((bf16[4,16,1792]{2,1,0:T(8,128)(2,1)}), bf16[4,16,1792]{2,1,0:T(8,128)(2,1)S(1)}, u32[]{:S(2)}, u32[]{:S(2)}) async-start(bf16[4,16,1792]{2,1,0:T(8,128)(2,1)} %broadcast_in_dim.15), calls=%async_computation.3 | async-start | bytes 458752 | tf_op jit(solution)/shard_map/while/body/all_to_all | solution.py:91
  113.3 24.1 %copy-start.3 = (f32[256,1792]{1,0:T(8,128)S(1)}, f32[256,1792]{1,0:T(8,128)}, u32[]{:S(2)}) copy-start(f32[256,1792]{1,0:T(8,128)} %param.9) | copy-start | bytes 5505028
  113.6 23.8 %copy-start.2 = (f32[256,1792]{1,0:T(8,128)S(1)}, f32[256,1792]{1,0:T(8,128)}, u32[]{:S(2)}) copy-start(f32[256,1792]{1,0:T(8,128)} %param.8) | copy-start | bytes 5505028
  113.7 67.7 %collective-permute-start.5 = (bf16[1024,128]{1,0:T(8,128)(2,1)S(1)}, bf16[1024,128]{1,0:T(8,128)(2,1)S(1)}, u32[]{:S(2)}, u32[]{:S(2)}) collective-permute-start(bf16[1024,128]{1,0:T(8,128)(2,1)S(1)} %slice.12), channel_id=1, source_target_pairs={{0,2},{2,0},{1,3},{3,1},{4,6},{6,4},{5,7},{7,5},{8,10},{10,8},{9,1... | collective-permute-start | bytes 786440 | tf_op jit(solution)/shard_map/ppermute | solution.py:138

commit v3 on v2

--- a/solution.py
+++ b/solution.py
@@ -116,27 +116,38 @@
     anchor = lax.dynamic_slice_in_dim(base, x * per_x, per_x, 0).astype(bf16).astype(f32)
     total = (terms.astype(f32).sum(axis=0) - n_x * anchor).astype(bf16)
 
-    pieces = [lax.ppermute(part[step], "y", shift("y", n_y, step)) for step in range(1, n_y)]
+    part = [part[0]] + [lax.ppermute(part[step], "y", shift("y", n_y, step)) for step in range(1, n_y)]
 
-    def over_z(total):
+    once = 1 + (h >> 4)
+
+    def over_zi(total):
         terms = exchange(total.reshape(n_zi, per_zi, width), "zi")
-        total = terms.astype(f32).sum(axis=0).astype(bf16)
-        terms = exchange(total.reshape(n_zo, own, width), "zo")
-        outer_grad = (-terms.astype(f32).sum(axis=0) / groups).astype(bf16)
-        gathered = gather_small(outer_grad, "zo", n_zo).reshape(per_zi, width)
-        return gather_small(gathered, "zi", n_zi).reshape(per_x, width)
+        return terms.astype(f32).sum(axis=0).astype(bf16)
 
-    outer_grad = lax.fori_loop(0, 1 + (h >> 4), lambda _, value: over_z(value), total)
+    empty = jnp.zeros((per_zi, width), bf16)
+    total = lax.fori_loop(0, once, lambda _, carry: (carry[0] + carry[0], over_zi(carry[0])), (total, empty))[1]
 
-    pieces = lax.optimization_barrier((outer_grad, *pieces))[1:]
-    total = part[0].astype(f32)
-    for piece in pieces:
-        total += piece.astype(f32)
-    mine, other = total[:, :LANES], total[:, LANES:].astype(bf16)
-    mine, other = lax.optimization_barrier((mine, other))
-    outer_grad = after(outer_grad, other)
+    total, *part = lax.optimization_barrier((total, *part))
+
+    terms = gather_small(total, "zo", n_zo)
+
+    kv = part[0].astype(f32)
+    for piece in part[1:]:
+        kv += piece.astype(f32)
+    mine, other = lax.optimization_barrier((kv[:, :LANES], kv[:, LANES:].astype(bf16)))
     there = lax.ppermute(other, "h", swap)
-    outer_grad = lax.all_gather(outer_grad, "x", axis=0, tiled=True).astype(f32)
+
+    terms = after(terms, other)
+    outer_grad = (-terms.astype(f32).sum(axis=0) / groups).astype(bf16)
+
+    def over_zi_and_x(outer_grad):
+        gathered = gather_small(outer_grad, "zi", n_zi).reshape(per_x, width)
+        return lax.all_gather(gathered, "x", axis=0, tiled=True)
+
+    empty = jnp.zeros((rows, width), bf16)
+    outer_grad = lax.fori_loop(
+        0, once, lambda _, carry: (carry[0] + carry[0], over_zi_and_x(carry[0])), (outer_grad, empty)
+    )[1].astype(f32)
 
     def step(outer_grad, base, momentum):
         new_momentum = 0.9 * momentum + outer_grad

time: 183 us -> 175 us (0.956)
  the two profiles are of different devices: /device:TPU:33 before, /device:TPU:8 now
where the time goes in v3:
time: 175 us; the launch traced here: 174 us
  waiting for transfers between devices  68.7 us (39%)
  starting transfers between devices  62.5 us (36%)
  blocking collectives  14.8 us (8%)
  other arithmetic  12.4 us (7%)
  Pallas kernels  8.17 us (5%)
  local copies, waits for them, and re-layouts  6.21 us (4%)
    all_to_all x4, waiting for transfers between devices, exchange(): return lax.all_to_all(array, axis, split_axis=0, concat_axis=0, tiled=True)  63.1 us
    all_to_all x4, starting transfers between devices, exchange(): return lax.all_to_all(array, axis, split_axis=0, concat_axis=0, tiled=True)  22.7 us
    ppermute x3, starting transfers between devices, shards(): lax.ppermute(part[step], 'y', shift('y', n_y, step))  20.9 us
    all_gather x1, blocking collectives, over_zi_and_x(): return lax.all_gather(gathered, 'x', axis=0, tiled=True)  14.8 us
    ppermute x1, starting transfers between devices, shards(): there = lax.ppermute(other, 'h', swap)  14.6 us
    pallas_call x1, Pallas kernels, project(): pl.pallas_call(project_kernel, out_shape=[jax.ShapeDtypeStruct((rows, 2 *...  6.81 us
    ppermute x3, waiting for transfers between devices, shards(): lax.ppermute(part[step], 'y', shift('y', n_y, step))  5.6 us
  transfers between devices with their start and end apart: 10, of which 4 were waited for; matrix products, arithmetic and copies ran while one was open for 8% of the time, Pallas kernels for 4%

profile of v3, /device:TPU:8, one launch (start us, length us, event | category | flops | bytes accessed | tf_op | source)
XLA Modules:
  0.0 173.6 jit_solution(9718850330502575256)
XLA Ops:
  0.6 0.1 pad_add_fusion.place_ref
  0.7 0.0 copy-start
  0.7 1.6 copy-done
  2.3 0.0 copy-start.1
  2.3 1.4 shard_map.84
  3.7 1.9 %collective-permute-start.1 = (bf16[512,1024]{1,0:T(8,128)(2,1)S(1)}, bf16[512,1024]{1,0:T(8,128)(2,1)}, u32[]{:S(2)}, u32[]{:S(2)}) collective-permute-start(bf16[512,1024]{1,0:T(8,128)(2,1)S(1)} %shard_map.84), channel_id=1, source_target_pairs={{0,1},{1,0},{2,3},{3,2},{4,5},{5,4},{6,7},{7,6},{8,9},{9,8},{10,11... | collective-permute-start | bytes 3145736 | tf_op jit(solution)/shard_map/ppermute | solution.py:112
  5.6 2.4 %collective-permute-start = (bf16[1024,512]{1,0:T(8,128)(2,1)}, bf16[1024,512]{1,0:T(8,128)(2,1)}, u32[]{:S(2)}, u32[]{:S(2)}) collective-permute-start(bf16[1024,512]{1,0:T(8,128)(2,1)} %own_ref.1), channel_id=1, source_target_pairs={{0,1},{1,0},{2,3},{3,2},{4,5},{5,4},{6,7},{7,6},{8,9},{9,8},{10,11... | collective-permute-start | bytes 3145736 | tf_op jit(solution)/shard_map/ppermute | solution.py:111
  8.0 4.3 %all-to-all-start.2 = ((bf16[4,64,1792]{2,1,0:T(8,128)(2,1)}), bf16[4,64,1792]{2,1,0:T(8,128)(2,1)}, u32[]{:S(2)}, u32[]{:S(2)}) async-start(bf16[4,64,1792]{2,1,0:T(8,128)(2,1)} %bitcast.11), calls=%async_computation.2 | async-start | bytes 1835008 | tf_op jit(solution)/shard_map/all_to_all | solution.py:91
  12.3 0.0 collective-permute-done.1.packed_ref
  12.3 0.0 collective-permute-done.sibling_ref
  12.3 0.0 copy-done.1
  12.4 6.8 %shard_map.85 = (bf16[1024,256]{1,0:T(8,128)(2,1)S(1)}, bf16[1024,256]{1,0:T(8,128)(2,1)}, bf16[1024,256]{1,0:T(8,128)(2,1)}, bf16[1024,256]{1,0:T(8,128)(2,1)S(1)}) custom-call(s32[3]{0:T(128)S(1)} %pad_add_fusion.place_ref, bf16[1024,512]{1,0:T(8,128)(2,1)} %own_ref.1, bf16[1024,512]{1,0:T(8,128)(2,1)} %collective-permute-done.sibling_ref, ...), custom_call_target="tpu_custom_call" | custom-call | flops 2147483648 | bytes 6291456 | tf_op jit(solution)/shard_map/pallas_call | solution.py:60
  19.2 3.5 %collective-permute-start.2 = (bf16[1024,256]{1,0:T(8,128)(2,1)}, bf16[1024,256]{1,0:T(8,128)(2,1)S(1)}, u32[]{:S(2)}, u32[]{:S(2)}) collective-permute-start(bf16[1024,256]{1,0:T(8,128)(2,1)} %get-tuple-element.93), channel_id=1, source_target_pairs={{0,4},{4,8},{8,12},{12,0},{1,5},{5,9},{9,13},{13,1},{2,6},{6,10},{... | collective-permute-start | bytes 1572872 | tf_op jit(solution)/shard_map/ppermute | solution.py:119
  22.6 15.5 %collective-permute-start.3 = (bf16[1024,256]{1,0:T(8,128)(2,1)}, bf16[1024,256]{1,0:T(8,128)(2,1)}, u32[]{:S(2)}, u32[]{:S(2)}) collective-permute-start(bf16[1024,256]{1,0:T(8,128)(2,1)} %get-tuple-element.94), channel_id=1, source_target_pairs={{0,8},{4,12},{8,0},{12,4},{1,9},{5,13},{9,1},{13,5},{2,10},{6,14},... | collective-permute-start | bytes 1572872 | tf_op jit(solution)/shard_map/ppermute | solution.py:119
  38.1 1.9 %collective-permute-start.4 = (bf16[1024,256]{1,0:T(8,128)(2,1)S(1)}, bf16[1024,256]{1,0:T(8,128)(2,1)}, u32[]{:S(2)}, u32[]{:S(2)}) collective-permute-start(bf16[1024,256]{1,0:T(8,128)(2,1)S(1)} %get-tuple-element.95), channel_id=1, source_target_pairs={{0,12},{4,0},{8,4},{12,8},{1,13},{5,1},{9,5},{13,9},{2,14},{6,2},{... | collective-permute-start | bytes 1572872 | tf_op jit(solution)/shard_map/ppermute | solution.py:119
  40.0 0.0 all-to-all-done.2
  40.0 1.4 convert_reduce_fusion
  41.4 1.1 subtract_convert_fusion.1
  42.5 0.6 broadcast_in_dim.12
  43.1 12.8 %while.26 = (s32[]{:T(128)}, bf16[64,1792]{1,0:T(8,128)(2,1)S(1)}, bf16[16,1792]{1,0:T(8,128)(2,1)}, s32[]{:T(128)}, s32[]{:T(128)}, /*index=5*/bf16[]{:T(256)}) while((s32[]{:T(128)}, bf16[64,1792]{1,0:T(8,128)(2,1)S(1)}, bf16[16,1792]{1,0:T(8,128)(2,1)}, s32[]{:T(128)}, s32[]{:T(128)}, /*index=5*/bf16[]{:T(256)}) %tuple.54), condition=%wide.region_3.0_spmd, body=%wide.region_1.0_spmd.sunk | while | flops 200706 | bytes 2121831 | solution.py:128
  43.1 0.7 copy.13
  43.8 3.4 %all-to-all-start = ((bf16[4,16,1792]{2,1,0:T(8,128)(2,1)}), bf16[4,16,1792]{2,1,0:T(8,128)(2,1)S(1)}, u32[]{:S(2)}, u32[]{:S(2)}) async-start(bf16[4,16,1792]{2,1,0:T(8,128)(2,1)} %bitcast.8), calls=%async_computation | async-start | bytes 458752 | tf_op jit(solution)/shard_map/while/body/all_to_all | solution.py:91
  47.2 1.1 add.90
  48.3 6.9 %all-to-all-done = bf16[4,16,1792]{2,1,0:T(8,128)(2,1)S(1)} async-done(((bf16[4,16,1792]{2,1,0:T(8,128)(2,1)}), bf16[4,16,1792]{2,1,0:T(8,128)(2,1)S(1)}, u32[]{:S(2)}, u32[]{:S(2)}) %all-to-all-start) | async-done | bytes 229408 | tf_op jit(solution)/shard_map/while/body/all_to_all | solution.py:91
  55.2 0.7 reduce_sum.35
  55.9 0.0 collective-permute-done.2
  55.9 0.0 collective-permute-done.3
  55.9 5.6 %collective-permute-done.4 = bf16[1024,256]{1,0:T(8,128)(2,1)} collective-permute-done((bf16[1024,256]{1,0:T(8,128)(2,1)S(1)}, bf16[1024,256]{1,0:T(8,128)(2,1)}, u32[]{:S(2)}, u32[]{:S(2)}) %collective-permute-start.4) | collective-permute-done | bytes 524320 | tf_op jit(solution)/shard_map/ppermute | solution.py:119
  61.5 1.5 broadcast_in_dim.13
  63.0 11.4 %all-to-all-start.3 = ((bf16[4,16,1792]{2,1,0:T(8,128)(2,1)}), bf16[4,16,1792]{2,1,0:T(8,128)(2,1)S(1)}, u32[]{:S(2)}, u32[]{:S(2)}) async-start(bf16[4,16,1792]{2,1,0:T(8,128)(2,1)} %broadcast_in_dim.13), calls=%async_computation.3 | async-start | bytes 458752 | tf_op jit(solution)/shard_map/all_to_all | solution.py:91
  74.3 1.4 convert_add_fusion
  75.8 0.0 copy-start.3
  75.8 14.6 %collective-permute-start.5 = (bf16[1024,128]{1,0:T(8,128)(2,1)S(1)}, bf16[1024,128]{1,0:T(8,128)(2,1)}, u32[]{:S(2)}, u32[]{:S(2)}) collective-permute-start(bf16[1024,128]{1,0:T(8,128)(2,1)S(1)} %slice.12), channel_id=1, source_target_pairs={{0,2},{2,0},{1,3},{3,1},{4,6},{6,4},{5,7},{7,5},{8,10},{10,8},{9,1... | collective-permute-start | bytes 786440 | tf_op jit(solution)/shard_map/ppermute | solution.py:138
  90.4 44.1 %all-to-all-done.3 = bf16[4,16,1792]{2,1,0:T(8,128)(2,1)S(1)} async-done(((bf16[4,16,1792]{2,1,0:T(8,128)(2,1)}), bf16[4,16,1792]{2,1,0:T(8,128)(2,1)S(1)}, u32[]{:S(2)}, u32[]{:S(2)}) %all-to-all-start.3) | async-done | bytes 229408 | tf_op jit(solution)/shard_map/all_to_all | solution.py:91
  134.6 1.0 broadcast_in_dim.14
  135.6 0.0 copy-start.4
  135.6 0.0 copy-done.3
  135.6 31.3 %while.27 = (s32[]{:T(128)}, bf16[16,1792]{1,0:T(8,128)(2,1)S(1)}, bf16[256,1792]{1,0:T(8,128)(2,1)}, s32[]{:T(128)}, s32[]{:T(128)}) while((s32[]{:T(128)}, bf16[16,1792]{1,0:T(8,128)(2,1)S(1)}, bf16[256,1792]{1,0:T(8,128)(2,1)}, s32[]{:T(128)}, s32[]{:T(128)}) %tuple.57), condition=%wide.region_6.0_spmd, body=%wide.region_5.0_spmd.sunk | while | flops 28674 | bytes 2293853 | solution.py:148
  135.6 0.7 broadcast_in_dim.16
  136.3 3.7 %all-to-all-start.1 = ((bf16[4,16,1792]{2,1,0:T(8,128)(2,1)}), bf16[4,16,1792]{2,1,0:T(8,128)(2,1)S(1)}, u32[]{:S(2)}, u32[]{:S(2)}) async-start(bf16[4,16,1792]{2,1,0:T(8,128)(2,1)} %broadcast_in_dim.16), calls=%async_computation.1 | async-start | bytes 458752 | tf_op jit(solution)/shard_map/while/body/all_to_all | solution.py:91
  140.1 12.1 %all-to-all-done.1 = bf16[4,16,1792]{2,1,0:T(8,128)(2,1)S(1)} async-done(((bf16[4,16,1792]{2,1,0:T(8,128)(2,1)}), bf16[4,16,1792]{2,1,0:T(8,128)(2,1)S(1)}, u32[]{:S(2)}, u32[]{:S(2)}) %all-to-all-start.1) | async-done | bytes 229408 | tf_op jit(solution)/shard_map/while/body/all_to_all | solution.py:91
  152.1 14.8 %all_gather.4 = bf16[256,1792]{1,0:T(8,128)(2,1)} all-gather(bf16[64,1792]{1,0:T(8,128)(2,1)S(1)} %bitcast.10), channel_id=1, replica_groups=mesh['zo'=4,'zi'=4,'x'=4,'y'=4,'h'=2,'c'=2] {'x'}, dimensions={0}, use_global_device_ids=true | all-gather | bytes 1146880 | tf_op jit(solution)/shard_map/while/body/all_gather | solution.py:145
  166.9 0.0 copy-done.4
  166.9 0.0 copy-start.2
  166.9 3.3 %subtract_convert_fusion = bf16[256,1792]{1,0:T(8,128)(2,1)} fusion(f32[256,1792]{1,0:T(8,128)S(1)} %copy-done.4, f32[256,1792]{1,0:T(8,128)} %param.11, bf16[256,1792]{1,0:T(8,128)(2,1)} %get-tuple-element.105), kind=kLoop, calls=%fused_computation | loop fusion | flops 3670016 | bytes 5505024 | tf_op jit(solution)/shard_map/convert_element_type | solution.py:156
  170.2 0.0 copy-done.2
  170.2 0.0 slice-start
  170.2 0.1 convert_element_type.55
  170.3 1.5 multiply_subtract_fusion
  171.8 0.0 collective-permute-done.5
  171.8 0.0 slice-done
  171.8 1.7 add_convert_fusion
  (4 shorter events, 0.1 us)
Async XLA Ops:
  0.7 1.6 copy-start
  2.3 10.0 %copy-start.1 = (bf16[512,2048]{1,0:T(8,128)(2,1)S(1)}, bf16[512,2048]{1,0:T(8,128)(2,1)}, u32[]{:S(2)}) copy-start(bf16[512,2048]{1,0:T(8,128)(2,1)} %far_ref.3) | copy-start | bytes 6291460
  3.7 8.7 %collective-permute-start.1 = (bf16[512,1024]{1,0:T(8,128)(2,1)S(1)}, bf16[512,1024]{1,0:T(8,128)(2,1)}, u32[]{:S(2)}, u32[]{:S(2)}) collective-permute-start(bf16[512,1024]{1,0:T(8,128)(2,1)S(1)} %shard_map.84), channel_id=1, source_target_pairs={{0,1},{1,0},{2,3},{3,2},{4,5},{5,4},{6,7},{7,6},{8,9},{9,8},{10,11... | collective-permute-start | bytes 3145736 | tf_op jit(solution)/shard_map/ppermute | solution.py:112
  5.6 6.7 %collective-permute-start = (bf16[1024,512]{1,0:T(8,128)(2,1)}, bf16[1024,512]{1,0:T(8,128)(2,1)}, u32[]{:S(2)}, u32[]{:S(2)}) collective-permute-start(bf16[1024,512]{1,0:T(8,128)(2,1)} %own_ref.1), channel_id=1, source_target_pairs={{0,1},{1,0},{2,3},{3,2},{4,5},{5,4},{6,7},{7,6},{8,9},{9,8},{10,11... | collective-permute-start | bytes 3145736 | tf_op jit(solution)/shard_map/ppermute | solution.py:111
  8.0 32.0 %all-to-all-start.2 = ((bf16[4,64,1792]{2,1,0:T(8,128)(2,1)}), bf16[4,64,1792]{2,1,0:T(8,128)(2,1)}, u32[]{:S(2)}, u32[]{:S(2)}) async-start(bf16[4,64,1792]{2,1,0:T(8,128)(2,1)} %bitcast.11), calls=%async_computation.2 | async-start | bytes 1835008 | tf_op jit(solution)/shard_map/all_to_all | solution.py:91
  19.2 36.7 %collective-permute-start.2 = (bf16[1024,256]{1,0:T(8,128)(2,1)}, bf16[1024,256]{1,0:T(8,128)(2,1)S(1)}, u32[]{:S(2)}, u32[]{:S(2)}) collective-permute-start(bf16[1024,256]{1,0:T(8,128)(2,1)} %get-tuple-element.93), channel_id=1, source_target_pairs={{0,4},{4,8},{8,12},{12,0},{1,5},{5,9},{9,13},{13,1},{2,6},{6,10},{... | collective-permute-start | bytes 1572872 | tf_op jit(solution)/shard_map/ppermute | solution.py:119
  22.6 33.2 %collective-permute-start.3 = (bf16[1024,256]{1,0:T(8,128)(2,1)}, bf16[1024,256]{1,0:T(8,128)(2,1)}, u32[]{:S(2)}, u32[]{:S(2)}) collective-permute-start(bf16[1024,256]{1,0:T(8,128)(2,1)} %get-tuple-element.94), channel_id=1, source_target_pairs={{0,8},{4,12},{8,0},{12,4},{1,9},{5,13},{9,1},{13,5},{2,10},{6,14},... | collective-permute-start | bytes 1572872 | tf_op jit(solution)/shard_map/ppermute | solution.py:119
  38.1 23.4 %collective-permute-start.4 = (bf16[1024,256]{1,0:T(8,128)(2,1)S(1)}, bf16[1024,256]{1,0:T(8,128)(2,1)}, u32[]{:S(2)}, u32[]{:S(2)}) collective-permute-start(bf16[1024,256]{1,0:T(8,128)(2,1)S(1)} %get-tuple-element.95), channel_id=1, source_target_pairs={{0,12},{4,0},{8,4},{12,8},{1,13},{5,1},{9,5},{13,9},{2,14},{6,2},{... | collective-permute-start | bytes 1572872 | tf_op jit(solution)/shard_map/ppermute | solution.py:119
  43.8 11.4 %all-to-all-start = ((bf16[4,16,1792]{2,1,0:T(8,128)(2,1)}), bf16[4,16,1792]{2,1,0:T(8,128)(2,1)S(1)}, u32[]{:S(2)}, u32[]{:S(2)}) async-start(bf16[4,16,1792]{2,1,0:T(8,128)(2,1)} %bitcast.8), calls=%async_computation | async-start | bytes 458752 | tf_op jit(solution)/shard_map/while/body/all_to_all | solution.py:91
  63.0 71.6 %all-to-all-start.3 = ((bf16[4,16,1792]{2,1,0:T(8,128)(2,1)}), bf16[4,16,1792]{2,1,0:T(8,128)(2,1)S(1)}, u32[]{:S(2)}, u32[]{:S(2)}) async-start(bf16[4,16,1792]{2,1,0:T(8,128)(2,1)} %broadcast_in_dim.13), calls=%async_computation.3 | async-start | bytes 458752 | tf_op jit(solution)/shard_map/all_to_all | solution.py:91
  75.8 59.8 %copy-start.3 = (f32[1024,256]{1,0:T(8,128)}, f32[1024,256]{1,0:T(8,128)S(1)}, u32[]{:S(2)}) copy-start(f32[1024,256]{1,0:T(8,128)S(1)} %convert_add_fusion) | copy-start | bytes 3145732
  75.8 96.0 %collective-permute-start.5 = (bf16[1024,128]{1,0:T(8,128)(2,1)S(1)}, bf16[1024,128]{1,0:T(8,128)(2,1)}, u32[]{:S(2)}, u32[]{:S(2)}) collective-permute-start(bf16[1024,128]{1,0:T(8,128)(2,1)S(1)} %slice.12), channel_id=1, source_target_pairs={{0,2},{2,0},{1,3},{3,1},{4,6},{6,4},{5,7},{7,5},{8,10},{10,8},{9,1... | collective-permute-start | bytes 786440 | tf_op jit(solution)/shard_map/ppermute | solution.py:138
  135.6 31.3 %copy-start.4 = (f32[256,1792]{1,0:T(8,128)S(1)}, f32[256,1792]{1,0:T(8,128)}, u32[]{:S(2)}) copy-start(f32[256,1792]{1,0:T(8,128)} %param.10) | copy-start | bytes 5505028
  136.3 15.8 %all-to-all-start.1 = ((bf16[4,16,1792]{2,1,0:T(8,128)(2,1)}), bf16[4,16,1792]{2,1,0:T(8,128)(2,1)S(1)}, u32[]{:S(2)}, u32[]{:S(2)}) async-start(bf16[4,16,1792]{2,1,0:T(8,128)(2,1)} %broadcast_in_dim.16), calls=%async_computation.1 | async-start | bytes 458752 | tf_op jit(solution)/shard_map/while/body/all_to_all | solution.py:91
  166.9 3.3 %copy-start.2 = (bf16[256,1792]{1,0:T(8,128)(2,1)S(1)}, bf16[256,1792]{1,0:T(8,128)(2,1)}, u32[]{:S(2)}) copy-start(bf16[256,1792]{1,0:T(8,128)(2,1)} %get-tuple-element.105) | copy-start | bytes 2752516
  170.2 1.6 slice-start

commit v4 on v3

--- a/solution.py
+++ b/solution.py
@@ -106,30 +106,34 @@
     per_x, per_zi = rows // n_x, rows // (n_x * n_zi)
 
     terms = exchange(local_weights[0].reshape(n_x, per_x, width), "x")
+    anchor = lax.dynamic_slice_in_dim(base, x * per_x, per_x, 0).astype(bf16).astype(f32)
+    total = (terms.astype(f32).sum(axis=0) - n_x * anchor).astype(bf16)
 
     place = jnp.stack([h, c, y]).astype(jnp.int32)
     sibling = lax.ppermute(tokens, "c", swap)
     packed = lax.ppermute(pack(place, weight, n_y), "c", swap)
+
+    total, sibling, packed = lax.optimization_barrier((total, sibling, packed))
+    terms = exchange(total.reshape(n_zi, per_zi, width), "zi")
     part = project(place, tokens, sibling, weight, packed, n_y)
-
     terms = after(terms, *part)
-    anchor = lax.dynamic_slice_in_dim(base, x * per_x, per_x, 0).astype(bf16).astype(f32)
-    total = (terms.astype(f32).sum(axis=0) - n_x * anchor).astype(bf16)
-
+    total = terms.astype(f32).sum(axis=0).astype(bf16)
+    total, *part = lax.optimization_barrier((total, *part))
     part = [part[0]] + [lax.ppermute(part[step], "y", shift("y", n_y, step)) for step in range(1, n_y)]
 
     once = 1 + (h >> 4)
 
-    def over_zi(total):
-        terms = exchange(total.reshape(n_zi, per_zi, width), "zi")
-        return terms.astype(f32).sum(axis=0).astype(bf16)
+    def alone(function, value, shape):
+        carry = (value, jnp.zeros(shape, bf16))
+        return lax.fori_loop(0, once, lambda _, carry: (-carry[0], function(carry[0])), carry)[1]
 
-    empty = jnp.zeros((per_zi, width), bf16)
-    total = lax.fori_loop(0, once, lambda _, carry: (carry[0] + carry[0], over_zi(carry[0])), (total, empty))[1]
+    def over_zo(total):
+        terms = gather_small(total, "zo", n_zo)
+        return (-terms.astype(f32).sum(axis=0) / groups).astype(bf16)
 
-    total, *part = lax.optimization_barrier((total, *part))
-
-    terms = gather_small(total, "zo", n_zo)
+    outer_grad = alone(over_zo, total, (per_zi, width))
+    outer_grad, *part = lax.optimization_barrier((outer_grad, *part))
+    gathered = gather_small(outer_grad, "zi", n_zi)
 
     kv = part[0].astype(f32)
     for piece in part[1:]:
@@ -137,17 +141,9 @@
     mine, other = lax.optimization_barrier((kv[:, :LANES], kv[:, LANES:].astype(bf16)))
     there = lax.ppermute(other, "h", swap)
 
-    terms = after(terms, other)
-    outer_grad = (-terms.astype(f32).sum(axis=0) / groups).astype(bf16)
-
-    def over_zi_and_x(outer_grad):
-        gathered = gather_small(outer_grad, "zi", n_zi).reshape(per_x, width)
-        return lax.all_gather(gathered, "x", axis=0, tiled=True)
-
-    empty = jnp.zeros((rows, width), bf16)
-    outer_grad = lax.fori_loop(
-        0, once, lambda _, carry: (carry[0] + carry[0], over_zi_and_x(carry[0])), (outer_grad, empty)
-    )[1].astype(f32)
+    gathered = after(gathered, other).reshape(per_x, width)
+    outer_grad = alone(lambda value: lax.all_gather(value, "x", axis=0, tiled=True), gathered, (rows, width))
+    outer_grad = outer_grad.astype(f32)
 
     def step(outer_grad, base, momentum):
         new_momentum = 0.9 * momentum + outer_grad

time: 175 us -> 170 us (0.971)
  waiting for transfers between devices: 68.7 us -> 64.5 us
    ppermute x1, waiting for transfers between devices: 0.01 us -> 30 us  [shards(): there = lax.ppermute(other, 'h', swap)]
    all_to_all x4, waiting for transfers between devices: 63.1 us -> 34.5 us  [exchange(): return lax.all_to_all(array, axis, split_axis=0, concat_axis=0, tiled=True)]
    all_to_all x4, starting transfers between devices: 22.7 us -> 31.3 us  [exchange(): return lax.all_to_all(array, axis, split_axis=0, concat_axis=0, tiled=True)]
    ppermute x3, starting transfers between devices: 20.9 us -> 14.6 us  [shards(): lax.ppermute(part[step], 'y', shift('y', n_y, step))]
    ppermute x3, waiting for transfers between devices: 5.6 us -> 0.01 us  [shards(): lax.ppermute(part[step], 'y', shift('y', n_y, step))]
  transfers between devices with their start and end apart: 10 -> 10, of which waited for: 4 -> 3; matrix products, arithmetic and copies ran while one was open for 8% -> 7% of each run, Pallas kernels for 4% -> 4%
where the time goes in v4:
time: 170 us; the launch traced here: 169 us
  waiting for transfers between devices  64.5 us (38%)
  starting transfers between devices  63.4 us (37%)
  blocking collectives  14.3 us (8%)
  other arithmetic  11.9 us (7%)
  Pallas kernels  7.23 us (4%)
  local copies, waits for them, and re-layouts  7.17 us (4%)
    all_to_all x4, waiting for transfers between devices, exchange(): return lax.all_to_all(array, axis, split_axis=0, concat_axis=0, tiled=True)  34.5 us
    all_to_all x4, starting transfers between devices, exchange(): return lax.all_to_all(array, axis, split_axis=0, concat_axis=0, tiled=True)  31.3 us
    ppermute x1, waiting for transfers between devices, shards(): there = lax.ppermute(other, 'h', swap)  30 us
    ppermute x3, starting transfers between devices, shards(): lax.ppermute(part[step], 'y', shift('y', n_y, step))  14.6 us
    all_gather x1, blocking collectives, shards(): lax.all_gather(value, 'x', axis=0, tiled=True)  14.3 us
    ppermute x1, starting transfers between devices, shards(): there = lax.ppermute(other, 'h', swap)  13 us
    pallas_call x1, Pallas kernels, project(): pl.pallas_call(project_kernel, out_shape=[jax.ShapeDtypeStruct((rows, 2 *...  5.86 us
  transfers between devices with their start and end apart: 10, of which 3 were waited for; matrix products, arithmetic and copies ran while one was open for 7% of the time, Pallas kernels for 4%

profile of v4, /device:TPU:8, one launch (start us, length us, event | category | flops | bytes accessed | tf_op | source)
XLA Modules:
  0.0 169.3 jit_solution(8591026298920067912)
XLA Ops:
  0.6 4.3 %all-to-all-start.1 = ((bf16[4,64,1792]{2,1,0:T(8,128)(2,1)}), bf16[4,64,1792]{2,1,0:T(8,128)(2,1)}, u32[]{:S(2)}, u32[]{:S(2)}) async-start(bf16[4,64,1792]{2,1,0:T(8,128)(2,1)} %bitcast.7), calls=%async_computation.1 | async-start | bytes 1835008 | tf_op jit(solution)/shard_map/all_to_all | solution.py:91
  4.9 0.1 pad_add_fusion.place_ref
  5.0 0.0 copy-start
  5.0 1.6 copy-done
  6.6 1.4 shard_map.84
  8.0 0.0 copy-start.1
  8.0 2.1 %collective-permute-start.1 = (bf16[512,1024]{1,0:T(8,128)(2,1)S(1)}, bf16[512,1024]{1,0:T(8,128)(2,1)}, u32[]{:S(2)}, u32[]{:S(2)}) collective-permute-start(bf16[512,1024]{1,0:T(8,128)(2,1)S(1)} %shard_map.84), channel_id=1, source_target_pairs={{0,1},{1,0},{2,3},{3,2},{4,5},{5,4},{6,7},{7,6},{8,9},{9,8},{10,11... | collective-permute-start | bytes 3145736 | tf_op jit(solution)/shard_map/ppermute | solution.py:114
  10.0 2.4 %collective-permute-start = (bf16[1024,512]{1,0:T(8,128)(2,1)}, bf16[1024,512]{1,0:T(8,128)(2,1)}, u32[]{:S(2)}, u32[]{:S(2)}) collective-permute-start(bf16[1024,512]{1,0:T(8,128)(2,1)} %own_ref.1), channel_id=1, source_target_pairs={{0,1},{1,0},{2,3},{3,2},{4,5},{5,4},{6,7},{7,6},{8,9},{9,8},{10,11... | collective-permute-start | bytes 3145736 | tf_op jit(solution)/shard_map/ppermute | solution.py:113
  12.5 6.4 %all-to-all-done.1 = bf16[4,64,1792]{2,1,0:T(8,128)(2,1)} async-done(((bf16[4,64,1792]{2,1,0:T(8,128)(2,1)}), bf16[4,64,1792]{2,1,0:T(8,128)(2,1)}, u32[]{:S(2)}, u32[]{:S(2)}) %all-to-all-start.1) | async-done | bytes 917536 | tf_op jit(solution)/shard_map/all_to_all | solution.py:91
  18.9 1.4 convert_reduce_fusion.1
  20.3 1.8 %subtract_convert_fusion.1 = bf16[64,1792]{1,0:T(8,128)(2,1)} fusion(f32[64,1792]{1,0:T(8,128)S(1)} %convert_reduce_fusion.1, f32[256,1792]{1,0:T(8,128)} %param.10, s32[]{:T(128)S(6)} %select_n.9), kind=kLoop, calls=%fused_computation.7 | loop fusion | flops 458752 | bytes 917508 | tf_op jit(solution)/shard_map/convert_element_type | solution.py:110
  22.0 0.0 collective-permute-done.1.packed_ref
  22.0 0.0 collective-permute-done.sibling_ref
  22.0 5.9 %all-to-all-start.2 = ((bf16[4,16,1792]{2,1,0:T(8,128)(2,1)}), bf16[4,16,1792]{2,1,0:T(8,128)(2,1)S(1)}, u32[]{:S(2)}, u32[]{:S(2)}) async-start(bf16[4,16,1792]{2,1,0:T(8,128)(2,1)} %bitcast.4), calls=%async_computation.2 | async-start | bytes 458752 | tf_op jit(solution)/shard_map/all_to_all | solution.py:91
  27.9 0.0 copy-done.1
  27.9 5.9 %shard_map.85 = (bf16[1024,256]{1,0:T(8,128)(2,1)S(1)}, bf16[1024,256]{1,0:T(8,128)(2,1)S(1)}, bf16[1024,256]{1,0:T(8,128)(2,1)S(1)}, bf16[1024,256]{1,0:T(8,128)(2,1)S(1)}) custom-call(s32[3]{0:T(128)S(1)} %pad_add_fusion.place_ref, bf16[1024,512]{1,0:T(8,128)(2,1)} %own_ref.1, bf16[1024,512]{1,0:T(8,128)(2,1)} %collective-permute-done.sibling_ref, ...), custom_call_target="tpu_custom_call" | custom-call | flops 2147483648 | bytes 6291456 | tf_op jit(solution)/shard_map/pallas_call | solution.py:60
  33.8 0.0 copy-start.2
  33.8 0.8 copy-done.2
  34.6 0.0 copy-start.3
  34.6 0.8 copy-done.3
  35.4 0.0 all-to-all-done.2
  35.4 3.5 %collective-permute-start.2 = (bf16[1024,256]{1,0:T(8,128)(2,1)}, bf16[1024,256]{1,0:T(8,128)(2,1)S(1)}, u32[]{:S(2)}, u32[]{:S(2)}) collective-permute-start(bf16[1024,256]{1,0:T(8,128)(2,1)} %copy-done.3), channel_id=1, source_target_pairs={{0,4},{4,8},{8,12},{12,0},{1,5},{5,9},{9,13},{13,1},{2,6},{6,10},{... | collective-permute-start | bytes 1572872 | tf_op jit(solution)/shard_map/ppermute | solution.py:122
  38.9 9.2 %collective-permute-start.3 = (bf16[1024,256]{1,0:T(8,128)(2,1)}, bf16[1024,256]{1,0:T(8,128)(2,1)S(1)}, u32[]{:S(2)}, u32[]{:S(2)}) collective-permute-start(bf16[1024,256]{1,0:T(8,128)(2,1)} %copy-done.2), channel_id=1, source_target_pairs={{0,8},{4,12},{8,0},{12,4},{1,9},{5,13},{9,1},{13,5},{2,10},{6,14},... | collective-permute-start | bytes 1572872 | tf_op jit(solution)/shard_map/ppermute | solution.py:122
  48.2 1.9 %collective-permute-start.4 = (bf16[1024,256]{1,0:T(8,128)(2,1)S(1)}, bf16[1024,256]{1,0:T(8,128)(2,1)}, u32[]{:S(2)}, u32[]{:S(2)}) collective-permute-start(bf16[1024,256]{1,0:T(8,128)(2,1)S(1)} %get-tuple-element.83), channel_id=1, source_target_pairs={{0,12},{4,0},{8,4},{12,8},{1,13},{5,1},{9,5},{13,9},{2,14},{6,2},{... | collective-permute-start | bytes 1572872 | tf_op jit(solution)/shard_map/ppermute | solution.py:122
  50.1 0.6 broadcast_in_dim.12
  50.7 47.2 %while.24 = (s32[]{:T(128)}, bf16[16,1792]{1,0:T(8,128)(2,1)S(1)}, bf16[16,1792]{1,0:T(8,128)(2,1)}, s32[]{:T(128)}, s32[]{:T(128)}) while((s32[]{:T(128)}, bf16[16,1792]{1,0:T(8,128)(2,1)S(1)}, bf16[16,1792]{1,0:T(8,128)(2,1)}, s32[]{:T(128)}, s32[]{:T(128)}) %tuple.50), condition=%wide.region_4.0_spmd, body=%wide.region_2.0_spmd.sunk | while | flops 315394 | bytes 1605725 | solution.py:128
  50.7 0.7 broadcast_in_dim.16
  51.4 17.7 %all-to-all-start = ((bf16[4,16,1792]{2,1,0:T(8,128)(2,1)}), bf16[4,16,1792]{2,1,0:T(8,128)(2,1)S(1)}, u32[]{:S(2)}, u32[]{:S(2)}) async-start(bf16[4,16,1792]{2,1,0:T(8,128)(2,1)} %broadcast_in_dim.16), calls=%async_computation | async-start | bytes 458752 | tf_op jit(solution)/shard_map/while/body/all_to_all | solution.py:91
  69.2 28.1 %all-to-all-done = bf16[4,16,1792]{2,1,0:T(8,128)(2,1)S(1)} async-done(((bf16[4,16,1792]{2,1,0:T(8,128)(2,1)}), bf16[4,16,1792]{2,1,0:T(8,128)(2,1)S(1)}, u32[]{:S(2)}, u32[]{:S(2)}) %all-to-all-start) | async-done | bytes 229408 | tf_op jit(solution)/shard_map/while/body/all_to_all | solution.py:91
  97.3 0.6 multiply_convert_fusion.2
  97.9 0.0 collective-permute-done.2
  97.9 0.0 collective-permute-done.3
  97.9 0.0 copy-start.7
  97.9 0.0 collective-permute-done.4
  97.9 1.6 broadcast_in_dim.13
  99.5 3.4 %all-to-all-start.3 = ((bf16[4,16,1792]{2,1,0:T(8,128)(2,1)}), bf16[4,16,1792]{2,1,0:T(8,128)(2,1)S(1)}, u32[]{:S(2)}, u32[]{:S(2)}) async-start(bf16[4,16,1792]{2,1,0:T(8,128)(2,1)} %broadcast_in_dim.13), calls=%async_computation.3 | async-start | bytes 458752 | tf_op jit(solution)/shard_map/all_to_all | solution.py:91
  102.9 0.0 copy-done.7
  102.9 1.4 convert_add_fusion
  104.4 0.0 copy-start.5
  104.4 13.0 %collective-permute-start.5 = (bf16[1024,128]{1,0:T(8,128)(2,1)S(1)}, bf16[1024,128]{1,0:T(8,128)(2,1)}, u32[]{:S(2)}, u32[]{:S(2)}) collective-permute-start(bf16[1024,128]{1,0:T(8,128)(2,1)S(1)} %slice.12), channel_id=1, source_target_pairs={{0,2},{2,0},{1,3},{3,1},{4,6},{6,4},{5,7},{7,5},{8,10},{10,8},{9,1... | collective-permute-start | bytes 786440 | tf_op jit(solution)/shard_map/ppermute | solution.py:142
  117.4 0.0 all-to-all-done.3
  117.4 0.0 copy-start.6
  117.4 1.0 broadcast_in_dim.14
  118.4 0.0 copy-done.5
  118.4 14.4 %while.25 = (s32[]{:T(128)}, bf16[64,1792]{1,0:T(8,128)(2,1)S(1)}, bf16[256,1792]{1,0:T(8,128)(2,1)}, s32[]{:T(128)}, s32[]{:T(128)}) while((s32[]{:T(128)}, bf16[64,1792]{1,0:T(8,128)(2,1)S(1)}, bf16[256,1792]{1,0:T(8,128)(2,1)}, s32[]{:T(128)}, s32[]{:T(128)}) %tuple.56), condition=%wide.region_6.0_spmd, body=%wide.region_5.0_spmd.sunk | while | flops 114690 | bytes 1605693 | solution.py:128
  118.4 14.3 %all_gather.4 = bf16[256,1792]{1,0:T(8,128)(2,1)} all-gather(bf16[64,1792]{1,0:T(8,128)(2,1)S(1)} %get-tuple-element.181), channel_id=1, replica_groups=mesh['zo'=4,'zi'=4,'x'=4,'y'=4,'h'=2,'c'=2] {'x'}, dimensions={0}, use_global_device_ids=true | all-gather | bytes 1146880 | tf_op jit(solution)/shard_map/while/body/all_gather | solution.py:145
  132.8 0.1 neg.15
  132.8 0.0 copy-done.6
  132.8 0.0 copy-start.4
  132.8 3.2 %subtract_convert_fusion = bf16[256,1792]{1,0:T(8,128)(2,1)} fusion(f32[256,1792]{1,0:T(8,128)S(1)} %copy-done.6, f32[256,1792]{1,0:T(8,128)} %param.11, bf16[256,1792]{1,0:T(8,128)(2,1)} %get-tuple-element.91), kind=kLoop, calls=%fused_computation.2 | loop fusion | flops 3670016 | bytes 5505024 | tf_op jit(solution)/shard_map/convert_element_type | solution.py:152
  136.0 0.0 copy-done.4
  136.0 0.0 slice-start
  136.0 0.1 convert_element_type.53
  136.2 1.5 multiply_subtract_fusion
  137.7 30.0 %collective-permute-done.5 = bf16[1024,128]{1,0:T(8,128)(2,1)} collective-permute-done((bf16[1024,128]{1,0:T(8,128)(2,1)S(1)}, bf16[1024,128]{1,0:T(8,128)(2,1)}, u32[]{:S(2)}, u32[]{:S(2)}) %collective-permute-start.5) | collective-permute-done | bytes 262176 | tf_op jit(solution)/shard_map/ppermute | solution.py:142
  167.6 0.0 slice-done
  167.6 1.7 %add_convert_fusion = bf16[1024,128]{1,0:T(8,128)(2,1)} fusion(f32[1024,128]{1,0:T(8,128)S(1)} %slice-done, bf16[1024,128]{1,0:T(8,128)(2,1)} %collective-permute-done.5), kind=kLoop, calls=%fused_computation.6 | loop fusion | flops 393216 | bytes 1048576 | tf_op jit(solution)/shard_map/convert_element_type | solution.py:158
  (4 shorter events, 0.1 us)
Async XLA Ops:
  0.6 18.3 %all-to-all-start.1 = ((bf16[4,64,1792]{2,1,0:T(8,128)(2,1)}), bf16[4,64,1792]{2,1,0:T(8,128)(2,1)}, u32[]{:S(2)}, u32[]{:S(2)}) async-start(bf16[4,64,1792]{2,1,0:T(8,128)(2,1)} %bitcast.7), calls=%async_computation.1 | async-start | bytes 1835008 | tf_op jit(solution)/shard_map/all_to_all | solution.py:91
  5.0 1.6 copy-start
  8.0 19.9 %copy-start.1 = (bf16[512,2048]{1,0:T(8,128)(2,1)S(1)}, bf16[512,2048]{1,0:T(8,128)(2,1)}, u32[]{:S(2)}) copy-start(bf16[512,2048]{1,0:T(8,128)(2,1)} %far_ref.3) | copy-start | bytes 6291460
  8.0 14.0 %collective-permute-start.1 = (bf16[512,1024]{1,0:T(8,128)(2,1)S(1)}, bf16[512,1024]{1,0:T(8,128)(2,1)}, u32[]{:S(2)}, u32[]{:S(2)}) collective-permute-start(bf16[512,1024]{1,0:T(8,128)(2,1)S(1)} %shard_map.84), channel_id=1, source_target_pairs={{0,1},{1,0},{2,3},{3,2},{4,5},{5,4},{6,7},{7,6},{8,9},{9,8},{10,11... | collective-permute-start | bytes 3145736 | tf_op jit(solution)/shard_map/ppermute | solution.py:114
  10.0 12.0 %collective-permute-start = (bf16[1024,512]{1,0:T(8,128)(2,1)}, bf16[1024,512]{1,0:T(8,128)(2,1)}, u32[]{:S(2)}, u32[]{:S(2)}) collective-permute-start(bf16[1024,512]{1,0:T(8,128)(2,1)} %own_ref.1), channel_id=1, source_target_pairs={{0,1},{1,0},{2,3},{3,2},{4,5},{5,4},{6,7},{7,6},{8,9},{9,8},{10,11... | collective-permute-start | bytes 3145736 | tf_op jit(solution)/shard_map/ppermute | solution.py:113
  22.0 13.4 %all-to-all-start.2 = ((bf16[4,16,1792]{2,1,0:T(8,128)(2,1)}), bf16[4,16,1792]{2,1,0:T(8,128)(2,1)S(1)}, u32[]{:S(2)}, u32[]{:S(2)}) async-start(bf16[4,16,1792]{2,1,0:T(8,128)(2,1)} %bitcast.4), calls=%async_computation.2 | async-start | bytes 458752 | tf_op jit(solution)/shard_map/all_to_all | solution.py:91
  33.8 0.8 copy-start.2
  34.6 0.8 copy-start.3
  35.4 62.5 %collective-permute-start.2 = (bf16[1024,256]{1,0:T(8,128)(2,1)}, bf16[1024,256]{1,0:T(8,128)(2,1)S(1)}, u32[]{:S(2)}, u32[]{:S(2)}) collective-permute-start(bf16[1024,256]{1,0:T(8,128)(2,1)} %copy-done.3), channel_id=1, source_target_pairs={{0,4},{4,8},{8,12},{12,0},{1,5},{5,9},{9,13},{13,1},{2,6},{6,10},{... | collective-permute-start | bytes 1572872 | tf_op jit(solution)/shard_map/ppermute | solution.py:122
  38.9 59.0 %collective-permute-start.3 = (bf16[1024,256]{1,0:T(8,128)(2,1)}, bf16[1024,256]{1,0:T(8,128)(2,1)S(1)}, u32[]{:S(2)}, u32[]{:S(2)}) collective-permute-start(bf16[1024,256]{1,0:T(8,128)(2,1)} %copy-done.2), channel_id=1, source_target_pairs={{0,8},{4,12},{8,0},{12,4},{1,9},{5,13},{9,1},{13,5},{2,10},{6,14},... | collective-permute-start | bytes 1572872 | tf_op jit(solution)/shard_map/ppermute | solution.py:122
  48.2 49.8 %collective-permute-start.4 = (bf16[1024,256]{1,0:T(8,128)(2,1)S(1)}, bf16[1024,256]{1,0:T(8,128)(2,1)}, u32[]{:S(2)}, u32[]{:S(2)}) collective-permute-start(bf16[1024,256]{1,0:T(8,128)(2,1)S(1)} %get-tuple-element.83), channel_id=1, source_target_pairs={{0,12},{4,0},{8,4},{12,8},{1,13},{5,1},{9,5},{13,9},{2,14},{6,2},{... | collective-permute-start | bytes 1572872 | tf_op jit(solution)/shard_map/ppermute | solution.py:122
  51.4 45.8 %all-to-all-start = ((bf16[4,16,1792]{2,1,0:T(8,128)(2,1)}), bf16[4,16,1792]{2,1,0:T(8,128)(2,1)S(1)}, u32[]{:S(2)}, u32[]{:S(2)}) async-start(bf16[4,16,1792]{2,1,0:T(8,128)(2,1)} %broadcast_in_dim.16), calls=%async_computation | async-start | bytes 458752 | tf_op jit(solution)/shard_map/while/body/all_to_all | solution.py:91
  97.9 5.0 %copy-start.7 = (bf16[1024,256]{1,0:T(8,128)(2,1)}, bf16[1024,256]{1,0:T(8,128)(2,1)S(1)}, u32[]{:S(2)}) copy-start(bf16[1024,256]{1,0:T(8,128)(2,1)S(1)} %collective-permute-done.3) | copy-start | bytes 1572868
  99.5 17.9 %all-to-all-start.3 = ((bf16[4,16,1792]{2,1,0:T(8,128)(2,1)}), bf16[4,16,1792]{2,1,0:T(8,128)(2,1)S(1)}, u32[]{:S(2)}, u32[]{:S(2)}) async-start(bf16[4,16,1792]{2,1,0:T(8,128)(2,1)} %broadcast_in_dim.13), calls=%async_computation.3 | async-start | bytes 458752 | tf_op jit(solution)/shard_map/all_to_all | solution.py:91
  104.4 14.1 %copy-start.5 = (f32[1024,256]{1,0:T(8,128)}, f32[1024,256]{1,0:T(8,128)S(1)}, u32[]{:S(2)}) copy-start(f32[1024,256]{1,0:T(8,128)S(1)} %convert_add_fusion) | copy-start | bytes 3145732
  104.4 63.2 %collective-permute-start.5 = (bf16[1024,128]{1,0:T(8,128)(2,1)S(1)}, bf16[1024,128]{1,0:T(8,128)(2,1)}, u32[]{:S(2)}, u32[]{:S(2)}) collective-permute-start(bf16[1024,128]{1,0:T(8,128)(2,1)S(1)} %slice.12), channel_id=1, source_target_pairs={{0,2},{2,0},{1,3},{3,1},{4,6},{6,4},{5,7},{7,5},{8,10},{10,8},{9,1... | collective-permute-start | bytes 786440 | tf_op jit(solution)/shard_map/ppermute | solution.py:142
  117.4 15.4 %copy-start.6 = (f32[256,1792]{1,0:T(8,128)S(1)}, f32[256,1792]{1,0:T(8,128)}, u32[]{:S(2)}) copy-start(f32[256,1792]{1,0:T(8,128)} %param.10) | copy-start | bytes 5505028
  132.8 3.2 %copy-start.4 = (bf16[256,1792]{1,0:T(8,128)(2,1)S(1)}, bf16[256,1792]{1,0:T(8,128)(2,1)}, u32[]{:S(2)}) copy-start(bf16[256,1792]{1,0:T(8,128)(2,1)} %get-tuple-element.91) | copy-start | bytes 2752516
  136.0 31.6 %slice-start = ((f32[1024,256]{1,0:T(8,128)}), f32[1024,128]{1,0:T(8,128)S(1)}, s32[]{:S(2)}) async-start(f32[1024,256]{1,0:T(8,128)} %copy-done.5), calls=%async_computation.4 | async-start | bytes 1048576 | tf_op jit(solution)/shard_map/slice | solution.py:141

commit v5 on v3

--- a/solution.py
+++ b/solution.py
@@ -5,7 +5,7 @@
 from jax.experimental.pallas import tpu as pltpu
 from jax.sharding import Mesh, PartitionSpec as P
 
-SIZES = (4, 4, 4, 4, 2, 2)
+SIZES = (2, 8, 4, 4, 2, 2)
 NAMES = ("zo", "zi", "x", "y", "h", "c")
 LANES = 128
 
@@ -115,39 +115,36 @@
     terms = after(terms, *part)
     anchor = lax.dynamic_slice_in_dim(base, x * per_x, per_x, 0).astype(bf16).astype(f32)
     total = (terms.astype(f32).sum(axis=0) - n_x * anchor).astype(bf16)
-
     part = [part[0]] + [lax.ppermute(part[step], "y", shift("y", n_y, step)) for step in range(1, n_y)]
 
     once = 1 + (h >> 4)
+
+    def alone(function, value, shape):
+        carry = (value, jnp.zeros(shape, bf16))
+        return lax.fori_loop(0, once, lambda _, carry: (-carry[0], function(carry[0])), carry)[1]
 
     def over_zi(total):
         terms = exchange(total.reshape(n_zi, per_zi, width), "zi")
         return terms.astype(f32).sum(axis=0).astype(bf16)
 
-    empty = jnp.zeros((per_zi, width), bf16)
-    total = lax.fori_loop(0, once, lambda _, carry: (carry[0] + carry[0], over_zi(carry[0])), (total, empty))[1]
-
+    total = alone(over_zi, total, (per_zi, width))
     total, *part = lax.optimization_barrier((total, *part))
 
-    terms = gather_small(total, "zo", n_zo)
-
+    across = lax.ppermute(total, "zo", swap)
     kv = part[0].astype(f32)
     for piece in part[1:]:
         kv += piece.astype(f32)
     mine, other = lax.optimization_barrier((kv[:, :LANES], kv[:, LANES:].astype(bf16)))
+    across = after(across, other)
+    outer_grad = (-(total.astype(f32) + across.astype(f32)) / groups).astype(bf16)
+    outer_grad, other = lax.optimization_barrier((outer_grad, other))
+
+    gathered = gather_small(outer_grad, "zi", n_zi)
     there = lax.ppermute(other, "h", swap)
 
-    terms = after(terms, other)
-    outer_grad = (-terms.astype(f32).sum(axis=0) / groups).astype(bf16)
-
-    def over_zi_and_x(outer_grad):
-        gathered = gather_small(outer_grad, "zi", n_zi).reshape(per_x, width)
-        return lax.all_gather(gathered, "x", axis=0, tiled=True)
-
-    empty = jnp.zeros((rows, width), bf16)
-    outer_grad = lax.fori_loop(
-        0, once, lambda _, carry: (carry[0] + carry[0], over_zi_and_x(carry[0])), (outer_grad, empty)
-    )[1].astype(f32)
+    gathered = after(gathered, other).reshape(per_x, width)
+    outer_grad = alone(lambda value: lax.all_gather(value, "x", axis=0, tiled=True), gathered, (rows, width))
+    outer_grad = outer_grad.astype(f32)
 
     def step(outer_grad, base, momentum):
         new_momentum = 0.9 * momentum + outer_grad

time: 175 us -> 158 us (0.903)
  the two profiles are of different devices: /device:TPU:8 before, /device:TPU:288 now
where the time goes in v5:
time: 158 us; the launch traced here: 157 us
  waiting for transfers between devices  63.7 us (40%)
  starting transfers between devices  53 us (34%)
  blocking collectives  14.3 us (9%)
  other arithmetic  12.2 us (8%)
  Pallas kernels  8.19 us (5%)
  local copies, waits for them, and re-layouts  4.67 us (3%)
    all_to_all x3, waiting for transfers between devices, exchange(): return lax.all_to_all(array, axis, split_axis=0, concat_axis=0, tiled=True)  52.4 us
    all_to_all x3, starting transfers between devices, exchange(): return lax.all_to_all(array, axis, split_axis=0, concat_axis=0, tiled=True)  23.4 us
    all_gather x1, blocking collectives, shards(): lax.all_gather(value, 'x', axis=0, tiled=True)  14.3 us
    ppermute x1, starting transfers between devices, shards(): there = lax.ppermute(other, 'h', swap)  11.8 us
    ppermute x3, starting transfers between devices, shards(): lax.ppermute(part[step], 'y', shift('y', n_y, step))  11.5 us
    ppermute x1, waiting for transfers between devices, shards(): across = lax.ppermute(total, 'zo', swap)  11.3 us
    pallas_call x1, Pallas kernels, project(): pl.pallas_call(project_kernel, out_shape=[jax.ShapeDtypeStruct((rows, 2 *...  6.83 us
    convert_element_type x1, other arithmetic, shards(): synced = step(outer_grad, base, momentum)[0].astype(bf16)  3.18 us
  transfers between devices with their start and end apart: 10, of which 3 were waited for; matrix products, arithmetic and copies ran while one was open for 8% of the time, Pallas kernels for 4%

profile of v5, /device:TPU:288, one launch (start us, length us, event | category | flops | bytes accessed | tf_op | source)
XLA Modules:
  0.0 156.9 jit_solution(3459276515935233143)
XLA Ops:
  0.6 0.1 pad_add_fusion.place_ref
  0.7 0.0 copy-start
  0.7 1.6 %copy-done = bf16[512,2048]{1,0:T(8,128)(2,1)S(1)} copy-done((bf16[512,2048]{1,0:T(8,128)(2,1)S(1)}, bf16[512,2048]{1,0:T(8,128)(2,1)}, u32[]{:S(2)}) %copy-start) | copy-done | bytes 2097176
  2.3 0.0 copy-start.1
  2.3 1.4 shard_map.84
  3.7 1.9 %collective-permute-start.1 = (bf16[512,1024]{1,0:T(8,128)(2,1)S(1)}, bf16[512,1024]{1,0:T(8,128)(2,1)}, u32[]{:S(2)}, u32[]{:S(2)}) collective-permute-start(bf16[512,1024]{1,0:T(8,128)(2,1)S(1)} %shard_map.84), channel_id=1, source_target_pairs={{0,1},{1,0},{2,3},{3,2},{4,5},{5,4},{6,7},{7,6},{8,9},{9,8},{10,11... | collective-permute-start | bytes 3145736 | tf_op jit(solution)/shard_map/ppermute | solution.py:112
  5.6 2.4 %collective-permute-start = (bf16[1024,512]{1,0:T(8,128)(2,1)}, bf16[1024,512]{1,0:T(8,128)(2,1)}, u32[]{:S(2)}, u32[]{:S(2)}) collective-permute-start(bf16[1024,512]{1,0:T(8,128)(2,1)} %own_ref.1), channel_id=1, source_target_pairs={{0,1},{1,0},{2,3},{3,2},{4,5},{5,4},{6,7},{7,6},{8,9},{9,8},{10,11... | collective-permute-start | bytes 3145736 | tf_op jit(solution)/shard_map/ppermute | solution.py:111
  8.0 4.3 %all-to-all-start.1 = ((bf16[4,64,1792]{2,1,0:T(8,128)(2,1)}), bf16[4,64,1792]{2,1,0:T(8,128)(2,1)}, u32[]{:S(2)}, u32[]{:S(2)}) async-start(bf16[4,64,1792]{2,1,0:T(8,128)(2,1)} %bitcast.9), calls=%async_computation.1 | async-start | bytes 1835008 | tf_op jit(solution)/shard_map/all_to_all | solution.py:91
  12.3 0.0 collective-permute-done.1.packed_ref
  12.3 0.0 collective-permute-done.sibling_ref
  12.3 0.0 copy-done.1
  12.4 6.8 %shard_map.85 = (bf16[1024,256]{1,0:T(8,128)(2,1)S(1)}, bf16[1024,256]{1,0:T(8,128)(2,1)}, bf16[1024,256]{1,0:T(8,128)(2,1)}, bf16[1024,256]{1,0:T(8,128)(2,1)S(1)}) custom-call(s32[3]{0:T(128)S(1)} %pad_add_fusion.place_ref, bf16[1024,512]{1,0:T(8,128)(2,1)} %own_ref.1, bf16[1024,512]{1,0:T(8,128)(2,1)} %collective-permute-done.sibling_ref, ...), custom_call_target="tpu_custom_call" | custom-call | flops 2147483648 | bytes 6291456 | tf_op jit(solution)/shard_map/pallas_call | solution.py:60
  19.2 3.5 %collective-permute-start.2 = (bf16[1024,256]{1,0:T(8,128)(2,1)}, bf16[1024,256]{1,0:T(8,128)(2,1)S(1)}, u32[]{:S(2)}, u32[]{:S(2)}) collective-permute-start(bf16[1024,256]{1,0:T(8,128)(2,1)} %get-tuple-element.96), channel_id=1, source_target_pairs={{0,4},{4,8},{8,12},{12,0},{1,5},{5,9},{9,13},{13,1},{2,6},{6,10},{... | collective-permute-start | bytes 1572872 | tf_op jit(solution)/shard_map/ppermute | solution.py:118
  22.7 4.8 %collective-permute-start.3 = (bf16[1024,256]{1,0:T(8,128)(2,1)}, bf16[1024,256]{1,0:T(8,128)(2,1)}, u32[]{:S(2)}, u32[]{:S(2)}) collective-permute-start(bf16[1024,256]{1,0:T(8,128)(2,1)} %get-tuple-element.97), channel_id=1, source_target_pairs={{0,8},{4,12},{8,0},{12,4},{1,9},{5,13},{9,1},{13,5},{2,10},{6,14},... | collective-permute-start | bytes 1572872 | tf_op jit(solution)/shard_map/ppermute | solution.py:118
  27.5 3.3 %collective-permute-start.4 = (bf16[1024,256]{1,0:T(8,128)(2,1)S(1)}, bf16[1024,256]{1,0:T(8,128)(2,1)}, u32[]{:S(2)}, u32[]{:S(2)}) collective-permute-start(bf16[1024,256]{1,0:T(8,128)(2,1)S(1)} %get-tuple-element.98), channel_id=1, source_target_pairs={{0,12},{4,0},{8,4},{12,8},{1,13},{5,1},{9,5},{13,9},{2,14},{6,2},{... | collective-permute-start | bytes 1572872 | tf_op jit(solution)/shard_map/ppermute | solution.py:118
  30.7 0.0 all-to-all-done.1
  30.8 1.4 convert_reduce_fusion
  32.1 1.1 subtract_convert_fusion.1
  33.2 0.6 broadcast_in_dim.9
  33.8 28.2 %while.26 = (s32[]{:T(128)}, bf16[64,1792]{1,0:T(8,128)(2,1)S(1)}, bf16[8,1792]{1,0:T(8,128)(2,1)}, s32[]{:T(128)}, s32[]{:T(128)}, /*index=5*/bf16[]{:T(256)}) while((s32[]{:T(128)}, bf16[64,1792]{1,0:T(8,128)(2,1)S(1)}, bf16[8,1792]{1,0:T(8,128)(2,1)}, s32[]{:T(128)}, s32[]{:T(128)}, /*index=5*/bf16[]{:T(256)}) %tuple.58), condition=%wide.region_3.0_spmd, body=%wide.region_1.0_spmd.sunk | while | flops 215042 | bytes 1863783 | solution.py:124
  33.8 0.7 copy.13
  34.5 12.6 %all-to-all-start = ((bf16[8,8,1792]{2,1,0:T(8,128)(2,1)}), bf16[8,8,1792]{2,1,0:T(8,128)(2,1)S(1)}, u32[]{:S(2)}, u32[]{:S(2)}) async-start(bf16[8,8,1792]{2,1,0:T(8,128)(2,1)} %bitcast.7), calls=%async_computation | async-start | bytes 458752 | tf_op jit(solution)/shard_map/while/body/all_to_all | solution.py:91
  47.1 1.0 neg.16
  48.1 13.2 %all-to-all-done = bf16[8,8,1792]{2,1,0:T(8,128)(2,1)S(1)} async-done(((bf16[8,8,1792]{2,1,0:T(8,128)(2,1)}), bf16[8,8,1792]{2,1,0:T(8,128)(2,1)S(1)}, u32[]{:S(2)}, u32[]{:S(2)}) %all-to-all-start) | async-done | bytes 229408 | tf_op jit(solution)/shard_map/while/body/all_to_all | solution.py:91
  61.3 0.6 reduce_sum.24
  62.0 0.0 collective-permute-done.2
  62.0 0.0 collective-permute-done.3
  62.0 0.0 collective-permute-done.4
  62.0 0.0 copy-start.5
  62.0 1.9 %collective-permute-start.5 = (bf16[8,1792]{1,0:T(8,128)(2,1)}, bf16[8,1792]{1,0:T(8,128)(2,1)S(1)}, u32[]{:S(2)}, u32[]{:S(2)}) collective-permute-start(bf16[8,1792]{1,0:T(8,128)(2,1)} %get-tuple-element.101), channel_id=1, source_target_pairs={{0,512},{512,0},{1,513},{513,1},{2,514},{514,2},{3,515},{515,3},{4... | collective-permute-start | bytes 86024 | tf_op jit(solution)/shard_map/ppermute | solution.py:133
  63.9 1.4 convert_add_fusion
  65.4 0.0 copy-start.3
  65.4 11.3 %collective-permute-done.5 = bf16[8,1792]{1,0:T(8,128)(2,1)S(1)} collective-permute-done((bf16[8,1792]{1,0:T(8,128)(2,1)}, bf16[8,1792]{1,0:T(8,128)(2,1)S(1)}, u32[]{:S(2)}, u32[]{:S(2)}) %collective-permute-start.5) | collective-permute-done | bytes 28704 | tf_op jit(solution)/shard_map/ppermute | solution.py:133
  76.7 0.0 copy-done.5
  76.7 0.7 broadcast_in_dim.10
  77.4 6.4 %all-to-all-start.2 = ((bf16[8,8,1792]{2,1,0:T(8,128)(2,1)}), bf16[8,8,1792]{2,1,0:T(8,128)(2,1)S(1)}, u32[]{:S(2)}, u32[]{:S(2)}) async-start(bf16[8,8,1792]{2,1,0:T(8,128)(2,1)} %broadcast_in_dim.10), calls=%async_computation.2 | async-start | bytes 458752 | tf_op jit(solution)/shard_map/all_to_all | solution.py:91
  83.8 11.8 %collective-permute-start.6 = (bf16[1024,128]{1,0:T(8,128)(2,1)S(1)}, bf16[1024,128]{1,0:T(8,128)(2,1)}, u32[]{:S(2)}, u32[]{:S(2)}) collective-permute-start(bf16[1024,128]{1,0:T(8,128)(2,1)S(1)} %slice.12), channel_id=1, source_target_pairs={{0,2},{2,0},{1,3},{3,1},{4,6},{6,4},{5,7},{7,5},{8,10},{10,8},{9,1... | collective-permute-start | bytes 786440 | tf_op jit(solution)/shard_map/ppermute | solution.py:143
  95.7 39.2 %all-to-all-done.2 = bf16[8,8,1792]{2,1,0:T(8,128)(2,1)S(1)} async-done(((bf16[8,8,1792]{2,1,0:T(8,128)(2,1)}), bf16[8,8,1792]{2,1,0:T(8,128)(2,1)S(1)}, u32[]{:S(2)}, u32[]{:S(2)}) %all-to-all-start.2) | async-done | bytes 229408 | tf_op jit(solution)/shard_map/all_to_all | solution.py:91
  134.9 0.0 copy-start.4
  134.9 1.0 broadcast_in_dim.11
  136.0 0.0 copy-done.3
  136.0 14.4 %while.27 = (s32[]{:T(128)}, bf16[64,1792]{1,0:T(8,128)(2,1)S(1)}, bf16[256,1792]{1,0:T(8,128)(2,1)}, s32[]{:T(128)}, s32[]{:T(128)}) while((s32[]{:T(128)}, bf16[64,1792]{1,0:T(8,128)(2,1)S(1)}, bf16[256,1792]{1,0:T(8,128)(2,1)}, s32[]{:T(128)}, s32[]{:T(128)}) %tuple.64), condition=%wide.region_5.0_spmd, body=%wide.region_4.0_spmd.sunk | while | flops 114690 | bytes 1605693 | solution.py:124
  136.0 14.3 %all_gather.4 = bf16[256,1792]{1,0:T(8,128)(2,1)} all-gather(bf16[64,1792]{1,0:T(8,128)(2,1)S(1)} %get-tuple-element.204), channel_id=1, replica_groups=mesh['zo'=2,'zi'=8,'x'=4,'y'=4,'h'=2,'c'=2] {'x'}, dimensions={0}, use_global_device_ids=true | all-gather | bytes 1146880 | tf_op jit(solution)/shard_map/while/body/all_gather | solution.py:146
  150.3 0.1 neg.17
  150.3 0.0 copy-done.4
  150.3 0.0 copy-start.2
  150.3 3.2 %subtract_convert_fusion = bf16[256,1792]{1,0:T(8,128)(2,1)} fusion(f32[256,1792]{1,0:T(8,128)S(1)} %copy-done.4, f32[256,1792]{1,0:T(8,128)} %param.11, bf16[256,1792]{1,0:T(8,128)(2,1)} %get-tuple-element.111), kind=kLoop, calls=%fused_computation | loop fusion | flops 3670016 | bytes 5505024 | tf_op jit(solution)/shard_map/convert_element_type | solution.py:153
  153.5 0.0 copy-done.2
  153.5 0.0 slice-start
  153.5 0.1 convert_element_type.59
  153.7 1.5 multiply_subtract_fusion
  155.2 0.0 collective-permute-done.6
  155.2 0.0 slice-done
  155.2 1.7 %add_convert_fusion = bf16[1024,128]{1,0:T(8,128)(2,1)} fusion(f32[1024,128]{1,0:T(8,128)S(1)} %slice-done, bf16[1024,128]{1,0:T(8,128)(2,1)} %collective-permute-done.6), kind=kLoop, calls=%fused_computation.4 | loop fusion | flops 393216 | bytes 1048576 | tf_op jit(solution)/shard_map/convert_element_type | solution.py:159
  (2 shorter events, 0.0 us)
Async XLA Ops:
  0.7 1.6 %copy-start = (bf16[512,2048]{1,0:T(8,128)(2,1)S(1)}, bf16[512,2048]{1,0:T(8,128)(2,1)}, u32[]{:S(2)}) copy-start(bf16[512,2048]{1,0:T(8,128)(2,1)} %far_ref.3) | copy-start | bytes 6291460
  2.3 10.0 %copy-start.1 = (bf16[512,2048]{1,0:T(8,128)(2,1)S(1)}, bf16[512,2048]{1,0:T(8,128)(2,1)}, u32[]{:S(2)}) copy-start(bf16[512,2048]{1,0:T(8,128)(2,1)} %far_ref.3) | copy-start | bytes 6291460
  3.7 8.7 %collective-permute-start.1 = (bf16[512,1024]{1,0:T(8,128)(2,1)S(1)}, bf16[512,1024]{1,0:T(8,128)(2,1)}, u32[]{:S(2)}, u32[]{:S(2)}) collective-permute-start(bf16[512,1024]{1,0:T(8,128)(2,1)S(1)} %shard_map.84), channel_id=1, source_target_pairs={{0,1},{1,0},{2,3},{3,2},{4,5},{5,4},{6,7},{7,6},{8,9},{9,8},{10,11... | collective-permute-start | bytes 3145736 | tf_op jit(solution)/shard_map/ppermute | solution.py:112
  5.6 6.7 %collective-permute-start = (bf16[1024,512]{1,0:T(8,128)(2,1)}, bf16[1024,512]{1,0:T(8,128)(2,1)}, u32[]{:S(2)}, u32[]{:S(2)}) collective-permute-start(bf16[1024,512]{1,0:T(8,128)(2,1)} %own_ref.1), channel_id=1, source_target_pairs={{0,1},{1,0},{2,3},{3,2},{4,5},{5,4},{6,7},{7,6},{8,9},{9,8},{10,11... | collective-permute-start | bytes 3145736 | tf_op jit(solution)/shard_map/ppermute | solution.py:111
  8.0 22.7 %all-to-all-start.1 = ((bf16[4,64,1792]{2,1,0:T(8,128)(2,1)}), bf16[4,64,1792]{2,1,0:T(8,128)(2,1)}, u32[]{:S(2)}, u32[]{:S(2)}) async-start(bf16[4,64,1792]{2,1,0:T(8,128)(2,1)} %bitcast.9), calls=%async_computation.1 | async-start | bytes 1835008 | tf_op jit(solution)/shard_map/all_to_all | solution.py:91
  19.2 42.8 %collective-permute-start.2 = (bf16[1024,256]{1,0:T(8,128)(2,1)}, bf16[1024,256]{1,0:T(8,128)(2,1)S(1)}, u32[]{:S(2)}, u32[]{:S(2)}) collective-permute-start(bf16[1024,256]{1,0:T(8,128)(2,1)} %get-tuple-element.96), channel_id=1, source_target_pairs={{0,4},{4,8},{8,12},{12,0},{1,5},{5,9},{9,13},{13,1},{2,6},{6,10},{... | collective-permute-start | bytes 1572872 | tf_op jit(solution)/shard_map/ppermute | solution.py:118
  22.7 39.3 %collective-permute-start.3 = (bf16[1024,256]{1,0:T(8,128)(2,1)}, bf16[1024,256]{1,0:T(8,128)(2,1)}, u32[]{:S(2)}, u32[]{:S(2)}) collective-permute-start(bf16[1024,256]{1,0:T(8,128)(2,1)} %get-tuple-element.97), channel_id=1, source_target_pairs={{0,8},{4,12},{8,0},{12,4},{1,9},{5,13},{9,1},{13,5},{2,10},{6,14},... | collective-permute-start | bytes 1572872 | tf_op jit(solution)/shard_map/ppermute | solution.py:118
  27.5 34.5 %collective-permute-start.4 = (bf16[1024,256]{1,0:T(8,128)(2,1)S(1)}, bf16[1024,256]{1,0:T(8,128)(2,1)}, u32[]{:S(2)}, u32[]{:S(2)}) collective-permute-start(bf16[1024,256]{1,0:T(8,128)(2,1)S(1)} %get-tuple-element.98), channel_id=1, source_target_pairs={{0,12},{4,0},{8,4},{12,8},{1,13},{5,1},{9,5},{13,9},{2,14},{6,2},{... | collective-permute-start | bytes 1572872 | tf_op jit(solution)/shard_map/ppermute | solution.py:118
  34.5 26.8 %all-to-all-start = ((bf16[8,8,1792]{2,1,0:T(8,128)(2,1)}), bf16[8,8,1792]{2,1,0:T(8,128)(2,1)S(1)}, u32[]{:S(2)}, u32[]{:S(2)}) async-start(bf16[8,8,1792]{2,1,0:T(8,128)(2,1)} %bitcast.7), calls=%async_computation | async-start | bytes 458752 | tf_op jit(solution)/shard_map/while/body/all_to_all | solution.py:91
  62.0 14.7 %copy-start.5 = (bf16[8,1792]{1,0:T(8,128)(2,1)S(1)}, bf16[8,1792]{1,0:T(8,128)(2,1)}, u32[]{:S(2)}) copy-start(bf16[8,1792]{1,0:T(8,128)(2,1)} %get-tuple-element.101) | copy-start | bytes 86020
  62.0 14.7 %collective-permute-start.5 = (bf16[8,1792]{1,0:T(8,128)(2,1)}, bf16[8,1792]{1,0:T(8,128)(2,1)S(1)}, u32[]{:S(2)}, u32[]{:S(2)}) collective-permute-start(bf16[8,1792]{1,0:T(8,128)(2,1)} %get-tuple-element.101), channel_id=1, source_target_pairs={{0,512},{512,0},{1,513},{513,1},{2,514},{514,2},{3,515},{515,3},{4... | collective-permute-start | bytes 86024 | tf_op jit(solution)/shard_map/ppermute | solution.py:133
  65.4 70.6 %copy-start.3 = (f32[1024,256]{1,0:T(8,128)}, f32[1024,256]{1,0:T(8,128)S(1)}, u32[]{:S(2)}) copy-start(f32[1024,256]{1,0:T(8,128)S(1)} %convert_add_fusion) | copy-start | bytes 3145732
  77.4 57.5 %all-to-all-start.2 = ((bf16[8,8,1792]{2,1,0:T(8,128)(2,1)}), bf16[8,8,1792]{2,1,0:T(8,128)(2,1)S(1)}, u32[]{:S(2)}, u32[]{:S(2)}) async-start(bf16[8,8,1792]{2,1,0:T(8,128)(2,1)} %broadcast_in_dim.10), calls=%async_computation.2 | async-start | bytes 458752 | tf_op jit(solution)/shard_map/all_to_all | solution.py:91
  83.8 71.3 %collective-permute-start.6 = (bf16[1024,128]{1,0:T(8,128)(2,1)S(1)}, bf16[1024,128]{1,0:T(8,128)(2,1)}, u32[]{:S(2)}, u32[]{:S(2)}) collective-permute-start(bf16[1024,128]{1,0:T(8,128)(2,1)S(1)} %slice.12), channel_id=1, source_target_pairs={{0,2},{2,0},{1,3},{3,1},{4,6},{6,4},{5,7},{7,5},{8,10},{10,8},{9,1... | collective-permute-start | bytes 786440 | tf_op jit(solution)/shard_map/ppermute | solution.py:143
  134.9 15.4 %copy-start.4 = (f32[256,1792]{1,0:T(8,128)S(1)}, f32[256,1792]{1,0:T(8,128)}, u32[]{:S(2)}) copy-start(f32[256,1792]{1,0:T(8,128)} %param.10) | copy-start | bytes 5505028
  150.3 3.2 %copy-start.2 = (bf16[256,1792]{1,0:T(8,128)(2,1)S(1)}, bf16[256,1792]{1,0:T(8,128)(2,1)}, u32[]{:S(2)}) copy-start(bf16[256,1792]{1,0:T(8,128)(2,1)} %get-tuple-element.111) | copy-start | bytes 2752516
  153.5 1.6 %slice-start = ((f32[1024,256]{1,0:T(8,128)}), f32[1024,128]{1,0:T(8,128)S(1)}, s32[]{:S(2)}) async-start(f32[1024,256]{1,0:T(8,128)} %copy-done.3), calls=%async_computation.3 | async-start | bytes 1048576 | tf_op jit(solution)/shard_map/slice | solution.py:137

commit v6 on v4

--- a/solution.py
+++ b/solution.py
@@ -5,7 +5,7 @@
 from jax.experimental.pallas import tpu as pltpu
 from jax.sharding import Mesh, PartitionSpec as P
 
-SIZES = (4, 4, 4, 4, 2, 2)
+SIZES = (2, 8, 4, 4, 2, 2)
 NAMES = ("zo", "zi", "x", "y", "h", "c")
 LANES = 128
 
@@ -106,6 +106,7 @@
     per_x, per_zi = rows // n_x, rows // (n_x * n_zi)
 
     terms = exchange(local_weights[0].reshape(n_x, per_x, width), "x")
+
     anchor = lax.dynamic_slice_in_dim(base, x * per_x, per_x, 0).astype(bf16).astype(f32)
     total = (terms.astype(f32).sum(axis=0) - n_x * anchor).astype(bf16)
 
@@ -127,33 +128,32 @@
         carry = (value, jnp.zeros(shape, bf16))
         return lax.fori_loop(0, once, lambda _, carry: (-carry[0], function(carry[0])), carry)[1]
 
-    def over_zo(total):
-        terms = gather_small(total, "zo", n_zo)
-        return (-terms.astype(f32).sum(axis=0) / groups).astype(bf16)
+    def outer(total):
+        across = lax.ppermute(total, "zo", swap)
+        return (-(total.astype(f32) + across.astype(f32)) / groups).astype(bf16)
 
-    outer_grad = alone(over_zo, total, (per_zi, width))
-    outer_grad, *part = lax.optimization_barrier((outer_grad, *part))
+    outer_grad = alone(outer, total, (per_zi, width))
+    outer_grad, base, momentum, *part = lax.optimization_barrier((outer_grad, base, momentum, *part))
     gathered = gather_small(outer_grad, "zi", n_zi)
 
     kv = part[0].astype(f32)
     for piece in part[1:]:
         kv += piece.astype(f32)
-    mine, other = lax.optimization_barrier((kv[:, :LANES], kv[:, LANES:].astype(bf16)))
+    without = base - 0.567 * momentum
+    mine, other, without = lax.optimization_barrier((kv[:, :LANES], kv[:, LANES:].astype(bf16), without))
     there = lax.ppermute(other, "h", swap)
 
     gathered = after(gathered, other).reshape(per_x, width)
     outer_grad = alone(lambda value: lax.all_gather(value, "x", axis=0, tiled=True), gathered, (rows, width))
-    outer_grad = outer_grad.astype(f32)
 
-    def step(outer_grad, base, momentum):
-        new_momentum = 0.9 * momentum + outer_grad
-        return base - 0.7 * (outer_grad + 0.9 * new_momentum), new_momentum
+    synced = (without - 1.33 * outer_grad.astype(f32)).astype(bf16)
+    start = ((zo * n_zi + zi) * n_x + x) * own
 
-    synced = step(outer_grad, base, momentum)[0].astype(bf16)
-    start = ((zo * n_zi + zi) * n_x + x) * own
-    new_base, new_momentum = step(
-        *(lax.dynamic_slice_in_dim(a, start, own, 0) for a in (outer_grad, base, momentum))
-    )
+    def own_rows(array):
+        return lax.dynamic_slice_in_dim(array, start, own, 0).astype(f32)
+
+    new_base = own_rows(without) - 1.33 * own_rows(outer_grad)
+    new_momentum = 0.9 * own_rows(momentum) + own_rows(outer_grad)
     there = after(there, synced, new_base)
     keys_values = (mine + there.astype(f32)).astype(bf16)
     return new_base, new_momentum, synced, keys_values

time: 170 us -> 160 us (0.941)
  the two profiles are of different devices: /device:TPU:8 before, /device:TPU:296 now
where the time goes in v6:
time: 160 us; the launch traced here: 159 us
  waiting for transfers between devices  63.7 us (40%)
  starting transfers between devices  55.1 us (34%)
  blocking collectives  14.3 us (9%)
  other arithmetic  10.3 us (6%)
  local copies, waits for them, and re-layouts  7.3 us (5%)
  Pallas kernels  7.23 us (5%)
    all_to_all x3, waiting for transfers between devices, exchange(): return lax.all_to_all(array, axis, split_axis=0, concat_axis=0, tiled=True)  50.6 us
    all_to_all x3, starting transfers between devices, exchange(): return lax.all_to_all(array, axis, split_axis=0, concat_axis=0, tiled=True)  26.2 us
    all_gather x1, blocking collectives, shards(): lax.all_gather(value, 'x', axis=0, tiled=True)  14.3 us
    ppermute x1, waiting for transfers between devices, outer(): across = lax.ppermute(total, 'zo', swap)  12.5 us
    ppermute x1, starting transfers between devices, shards(): there = lax.ppermute(other, 'h', swap)  11.9 us
    ppermute x3, starting transfers between devices, shards(): lax.ppermute(part[step], 'y', shift('y', n_y, step))  10.7 us
    pallas_call x1, Pallas kernels, project(): pl.pallas_call(project_kernel, out_shape=[jax.ShapeDtypeStruct((rows, 2 *...  5.86 us
    unnamed x18, local copies, waits for them, and re-layouts  4.2 us
  transfers between devices with their start and end apart: 10, of which 5 were waited for; matrix products, arithmetic and copies ran while one was open for 7% of the time, Pallas kernels for 5%

profile of v6, /device:TPU:296, one launch (start us, length us, event | category | flops | bytes accessed | tf_op | source)
XLA Modules:
  0.0 158.7 jit_solution(697588766936872813)
XLA Ops:
  0.6 4.3 %all-to-all-start = ((bf16[4,64,1792]{2,1,0:T(8,128)(2,1)}), bf16[4,64,1792]{2,1,0:T(8,128)(2,1)}, u32[]{:S(2)}, u32[]{:S(2)}) async-start(bf16[4,64,1792]{2,1,0:T(8,128)(2,1)} %bitcast.7), calls=%async_computation | async-start | bytes 1835008 | tf_op jit(solution)/shard_map/all_to_all | solution.py:91
  4.9 1.9 %collective-permute-start.1 = (bf16[1024,512]{1,0:T(8,128)(2,1)}, bf16[1024,512]{1,0:T(8,128)(2,1)}, u32[]{:S(2)}, u32[]{:S(2)}) collective-permute-start(bf16[1024,512]{1,0:T(8,128)(2,1)} %own_ref.1), channel_id=1, source_target_pairs={{0,1},{1,0},{2,3},{3,2},{4,5},{5,4},{6,7},{7,6},{8,9},{9,8},{10,11... | collective-permute-start | bytes 3145736 | tf_op jit(solution)/shard_map/ppermute | solution.py:114
  6.9 0.1 pad_add_fusion.place_ref
  6.9 0.0 copy-start
  6.9 1.6 %copy-done = bf16[512,2048]{1,0:T(8,128)(2,1)S(1)} copy-done((bf16[512,2048]{1,0:T(8,128)(2,1)S(1)}, bf16[512,2048]{1,0:T(8,128)(2,1)}, u32[]{:S(2)}) %copy-start) | copy-done | bytes 2097176
  8.5 1.4 shard_map.84
  9.9 0.0 copy-start.1
  9.9 2.5 %collective-permute-start.2 = (bf16[512,1024]{1,0:T(8,128)(2,1)S(1)}, bf16[512,1024]{1,0:T(8,128)(2,1)}, u32[]{:S(2)}, u32[]{:S(2)}) collective-permute-start(bf16[512,1024]{1,0:T(8,128)(2,1)S(1)} %shard_map.84), channel_id=1, source_target_pairs={{0,1},{1,0},{2,3},{3,2},{4,5},{5,4},{6,7},{7,6},{8,9},{9,8},{10,11... | collective-permute-start | bytes 3145736 | tf_op jit(solution)/shard_map/ppermute | solution.py:115
  12.5 6.4 %all-to-all-done = bf16[4,64,1792]{2,1,0:T(8,128)(2,1)} async-done(((bf16[4,64,1792]{2,1,0:T(8,128)(2,1)}), bf16[4,64,1792]{2,1,0:T(8,128)(2,1)}, u32[]{:S(2)}, u32[]{:S(2)}) %all-to-all-start) | async-done | bytes 917536 | tf_op jit(solution)/shard_map/all_to_all | solution.py:91
  18.9 1.4 convert_reduce_fusion
  20.2 1.8 %subtract_convert_fusion.1 = bf16[64,1792]{1,0:T(8,128)(2,1)} fusion(f32[64,1792]{1,0:T(8,128)S(1)} %convert_reduce_fusion, f32[256,1792]{1,0:T(8,128)} %param.10, s32[]{:T(128)S(6)} %select_n.4), kind=kLoop, calls=%fused_computation.7 | loop fusion | flops 458752 | bytes 917508 | tf_op jit(solution)/shard_map/convert_element_type | solution.py:111
  22.0 0.0 collective-permute-done.1.sibling_ref
  22.0 0.0 collective-permute-done.2.packed_ref
  22.0 12.6 %all-to-all-start.1 = ((bf16[8,8,1792]{2,1,0:T(8,128)(2,1)}), bf16[8,8,1792]{2,1,0:T(8,128)(2,1)S(1)}, u32[]{:S(2)}, u32[]{:S(2)}) async-start(bf16[8,8,1792]{2,1,0:T(8,128)(2,1)} %bitcast.4), calls=%async_computation.1 | async-start | bytes 458752 | tf_op jit(solution)/shard_map/all_to_all | solution.py:91
  34.6 0.0 copy-done.1
  34.6 5.9 %shard_map.85 = (bf16[1024,256]{1,0:T(8,128)(2,1)S(1)}, bf16[1024,256]{1,0:T(8,128)(2,1)S(1)}, bf16[1024,256]{1,0:T(8,128)(2,1)S(1)}, bf16[1024,256]{1,0:T(8,128)(2,1)S(1)}) custom-call(s32[3]{0:T(128)S(1)} %pad_add_fusion.place_ref, bf16[1024,512]{1,0:T(8,128)(2,1)} %own_ref.1, bf16[1024,512]{1,0:T(8,128)(2,1)} %collective-permute-done.1.sibling_ref, ...), custom_call_target="tpu_custom_call" | custom-call | flops 2147483648 | bytes 6291456 | tf_op jit(solution)/shard_map/pallas_call | solution.py:60
  40.5 0.0 copy-start.2
  40.5 0.8 copy-done.2
  41.3 0.0 copy-start.3
  41.3 0.8 copy-done.3
  42.1 6.4 %all-to-all-done.1 = bf16[8,8,1792]{2,1,0:T(8,128)(2,1)S(1)} async-done(((bf16[8,8,1792]{2,1,0:T(8,128)(2,1)}), bf16[8,8,1792]{2,1,0:T(8,128)(2,1)S(1)}, u32[]{:S(2)}, u32[]{:S(2)}) %all-to-all-start.1) | async-done | bytes 229408 | tf_op jit(solution)/shard_map/all_to_all | solution.py:91
  48.6 3.5 %collective-permute-start.3 = (bf16[1024,256]{1,0:T(8,128)(2,1)}, bf16[1024,256]{1,0:T(8,128)(2,1)S(1)}, u32[]{:S(2)}, u32[]{:S(2)}) collective-permute-start(bf16[1024,256]{1,0:T(8,128)(2,1)} %copy-done.3), channel_id=1, source_target_pairs={{0,4},{4,8},{8,12},{12,0},{1,5},{5,9},{9,13},{13,1},{2,6},{6,10},{... | collective-permute-start | bytes 1572872 | tf_op jit(solution)/shard_map/ppermute | solution.py:123
  52.1 2.8 %collective-permute-start.4 = (bf16[1024,256]{1,0:T(8,128)(2,1)}, bf16[1024,256]{1,0:T(8,128)(2,1)S(1)}, u32[]{:S(2)}, u32[]{:S(2)}) collective-permute-start(bf16[1024,256]{1,0:T(8,128)(2,1)} %copy-done.2), channel_id=1, source_target_pairs={{0,8},{4,12},{8,0},{12,4},{1,9},{5,13},{9,1},{13,5},{2,10},{6,14},... | collective-permute-start | bytes 1572872 | tf_op jit(solution)/shard_map/ppermute | solution.py:123
  54.9 4.3 %collective-permute-start.5 = (bf16[1024,256]{1,0:T(8,128)(2,1)S(1)}, bf16[1024,256]{1,0:T(8,128)(2,1)S(1)}, u32[]{:S(2)}, u32[]{:S(2)}) collective-permute-start(bf16[1024,256]{1,0:T(8,128)(2,1)S(1)} %get-tuple-element.86), channel_id=1, source_target_pairs={{0,12},{4,0},{8,4},{12,8},{1,13},{5,1},{9,5},{13,9},{2,14},{6,2},{... | collective-permute-start | bytes 1572872 | tf_op jit(solution)/shard_map/ppermute | solution.py:123
  59.3 0.6 broadcast_in_dim.9
  59.9 15.1 %while.24 = (s32[]{:T(128)}, bf16[8,1792]{1,0:T(8,128)(2,1)S(1)}, bf16[8,1792]{1,0:T(8,128)(2,1)}, s32[]{:T(128)}, s32[]{:T(128)}) while((s32[]{:T(128)}, bf16[8,1792]{1,0:T(8,128)(2,1)S(1)}, bf16[8,1792]{1,0:T(8,128)(2,1)}, s32[]{:T(128)}, s32[]{:T(128)}) %tuple.50), condition=%wide.region_3.0_spmd, body=%wide.region_2.0_spmd.sunk | while | flops 100354 | bytes 315493 | solution.py:129
  59.9 1.9 %collective-permute-start = (bf16[8,1792]{1,0:T(8,128)(2,1)S(1)}, bf16[8,1792]{1,0:T(8,128)(2,1)S(1)}, u32[]{:S(2)}, u32[]{:S(2)}) collective-permute-start(bf16[8,1792]{1,0:T(8,128)(2,1)S(1)} %copy.13), channel_id=1, source_target_pairs={{0,512},{512,0},{1,513},{513,1},{2,514},{514,2},{3,515},{515,3},{4... | collective-permute-start | bytes 86024 | tf_op jit(solution)/shard_map/while/body/ppermute | solution.py:132
  61.8 12.5 %collective-permute-done = bf16[8,1792]{1,0:T(8,128)(2,1)S(1)} collective-permute-done((bf16[8,1792]{1,0:T(8,128)(2,1)S(1)}, bf16[8,1792]{1,0:T(8,128)(2,1)S(1)}, u32[]{:S(2)}, u32[]{:S(2)}) %collective-permute-start) | collective-permute-done | bytes 28704 | tf_op jit(solution)/shard_map/while/body/ppermute | solution.py:132
  74.4 0.6 multiply_convert_fusion.2
  75.0 0.0 collective-permute-done.3
  75.0 0.0 collective-permute-done.4
  75.0 0.0 copy-start.7
  75.0 0.5 collective-permute-done.5
  75.5 0.0 copy-start.8
  75.5 1.4 broadcast_in_dim.10
  77.0 0.0 copy-done.7
  77.0 9.3 %all-to-all-start.2 = ((bf16[8,8,1792]{2,1,0:T(8,128)(2,1)}), bf16[8,8,1792]{2,1,0:T(8,128)(2,1)S(1)}, u32[]{:S(2)}, u32[]{:S(2)}) async-start(bf16[8,8,1792]{2,1,0:T(8,128)(2,1)} %broadcast_in_dim.10), calls=%async_computation.2 | async-start | bytes 458752 | tf_op jit(solution)/shard_map/all_to_all | solution.py:91
  86.2 0.0 copy-done.8
  86.2 0.0 copy-start.5
  86.3 0.0 copy-start.6
  86.3 1.6 %convert_add_fusion = f32[1024,256]{1,0:T(8,128)S(1)} fusion(bf16[1024,256]{1,0:T(8,128)(2,1)} %copy-done.8, bf16[1024,256]{1,0:T(8,128)(2,1)} %copy-done.7, bf16[1024,256]{1,0:T(8,128)(2,1)S(1)} %collective-permute-done.3, bf16[1024,256]{1,0:T(8,128)(2,1)S(1)} %get-tuple-element.87), kind=kLoop, calls=%fused_computation.4 | loop fusion | flops 1835008 | bytes 3145728 | tf_op jit(solution)/shard_map/add | solution.py:141
  87.9 0.0 copy-start.4
  87.9 1.0 copy-done.4
  88.9 0.0 copy-done.5
  88.9 0.0 copy-done.6
  88.9 0.2 multiply_subtract_fusion
  89.1 11.9 %collective-permute-start.6 = (bf16[1024,128]{1,0:T(8,128)(2,1)S(1)}, bf16[1024,128]{1,0:T(8,128)(2,1)S(1)}, u32[]{:S(2)}, u32[]{:S(2)}) collective-permute-start(bf16[1024,128]{1,0:T(8,128)(2,1)S(1)} %slice.12), channel_id=1, source_target_pairs={{0,2},{2,0},{1,3},{3,1},{4,6},{6,4},{5,7},{7,5},{8,10},{10,8},{9,1... | collective-permute-start | bytes 786440 | tf_op jit(solution)/shard_map/ppermute | solution.py:144
  101.0 37.7 %all-to-all-done.2 = bf16[8,8,1792]{2,1,0:T(8,128)(2,1)S(1)} async-done(((bf16[8,8,1792]{2,1,0:T(8,128)(2,1)}), bf16[8,8,1792]{2,1,0:T(8,128)(2,1)S(1)}, u32[]{:S(2)}, u32[]{:S(2)}) %all-to-all-start.2) | async-done | bytes 229408 | tf_op jit(solution)/shard_map/all_to_all | solution.py:91
  138.7 1.0 broadcast_in_dim.11
  139.7 14.4 %while.25 = (s32[]{:T(128)}, bf16[64,1792]{1,0:T(8,128)(2,1)S(1)}, bf16[256,1792]{1,0:T(8,128)(2,1)}, s32[]{:T(128)}, s32[]{:T(128)}) while((s32[]{:T(128)}, bf16[64,1792]{1,0:T(8,128)(2,1)S(1)}, bf16[256,1792]{1,0:T(8,128)(2,1)}, s32[]{:T(128)}, s32[]{:T(128)}) %tuple.56), condition=%wide.region_5.0_spmd, body=%wide.region_4.0_spmd.sunk | while | flops 114690 | bytes 1605693 | solution.py:129
  139.7 14.3 %all_gather.4 = bf16[256,1792]{1,0:T(8,128)(2,1)} all-gather(bf16[64,1792]{1,0:T(8,128)(2,1)S(1)} %get-tuple-element.187), channel_id=1, replica_groups=mesh['zo'=2,'zi'=8,'x'=4,'y'=4,'h'=2,'c'=2] {'x'}, dimensions={0}, use_global_device_ids=true | all-gather | bytes 1146880 | tf_op jit(solution)/shard_map/while/body/all_gather | solution.py:147
  154.0 0.1 neg.15
  154.1 0.0 slice-start
  154.1 2.4 %subtract_convert_fusion = bf16[256,1792]{1,0:T(8,128)(2,1)} fusion(f32[256,1792]{1,0:T(8,128)S(1)} %multiply_subtract_fusion, bf16[256,1792]{1,0:T(8,128)(2,1)} %get-tuple-element.97), kind=kLoop, calls=%fused_computation.1 | loop fusion | flops 1835008 | bytes 3670016 | tf_op jit(solution)/shard_map/convert_element_type | solution.py:149
  156.5 1.5 convert_add_fusion.1
  158.0 0.0 collective-permute-done.6
  158.0 0.0 slice-done
  158.0 0.8 add_convert_fusion
  (4 shorter events, 0.1 us)
Async XLA Ops:
  0.6 18.3 %all-to-all-start = ((bf16[4,64,1792]{2,1,0:T(8,128)(2,1)}), bf16[4,64,1792]{2,1,0:T(8,128)(2,1)}, u32[]{:S(2)}, u32[]{:S(2)}) async-start(bf16[4,64,1792]{2,1,0:T(8,128)(2,1)} %bitcast.7), calls=%async_computation | async-start | bytes 1835008 | tf_op jit(solution)/shard_map/all_to_all | solution.py:91
  4.9 17.1 %collective-permute-start.1 = (bf16[1024,512]{1,0:T(8,128)(2,1)}, bf16[1024,512]{1,0:T(8,128)(2,1)}, u32[]{:S(2)}, u32[]{:S(2)}) collective-permute-start(bf16[1024,512]{1,0:T(8,128)(2,1)} %own_ref.1), channel_id=1, source_target_pairs={{0,1},{1,0},{2,3},{3,2},{4,5},{5,4},{6,7},{7,6},{8,9},{9,8},{10,11... | collective-permute-start | bytes 3145736 | tf_op jit(solution)/shard_map/ppermute | solution.py:114
  6.9 1.6 %copy-start = (bf16[512,2048]{1,0:T(8,128)(2,1)S(1)}, bf16[512,2048]{1,0:T(8,128)(2,1)}, u32[]{:S(2)}) copy-start(bf16[512,2048]{1,0:T(8,128)(2,1)} %far_ref.3) | copy-start | bytes 6291460
  9.9 24.7 %copy-start.1 = (bf16[512,2048]{1,0:T(8,128)(2,1)S(1)}, bf16[512,2048]{1,0:T(8,128)(2,1)}, u32[]{:S(2)}) copy-start(bf16[512,2048]{1,0:T(8,128)(2,1)} %far_ref.3) | copy-start | bytes 6291460
  9.9 12.1 %collective-permute-start.2 = (bf16[512,1024]{1,0:T(8,128)(2,1)S(1)}, bf16[512,1024]{1,0:T(8,128)(2,1)}, u32[]{:S(2)}, u32[]{:S(2)}) collective-permute-start(bf16[512,1024]{1,0:T(8,128)(2,1)S(1)} %shard_map.84), channel_id=1, source_target_pairs={{0,1},{1,0},{2,3},{3,2},{4,5},{5,4},{6,7},{7,6},{8,9},{9,8},{10,11... | collective-permute-start | bytes 3145736 | tf_op jit(solution)/shard_map/ppermute | solution.py:115
  22.0 26.5 %all-to-all-start.1 = ((bf16[8,8,1792]{2,1,0:T(8,128)(2,1)}), bf16[8,8,1792]{2,1,0:T(8,128)(2,1)S(1)}, u32[]{:S(2)}, u32[]{:S(2)}) async-start(bf16[8,8,1792]{2,1,0:T(8,128)(2,1)} %bitcast.4), calls=%async_computation.1 | async-start | bytes 458752 | tf_op jit(solution)/shard_map/all_to_all | solution.py:91
  40.5 0.8 copy-start.2
  41.3 0.8 copy-start.3
  48.6 26.4 %collective-permute-start.3 = (bf16[1024,256]{1,0:T(8,128)(2,1)}, bf16[1024,256]{1,0:T(8,128)(2,1)S(1)}, u32[]{:S(2)}, u32[]{:S(2)}) collective-permute-start(bf16[1024,256]{1,0:T(8,128)(2,1)} %copy-done.3), channel_id=1, source_target_pairs={{0,4},{4,8},{8,12},{12,0},{1,5},{5,9},{9,13},{13,1},{2,6},{6,10},{... | collective-permute-start | bytes 1572872 | tf_op jit(solution)/shard_map/ppermute | solution.py:123
  52.1 22.9 %collective-permute-start.4 = (bf16[1024,256]{1,0:T(8,128)(2,1)}, bf16[1024,256]{1,0:T(8,128)(2,1)S(1)}, u32[]{:S(2)}, u32[]{:S(2)}) collective-permute-start(bf16[1024,256]{1,0:T(8,128)(2,1)} %copy-done.2), channel_id=1, source_target_pairs={{0,8},{4,12},{8,0},{12,4},{1,9},{5,13},{9,1},{13,5},{2,10},{6,14},... | collective-permute-start | bytes 1572872 | tf_op jit(solution)/shard_map/ppermute | solution.py:123
  54.9 20.6 %collective-permute-start.5 = (bf16[1024,256]{1,0:T(8,128)(2,1)S(1)}, bf16[1024,256]{1,0:T(8,128)(2,1)S(1)}, u32[]{:S(2)}, u32[]{:S(2)}) collective-permute-start(bf16[1024,256]{1,0:T(8,128)(2,1)S(1)} %get-tuple-element.86), channel_id=1, source_target_pairs={{0,12},{4,0},{8,4},{12,8},{1,13},{5,1},{9,5},{13,9},{2,14},{6,2},{... | collective-permute-start | bytes 1572872 | tf_op jit(solution)/shard_map/ppermute | solution.py:123
  59.9 14.5 %collective-permute-start = (bf16[8,1792]{1,0:T(8,128)(2,1)S(1)}, bf16[8,1792]{1,0:T(8,128)(2,1)S(1)}, u32[]{:S(2)}, u32[]{:S(2)}) collective-permute-start(bf16[8,1792]{1,0:T(8,128)(2,1)S(1)} %copy.13), channel_id=1, source_target_pairs={{0,512},{512,0},{1,513},{513,1},{2,514},{514,2},{3,515},{515,3},{4... | collective-permute-start | bytes 86024 | tf_op jit(solution)/shard_map/while/body/ppermute | solution.py:132
  75.0 2.0 %copy-start.7 = (bf16[1024,256]{1,0:T(8,128)(2,1)}, bf16[1024,256]{1,0:T(8,128)(2,1)S(1)}, u32[]{:S(2)}) copy-start(bf16[1024,256]{1,0:T(8,128)(2,1)S(1)} %collective-permute-done.4) | copy-start | bytes 1572868
  75.5 10.7 %copy-start.8 = (bf16[1024,256]{1,0:T(8,128)(2,1)}, bf16[1024,256]{1,0:T(8,128)(2,1)S(1)}, u32[]{:S(2)}) copy-start(bf16[1024,256]{1,0:T(8,128)(2,1)S(1)} %collective-permute-done.5) | copy-start | bytes 1572868
  77.0 61.8 %all-to-all-start.2 = ((bf16[8,8,1792]{2,1,0:T(8,128)(2,1)}), bf16[8,8,1792]{2,1,0:T(8,128)(2,1)S(1)}, u32[]{:S(2)}, u32[]{:S(2)}) async-start(bf16[8,8,1792]{2,1,0:T(8,128)(2,1)} %broadcast_in_dim.10), calls=%async_computation.2 | async-start | bytes 458752 | tf_op jit(solution)/shard_map/all_to_all | solution.py:91
  86.2 2.6 %copy-start.5 = (f32[256,1792]{1,0:T(8,128)S(1)}, f32[256,1792]{1,0:T(8,128)}, u32[]{:S(2)}) copy-start(f32[256,1792]{1,0:T(8,128)} %param.10) | copy-start | bytes 5505028
  86.3 2.7 %copy-start.6 = (f32[256,1792]{1,0:T(8,128)S(1)}, f32[256,1792]{1,0:T(8,128)}, u32[]{:S(2)}) copy-start(f32[256,1792]{1,0:T(8,128)} %param.11) | copy-start | bytes 5505028
  87.9 1.0 copy-start.4
  89.1 68.8 %collective-permute-start.6 = (bf16[1024,128]{1,0:T(8,128)(2,1)S(1)}, bf16[1024,128]{1,0:T(8,128)(2,1)S(1)}, u32[]{:S(2)}, u32[]{:S(2)}) collective-permute-start(bf16[1024,128]{1,0:T(8,128)(2,1)S(1)} %slice.12), channel_id=1, source_target_pairs={{0,2},{2,0},{1,3},{3,1},{4,6},{6,4},{5,7},{7,5},{8,10},{10,8},{9,1... | collective-permute-start | bytes 786440 | tf_op jit(solution)/shard_map/ppermute | solution.py:144
  154.1 3.9 %slice-start = ((f32[1024,256]{1,0:T(8,128)}), f32[1024,128]{1,0:T(8,128)S(1)}, s32[]{:S(2)}) async-start(f32[1024,256]{1,0:T(8,128)} %copy-done.4), calls=%async_computation.3 | async-start | bytes 1048576 | tf_op jit(solution)/shard_map/slice | solution.py:143

commit v7 on v6

v7 whole, which is shorter than its diff:
```python
import jax
import jax.numpy as jnp
from jax import lax
from jax.experimental import pallas as pl
from jax.experimental.pallas import tpu as pltpu
from jax.sharding import Mesh, PartitionSpec as P

SIZES = (2, 8, 4, 4, 2, 2)
NAMES = ("zo", "zi", "x", "y", "h", "c")
LANES = 128

bf16 = jnp.bfloat16
f32 = jnp.float32
VMEM = 20 << 20


def column(y, h, c):
    return y * 4 + h * 2 + c


def pack_kernel(place_ref, near_ref, far_ref, packed_ref):
    packed_ref[:, :LANES] = near_ref[...]
    packed_ref[:, LANES:] = far_ref[...]


def pack(place, weight, n_y):
    depth, width = weight.shape
    return pl.pallas_call(
        pack_kernel,
        out_shape=jax.ShapeDtypeStruct((depth, width // 2), bf16),
        grid_spec=pltpu.PrefetchScalarGridSpec(
            num_scalar_prefetch=1,
            grid=(n_y,),
            in_specs=[
                pl.BlockSpec((depth, LANES), lambda y, p: (0, column(y, p[0], 1 - p[1]))),
                pl.BlockSpec((depth, LANES), lambda y, p: (0, column(y, 1 - p[0], 1 - p[1]))),
            ],
            out_specs=pl.BlockSpec((depth, 2 * LANES), lambda y, _: (0, y)),
        ),
        cost_estimate=pl.CostEstimate(flops=0, bytes_accessed=weight.size * 2, transcendentals=0),
        compiler_params=pltpu.CompilerParams(vmem_limit_bytes=VMEM),
    )(place, weight, weight)


def project_kernel(place_ref, own_ref, sibling_ref, near_ref, far_ref, packed_ref, out_ref):
    mine = jnp.concatenate([near_ref[...], far_ref[...]], axis=1)
    total = jnp.dot(own_ref[...], mine, preferred_element_type=f32)
    total += jnp.dot(sibling_ref[...], packed_ref[...], preferred_element_type=f32)
    out_ref[0] = total.astype(bf16)


def project(place, own, sibling, weight, packed, n_y):
    rows, depth = own.shape
    width = weight.shape[1]
    return pl.pallas_call(
        project_kernel,
        out_shape=jax.ShapeDtypeStruct((n_y, rows, 2 * LANES), bf16),
        grid_spec=pltpu.PrefetchScalarGridSpec(
            num_scalar_prefetch=1,
            grid=(n_y,),
            in_specs=[
                pl.BlockSpec((rows, depth), lambda y, _: (0, 0)),
                pl.BlockSpec((rows, depth), lambda y, _: (0, 0)),
                pl.BlockSpec((depth, LANES), lambda y, p: (0, column(y, p[0], p[1]))),
                pl.BlockSpec((depth, LANES), lambda y, p: (0, column(y, 1 - p[0], p[1]))),
                pl.BlockSpec((depth, 2 * LANES), lambda y, _: (0, y)),
            ],
            out_specs=pl.BlockSpec((1, rows, 2 * LANES), lambda y, _: (y, 0, 0)),
        ),
        cost_estimate=pl.CostEstimate(
            flops=2 * rows * depth * width, bytes_accessed=rows * (4 * depth + width) + weight.size * 2, transcendentals=0
        ),
        compiler_params=pltpu.CompilerParams(vmem_limit_bytes=VMEM),
    )(place, own, sibling, weight, weight, packed)


def after(array, *earlier):
    return lax.optimization_barrier((array, *earlier))[0]


def exchange(array, axis):
    return lax.all_to_all(array, axis, split_axis=0, concat_axis=0, tiled=True)


def shards(local_weights, base, momentum, tokens, weight):
    sizes = dict(zip(NAMES, SIZES))
    zo, zi, x, _, h, c = (lax.axis_index(a) for a in NAMES)
    n_zo, n_zi, n_x, n_y = (sizes[a] for a in ("zo", "zi", "x", "y"))
    swap = [(0, 1), (1, 0)]
    groups = n_zo * n_zi * n_x
    rows, width = base.shape
    own = rows // groups
    per_x, per_zi = rows // n_x, rows // (n_x * n_zi)

    terms = exchange(local_weights[0].reshape(n_x, per_x, width), "x")

    anchor = lax.dynamic_slice_in_dim(base, x * per_x, per_x, 0).astype(bf16).astype(f32)
    total = terms[0].astype(f32) - n_x * anchor
    for term in range(1, n_x):
        total += terms[term].astype(f32)
    total = total.astype(bf16)

    place = jnp.stack([h, c]).astype(jnp.int32)
    sibling = lax.ppermute(tokens, "c", swap)
    packed = lax.ppermute(pack(place, weight, n_y), "c", swap)

    total, sibling, packed = lax.optimization_barrier((total, sibling, packed))
    terms = exchange(total.reshape(n_zi, per_zi, width), "zi")
    part = project(place, tokens, sibling, weight, packed, n_y)
    terms = after(terms, part)
    total = terms.astype(f32).sum(axis=0).astype(bf16)
    total, part = lax.optimization_barrier((total, part))
    part = exchange(part, "y")

    once = 1 + (h >> 4)

    def alone(function, value, shape):
        carry = (value, jnp.zeros(shape, bf16))
        return lax.fori_loop(0, once, lambda _, carry: (-carry[0], function(carry[0])), carry)[1]

    def outer(total):
        across = lax.ppermute(total, "zo", swap)
        outer_grad = (-(total.astype(f32) + across.astype(f32)) / groups).astype(bf16)
        return jnp.broadcast_to(outer_grad, (n_zi, per_zi, width))

    outer_grad = alone(outer, total, (n_zi, per_zi, width))
    outer_grad, base, momentum, part = lax.optimization_barrier((outer_grad, base, momentum, part))
    gathered = exchange(outer_grad, "zi")

    kv = part[0].astype(f32)
    for piece in range(1, n_y):
        kv += part[piece].astype(f32)
    without = base - 0.567 * momentum
    mine, other, without = lax.optimization_barrier((kv[:, :LANES], kv[:, LANES:].astype(bf16), without))
    gathered, other = lax.optimization_barrier((gathered, other))
    there = lax.ppermute(other, "h", swap)
    gathered = gathered.reshape(per_x, width)
    start = ((zo * n_zi + zi) * n_x + x) * own

    def own_rows(array):
        return lax.dynamic_slice_in_dim(array, start, own, 0).astype(f32)

    def finish(gathered):
        outer_grad = lax.all_gather(gathered, "x", axis=0, tiled=True)
        synced = (without - 1.33 * outer_grad.astype(f32)).astype(bf16)
        new_base = own_rows(without) - 1.33 * own_rows(outer_grad)
        new_momentum = 0.9 * own_rows(momentum) + own_rows(outer_grad)
        return synced, new_base, new_momentum

    empty = (jnp.zeros((rows, width), bf16), jnp.zeros((own, width), f32), jnp.zeros((own, width), f32))
    carry = (gathered, *empty)
    carry = lax.fori_loop(0, once, lambda _, carry: (-carry[0], *finish(carry[0])), carry)
    synced, new_base, new_momentum = carry[1:]
    there = after(there, synced, new_base)
    keys_values = (mine + there.astype(f32)).astype(bf16)
    return new_base, new_momentum, synced, keys_values


def solution(mesh):
    fine = Mesh(mesh.devices.reshape(SIZES), NAMES)
    replica, mp = NAMES[:3], NAMES[3:]
    return jax.shard_map(
        shards,
        mesh=fine,
        in_specs=(
            P(replica, None, mp),
            P(None, mp),
            P(None, mp),
            P(replica, mp),
            P(mp, None),
        ),
        out_specs=(P(replica, mp), P(replica, mp), P(None, mp), P(replica, mp)),
        check_vma=False,
    )
```

time: 160 us -> 159 us (level)
  the two profiles are of different devices: /device:TPU:296 before, /device:TPU:230 now
where the time goes in v7:
time: 159 us; the launch traced here: 158 us
  starting transfers between devices  64.9 us (41%)
  waiting for transfers between devices  56.3 us (35%)
  blocking collectives  14.3 us (9%)
  local copies, waits for them, and re-layouts  8.86 us (6%)
  Pallas kernels  7.78 us (5%)
  other arithmetic  5.44 us (3%)
    ppermute x1, waiting for transfers between devices, shards(): there = lax.ppermute(other, 'h', swap)  30.7 us
    all_to_all x4, starting transfers between devices, exchange(): return lax.all_to_all(array, axis, split_axis=0, concat_axis=0, tiled=True)  28.7 us
    all_to_all x4, waiting for transfers between devices, exchange(): return lax.all_to_all(array, axis, split_axis=0, concat_axis=0, tiled=True)  23.8 us
    ppermute x1, starting transfers between devices, shards(): there = lax.ppermute(other, 'h', swap)  17.5 us
    ppermute x1, starting transfers between devices, outer(): across = lax.ppermute(total, 'zo', swap)  14.4 us
    all_gather x1, blocking collectives, finish(): outer_grad = lax.all_gather(gathered, 'x', axis=0, tiled=True)  14.3 us
    pallas_call x1, Pallas kernels, project(): pl.pallas_call(project_kernel, out_shape=jax.ShapeDtypeStruct((n_y, rows,...  5.31 us
    unnamed x14, local copies, waits for them, and re-layouts  4.46 us
  transfers between devices with their start and end apart: 8, of which 6 were waited for; matrix products, arithmetic and copies ran while one was open for 6% of the time, Pallas kernels for 5%

profile of v7, /device:TPU:230, one launch (start us, length us, event | category | flops | bytes accessed | tf_op | source)
XLA Modules:
  0.0 158.4 jit_solution(1982949317629848673)
XLA Ops:
  0.6 0.0 copy-start.3
  0.6 4.9 %all-to-all-start = ((bf16[4,64,1792]{2,1,0:T(8,128)(2,1)}), bf16[4,64,1792]{2,1,0:T(8,128)(2,1)}, u32[]{:S(2)}, u32[]{:S(2)}) async-start(bf16[4,64,1792]{2,1,0:T(8,128)(2,1)} %bitcast.28), calls=%async_computation | async-start | bytes 1835008 | tf_op jit(solution)/shard_map/all_to_all | solution.py:82
  5.6 0.0 copy-done.3
  5.6 1.9 %collective-permute-start.1 = (bf16[1024,512]{1,0:T(8,128)(2,1)S(1)}, bf16[1024,512]{1,0:T(8,128)(2,1)}, u32[]{:S(2)}, u32[]{:S(2)}) collective-permute-start(bf16[1024,512]{1,0:T(8,128)(2,1)S(1)} %copy-done.3), channel_id=1, source_target_pairs={{0,1},{1,0},{2,3},{3,2},{4,5},{5,4},{6,7},{7,6},{8,9},{9,8},{10,11... | collective-permute-start | bytes 3145736 | tf_op jit(solution)/shard_map/ppermute | solution.py:104
  7.5 0.1 pad_add_fusion.place_ref
  7.6 0.0 copy-start
  7.6 1.6 %copy-done = bf16[512,2048]{1,0:T(8,128)(2,1)S(1)} copy-done((bf16[512,2048]{1,0:T(8,128)(2,1)S(1)}, bf16[512,2048]{1,0:T(8,128)(2,1)}, u32[]{:S(2)}) %copy-start) | copy-done | bytes 2097176
  9.1 0.0 copy-start.1
  9.1 2.5 %shard_map.84 = bf16[512,1024]{1,0:T(8,128)(2,1)} custom-call(s32[2]{0:T(128)S(1)} %pad_add_fusion.place_ref, bf16[512,2048]{1,0:T(8,128)(2,1)S(1)} %copy-done, bf16[512,2048]{1,0:T(8,128)(2,1)S(1)} %copy-done), custom_call_target="tpu_custom_call" | custom-call | bytes 2097152 | tf_op jit(solution)/shard_map/pallas_call | solution.py:28
  11.6 2.4 %collective-permute-start.2 = (bf16[512,1024]{1,0:T(8,128)(2,1)}, bf16[512,1024]{1,0:T(8,128)(2,1)}, u32[]{:S(2)}, u32[]{:S(2)}) collective-permute-start(bf16[512,1024]{1,0:T(8,128)(2,1)} %shard_map.84), channel_id=1, source_target_pairs={{0,1},{1,0},{2,3},{3,2},{4,5},{5,4},{6,7},{7,6},{8,9},{9,8},{10,11... | collective-permute-start | bytes 3145736 | tf_op jit(solution)/shard_map/ppermute | solution.py:105
  14.0 3.4 %all-to-all-done = bf16[4,64,1792]{2,1,0:T(8,128)(2,1)} async-done(((bf16[4,64,1792]{2,1,0:T(8,128)(2,1)}), bf16[4,64,1792]{2,1,0:T(8,128)(2,1)}, u32[]{:S(2)}, u32[]{:S(2)}) %all-to-all-start) | async-done | bytes 917536 | tf_op jit(solution)/shard_map/all_to_all | solution.py:82
  17.4 2.2 %fusion.1 = bf16[64,1792]{1,0:T(8,128)(2,1)} fusion(f32[256,1792]{1,0:T(8,128)} %param.10, s32[]{:T(128)S(6)} %select_n.11, bf16[4,64,1792]{2,1,0:T(8,128)(2,1)} %all-to-all-done), kind=kLoop, calls=%fused_computation.10 | loop fusion | flops 1261568 | bytes 1376260 | tf_op jit(solution)/shard_map/convert_element_type | solution.py:101
  19.7 0.0 collective-permute-done.1.sibling_ref
  19.7 0.0 collective-permute-done.2.packed_ref
  19.7 10.3 %all-to-all-start.1 = ((bf16[8,8,1792]{2,1,0:T(8,128)(2,1)}), bf16[8,8,1792]{2,1,0:T(8,128)(2,1)S(1)}, u32[]{:S(2)}, u32[]{:S(2)}) async-start(bf16[8,8,1792]{2,1,0:T(8,128)(2,1)} %bitcast.7), calls=%async_computation.1 | async-start | bytes 458752 | tf_op jit(solution)/shard_map/all_to_all | solution.py:82
  29.9 0.0 copy-done.1
  29.9 5.3 %shard_map.85 = bf16[4,1024,256]{2,1,0:T(8,128)(2,1)S(1)} custom-call(s32[2]{0:T(128)S(1)} %pad_add_fusion.place_ref, bf16[1024,512]{1,0:T(8,128)(2,1)S(1)} %copy-done.3, bf16[1024,512]{1,0:T(8,128)(2,1)} %collective-permute-done.1.sibling_ref, bf16[512,2048]{1,0:T(8,128)(2,1)S(1)} %copy-done.1, bf16[512,2048]{1,0:T(8,128)(2,1)S(1)} %copy-done.1, ...), custom_call_target="tpu_custom_call" | custom-call | flops 2147483648 | bytes 6291456 | tf_op jit(solution)/shard_map/pallas_call | solution.py:55
  35.2 0.0 copy-start.2
  35.2 1.3 copy-done.2
  36.6 4.6 %all-to-all-done.1 = bf16[8,8,1792]{2,1,0:T(8,128)(2,1)S(1)} async-done(((bf16[8,8,1792]{2,1,0:T(8,128)(2,1)}), bf16[8,8,1792]{2,1,0:T(8,128)(2,1)S(1)}, u32[]{:S(2)}, u32[]{:S(2)}) %all-to-all-start.1) | async-done | bytes 229408 | tf_op jit(solution)/shard_map/all_to_all | solution.py:82
  41.2 3.6 %all-to-all-start.2 = ((bf16[4,1024,256]{2,1,0:T(8,128)(2,1)}), bf16[4,1024,256]{2,1,0:T(8,128)(2,1)S(1)}, u32[]{:S(2)}, u32[]{:S(2)}) async-start(bf16[4,1024,256]{2,1,0:T(8,128)(2,1)} %copy-done.2), calls=%async_computation.2 | async-start | bytes 4194304 | tf_op jit(solution)/shard_map/all_to_all | solution.py:82
  44.8 0.7 broadcast_in_dim.9
  45.5 17.0 %while.30 = (s32[]{:T(128)}, bf16[8,1792]{1,0:T(8,128)(2,1)S(1)}, bf16[8,8,1792]{2,1,0:T(8,128)(2,1)}, s32[]{:T(128)}, s32[]{:T(128)}) while((s32[]{:T(128)}, bf16[8,1792]{1,0:T(8,128)(2,1)S(1)}, bf16[8,8,1792]{2,1,0:T(8,128)(2,1)}, s32[]{:T(128)}, s32[]{:T(128)}) %tuple.59), condition=%wide.region_2.0_spmd, body=%wide.region_1.0_spmd.sunk | while | flops 100354 | bytes 573541 | solution.py:119
  45.5 14.4 %collective-permute-start = (bf16[8,1792]{1,0:T(8,128)(2,1)S(1)}, bf16[8,1792]{1,0:T(8,128)(2,1)S(1)}, u32[]{:S(2)}, u32[]{:S(2)}) collective-permute-start(bf16[8,1792]{1,0:T(8,128)(2,1)S(1)} %copy.13), channel_id=1, source_target_pairs={{0,512},{512,0},{1,513},{513,1},{2,514},{514,2},{3,515},{515,3},{4... | collective-permute-start | bytes 86024 | tf_op jit(solution)/shard_map/while/body/ppermute | solution.py:122
  60.0 1.8 %collective-permute-done = bf16[8,1792]{1,0:T(8,128)(2,1)S(1)} collective-permute-done((bf16[8,1792]{1,0:T(8,128)(2,1)S(1)}, bf16[8,1792]{1,0:T(8,128)(2,1)S(1)}, u32[]{:S(2)}, u32[]{:S(2)}) %collective-permute-start) | collective-permute-done | bytes 28704 | tf_op jit(solution)/shard_map/while/body/ppermute | solution.py:122
  61.8 0.7 broadcast_in_dim.12
  62.5 9.0 %all-to-all-done.2 = bf16[4,1024,256]{2,1,0:T(8,128)(2,1)S(1)} async-done(((bf16[4,1024,256]{2,1,0:T(8,128)(2,1)}), bf16[4,1024,256]{2,1,0:T(8,128)(2,1)S(1)}, u32[]{:S(2)}, u32[]{:S(2)}) %all-to-all-start.2) | async-done | bytes 2097184 | tf_op jit(solution)/shard_map/all_to_all | solution.py:82
  71.5 9.9 %all-to-all-start.3 = ((bf16[8,8,1792]{2,1,0:T(8,128)(2,1)}), bf16[8,8,1792]{2,1,0:T(8,128)(2,1)S(1)}, u32[]{:S(2)}, u32[]{:S(2)}) async-start(bf16[8,8,1792]{2,1,0:T(8,128)(2,1)} %get-tuple-element.160), calls=%async_computation.3 | async-start | bytes 458752 | tf_op jit(solution)/shard_map/all_to_all | solution.py:82
  81.4 0.0 copy-start.5
  81.4 0.0 copy-start.6
  81.4 0.2 add_bitcast_fusion
  81.6 0.0 copy-start.4
  81.6 0.7 slice.64
  82.4 1.0 copy-done.5
  83.3 0.6 copy-done.6
  83.9 0.2 multiply_subtract_fusion
  84.1 0.0 copy-done.4
  84.2 6.8 %all-to-all-done.3 = bf16[8,8,1792]{2,1,0:T(8,128)(2,1)S(1)} async-done(((bf16[8,8,1792]{2,1,0:T(8,128)(2,1)}), bf16[8,8,1792]{2,1,0:T(8,128)(2,1)S(1)}, u32[]{:S(2)}, u32[]{:S(2)}) %all-to-all-start.3) | async-done | bytes 229408 | tf_op jit(solution)/shard_map/all_to_all | solution.py:82
  91.0 17.5 %collective-permute-start.3 = (bf16[1024,128]{1,0:T(8,128)(2,1)}, bf16[1024,128]{1,0:T(8,128)(2,1)S(1)}, u32[]{:S(2)}, u32[]{:S(2)}) collective-permute-start(bf16[1024,128]{1,0:T(8,128)(2,1)} %slice.64), channel_id=1, source_target_pairs={{0,2},{2,0},{1,3},{3,1},{4,6},{6,4},{5,7},{7,5},{8,10},{10,8},{9,1... | collective-permute-start | bytes 786440 | tf_op jit(solution)/shard_map/ppermute | solution.py:136
  108.6 1.0 broadcast_in_dim.10
  109.5 0.6 broadcast.22
  110.2 0.6 broadcast.22.clone
  110.8 0.0 slice-start
  110.8 16.1 %while.31 = (s32[]{:T(128)}, bf16[64,1792]{1,0:T(8,128)(2,1)S(1)}, bf16[256,1792]{1,0:T(8,128)(2,1)}, f32[4,1792]{1,0:T(4,128)}, f32[4,1792]{1,0:T(4,128)}, /*in...) while((s32[]{:T(128)}, bf16[64,1792]{1,0:T(8,128)(2,1)S(1)}, ...), condition=%wide.region_4.0_spmd, body=%wide.region_3.0_spmd.sunk | while | flops 1985538 | bytes 5404785 | solution.py:152
  110.8 14.3 %all_gather.6 = bf16[256,1792]{1,0:T(8,128)(2,1)S(1)} all-gather(bf16[64,1792]{1,0:T(8,128)(2,1)S(1)} %get-tuple-element.314), channel_id=1, replica_groups=mesh['zo'=2,'zi'=8,'x'=4,'y'=4,'h'=2,'c'=2] {'x'}, dimensions={0}, use_global_device_ids=true | all-gather | bytes 1146880 | tf_op jit(solution)/shard_map/while/body/all_gather | solution.py:144
  125.0 0.1 neg.17
  125.1 1.2 subtract_convert_fusion.2
  126.3 0.6 convert_add_fusion.5
  126.9 30.7 %collective-permute-done.3 = bf16[1024,128]{1,0:T(8,128)(2,1)S(1)} collective-permute-done((bf16[1024,128]{1,0:T(8,128)(2,1)}, bf16[1024,128]{1,0:T(8,128)(2,1)S(1)}, u32[]{:S(2)}, u32[]{:S(2)}) %collective-permute-start.3) | collective-permute-done | bytes 262176 | tf_op jit(solution)/shard_map/ppermute | solution.py:136
  157.6 0.0 slice-done
  157.6 0.8 add_convert_fusion
  (6 shorter events, 0.1 us)
Async XLA Ops:
  0.6 4.9 %copy-start.3 = (bf16[1024,512]{1,0:T(8,128)(2,1)S(1)}, bf16[1024,512]{1,0:T(8,128)(2,1)}, u32[]{:S(2)}) copy-start(bf16[1024,512]{1,0:T(8,128)(2,1)} %own_ref.1) | copy-start | bytes 3145732
  0.6 16.8 %all-to-all-start = ((bf16[4,64,1792]{2,1,0:T(8,128)(2,1)}), bf16[4,64,1792]{2,1,0:T(8,128)(2,1)}, u32[]{:S(2)}, u32[]{:S(2)}) async-start(bf16[4,64,1792]{2,1,0:T(8,128)(2,1)} %bitcast.28), calls=%async_computation | async-start | bytes 1835008 | tf_op jit(solution)/shard_map/all_to_all | solution.py:82
  5.6 14.1 %collective-permute-start.1 = (bf16[1024,512]{1,0:T(8,128)(2,1)S(1)}, bf16[1024,512]{1,0:T(8,128)(2,1)}, u32[]{:S(2)}, u32[]{:S(2)}) collective-permute-start(bf16[1024,512]{1,0:T(8,128)(2,1)S(1)} %copy-done.3), channel_id=1, source_target_pairs={{0,1},{1,0},{2,3},{3,2},{4,5},{5,4},{6,7},{7,6},{8,9},{9,8},{10,11... | collective-permute-start | bytes 3145736 | tf_op jit(solution)/shard_map/ppermute | solution.py:104
  7.6 1.6 %copy-start = (bf16[512,2048]{1,0:T(8,128)(2,1)S(1)}, bf16[512,2048]{1,0:T(8,128)(2,1)}, u32[]{:S(2)}) copy-start(bf16[512,2048]{1,0:T(8,128)(2,1)} %far_ref.3) | copy-start | bytes 6291460
  9.1 20.8 %copy-start.1 = (bf16[512,2048]{1,0:T(8,128)(2,1)S(1)}, bf16[512,2048]{1,0:T(8,128)(2,1)}, u32[]{:S(2)}) copy-start(bf16[512,2048]{1,0:T(8,128)(2,1)} %far_ref.3) | copy-start | bytes 6291460
  11.6 8.0 %collective-permute-start.2 = (bf16[512,1024]{1,0:T(8,128)(2,1)}, bf16[512,1024]{1,0:T(8,128)(2,1)}, u32[]{:S(2)}, u32[]{:S(2)}) collective-permute-start(bf16[512,1024]{1,0:T(8,128)(2,1)} %shard_map.84), channel_id=1, source_target_pairs={{0,1},{1,0},{2,3},{3,2},{4,5},{5,4},{6,7},{7,6},{8,9},{9,8},{10,11... | collective-permute-start | bytes 3145736 | tf_op jit(solution)/shard_map/ppermute | solution.py:105
  19.7 21.5 %all-to-all-start.1 = ((bf16[8,8,1792]{2,1,0:T(8,128)(2,1)}), bf16[8,8,1792]{2,1,0:T(8,128)(2,1)S(1)}, u32[]{:S(2)}, u32[]{:S(2)}) async-start(bf16[8,8,1792]{2,1,0:T(8,128)(2,1)} %bitcast.7), calls=%async_computation.1 | async-start | bytes 458752 | tf_op jit(solution)/shard_map/all_to_all | solution.py:82
  35.2 1.3 copy-start.2
  41.2 30.3 %all-to-all-start.2 = ((bf16[4,1024,256]{2,1,0:T(8,128)(2,1)}), bf16[4,1024,256]{2,1,0:T(8,128)(2,1)S(1)}, u32[]{:S(2)}, u32[]{:S(2)}) async-start(bf16[4,1024,256]{2,1,0:T(8,128)(2,1)} %copy-done.2), calls=%async_computation.2 | async-start | bytes 4194304 | tf_op jit(solution)/shard_map/all_to_all | solution.py:82
  45.5 16.2 %collective-permute-start = (bf16[8,1792]{1,0:T(8,128)(2,1)S(1)}, bf16[8,1792]{1,0:T(8,128)(2,1)S(1)}, u32[]{:S(2)}, u32[]{:S(2)}) collective-permute-start(bf16[8,1792]{1,0:T(8,128)(2,1)S(1)} %copy.13), channel_id=1, source_target_pairs={{0,512},{512,0},{1,513},{513,1},{2,514},{514,2},{3,515},{515,3},{4... | collective-permute-start | bytes 86024 | tf_op jit(solution)/shard_map/while/body/ppermute | solution.py:122
  71.5 19.5 %all-to-all-start.3 = ((bf16[8,8,1792]{2,1,0:T(8,128)(2,1)}), bf16[8,8,1792]{2,1,0:T(8,128)(2,1)S(1)}, u32[]{:S(2)}, u32[]{:S(2)}) async-start(bf16[8,8,1792]{2,1,0:T(8,128)(2,1)} %get-tuple-element.160), calls=%async_computation.3 | async-start | bytes 458752 | tf_op jit(solution)/shard_map/all_to_all | solution.py:82
  81.4 2.0 %copy-start.5 = (f32[256,1792]{1,0:T(8,128)S(1)}, f32[256,1792]{1,0:T(8,128)}, u32[]{:S(2)}) copy-start(f32[256,1792]{1,0:T(8,128)} %param.10) | copy-start | bytes 5505028
  81.4 2.5 %copy-start.6 = (f32[256,1792]{1,0:T(8,128)S(1)}, f32[256,1792]{1,0:T(8,128)}, u32[]{:S(2)}) copy-start(f32[256,1792]{1,0:T(8,128)} %param.11) | copy-start | bytes 5505028
  81.6 2.5 %copy-start.4 = (f32[1024,256]{1,0:T(8,128)}, f32[1024,256]{1,0:T(8,128)S(1)}, u32[]{:S(2)}) copy-start(f32[1024,256]{1,0:T(8,128)S(1)} %add_bitcast_fusion) | copy-start | bytes 3145732
  91.0 66.6 %collective-permute-start.3 = (bf16[1024,128]{1,0:T(8,128)(2,1)}, bf16[1024,128]{1,0:T(8,128)(2,1)S(1)}, u32[]{:S(2)}, u32[]{:S(2)}) collective-permute-start(bf16[1024,128]{1,0:T(8,128)(2,1)} %slice.64), channel_id=1, source_target_pairs={{0,2},{2,0},{1,3},{3,1},{4,6},{6,4},{5,7},{7,5},{8,10},{10,8},{9,1... | collective-permute-start | bytes 786440 | tf_op jit(solution)/shard_map/ppermute | solution.py:136
  110.8 46.8 %slice-start = ((f32[1024,256]{1,0:T(8,128)}), f32[1024,128]{1,0:T(8,128)S(1)}, s32[]{:S(2)}) async-start(f32[1024,256]{1,0:T(8,128)} %copy-done.4), calls=%async_computation.4 | async-start | bytes 1048576 | tf_op jit(solution)/shard_map/slice | solution.py:134

commit v8 on v7

--- a/solution.py
+++ b/solution.py
@@ -32,8 +32,8 @@
             num_scalar_prefetch=1,
             grid=(n_y,),
             in_specs=[
-                pl.BlockSpec((depth, LANES), lambda y, p: (0, column(y, p[0], 1 - p[1]))),
-                pl.BlockSpec((depth, LANES), lambda y, p: (0, column(y, 1 - p[0], 1 - p[1]))),
+                pl.BlockSpec((depth, LANES), lambda y, p: (0, column((y + p[2]) % n_y, p[0], 1 - p[1]))),
+                pl.BlockSpec((depth, LANES), lambda y, p: (0, column((y + p[2]) % n_y, 1 - p[0], 1 - p[1]))),
             ],
             out_specs=pl.BlockSpec((depth, 2 * LANES), lambda y, _: (0, y)),
         ),
@@ -42,11 +42,16 @@
     )(place, weight, weight)
 
 
-def project_kernel(place_ref, own_ref, sibling_ref, near_ref, far_ref, packed_ref, out_ref):
+def project_kernel(place_ref, own_ref, sibling_ref, near_ref, far_ref, packed_ref, *out_refs):
     mine = jnp.concatenate([near_ref[...], far_ref[...]], axis=1)
     total = jnp.dot(own_ref[...], mine, preferred_element_type=f32)
     total += jnp.dot(sibling_ref[...], packed_ref[...], preferred_element_type=f32)
-    out_ref[0] = total.astype(bf16)
+    total = total.astype(bf16)
+    for step, out_ref in enumerate(out_refs):
+
+        @pl.when(pl.program_id(0) == step)
+        def _(out_ref=out_ref):
+            out_ref[...] = total
 
 
 def project(place, own, sibling, weight, packed, n_y):
@@ -54,24 +59,28 @@
     width = weight.shape[1]
     return pl.pallas_call(
         project_kernel,
-        out_shape=jax.ShapeDtypeStruct((n_y, rows, 2 * LANES), bf16),
+        out_shape=[jax.ShapeDtypeStruct((rows, 2 * LANES), bf16)] * n_y,
         grid_spec=pltpu.PrefetchScalarGridSpec(
             num_scalar_prefetch=1,
             grid=(n_y,),
             in_specs=[
                 pl.BlockSpec((rows, depth), lambda y, _: (0, 0)),
                 pl.BlockSpec((rows, depth), lambda y, _: (0, 0)),
-                pl.BlockSpec((depth, LANES), lambda y, p: (0, column(y, p[0], p[1]))),
-                pl.BlockSpec((depth, LANES), lambda y, p: (0, column(y, 1 - p[0], p[1]))),
+                pl.BlockSpec((depth, LANES), lambda y, p: (0, column((y + p[2]) % n_y, p[0], p[1]))),
+                pl.BlockSpec((depth, LANES), lambda y, p: (0, column((y + p[2]) % n_y, 1 - p[0], p[1]))),
                 pl.BlockSpec((depth, 2 * LANES), lambda y, _: (0, y)),
             ],
-            out_specs=pl.BlockSpec((1, rows, 2 * LANES), lambda y, _: (y, 0, 0)),
+            out_specs=[pl.BlockSpec((rows, 2 * LANES), lambda y, _: (0, 0))] * n_y,
         ),
         cost_estimate=pl.CostEstimate(
             flops=2 * rows * depth * width, bytes_accessed=rows * (4 * depth + width) + weight.size * 2, transcendentals=0
         ),
         compiler_params=pltpu.CompilerParams(vmem_limit_bytes=VMEM),
     )(place, own, sibling, weight, weight, packed)
+
+
+def shift(axis, size, step):
+    return [(i, (i + step) % size) for i in range(size)]
 
 
 def after(array, *earlier):
@@ -84,7 +93,7 @@
 
 def shards(local_weights, base, momentum, tokens, weight):
     sizes = dict(zip(NAMES, SIZES))
-    zo, zi, x, _, h, c = (lax.axis_index(a) for a in NAMES)
+    zo, zi, x, y, h, c = (lax.axis_index(a) for a in NAMES)
     n_zo, n_zi, n_x, n_y = (sizes[a] for a in ("zo", "zi", "x", "y"))
     swap = [(0, 1), (1, 0)]
     groups = n_zo * n_zi * n_x
@@ -100,17 +109,16 @@
         total += terms[term].astype(f32)
     total = total.astype(bf16)
 
-    place = jnp.stack([h, c]).astype(jnp.int32)
+    place = jnp.stack([h, c, y]).astype(jnp.int32)
     sibling = lax.ppermute(tokens, "c", swap)
     packed = lax.ppermute(pack(place, weight, n_y), "c", swap)
 
     total, sibling, packed = lax.optimization_barrier((total, sibling, packed))
     terms = exchange(total.reshape(n_zi, per_zi, width), "zi")
     part = project(place, tokens, sibling, weight, packed, n_y)
-    terms = after(terms, part)
+    terms = after(terms, *part)
     total = terms.astype(f32).sum(axis=0).astype(bf16)
-    total, part = lax.optimization_barrier((total, part))
-    part = exchange(part, "y")
+    part = [part[0]] + [lax.ppermute(part[step], "y", shift("y", n_y, step)) for step in range(1, n_y)]
 
     once = 1 + (h >> 4)
 
@@ -123,8 +131,8 @@
         outer_grad = (-(total.astype(f32) + across.astype(f32)) / groups).astype(bf16)
         return jnp.broadcast_to(outer_grad, (n_zi, per_zi, width))
 
-    outer_grad = alone(outer, total, (n_zi, per_zi, width))
-    outer_grad, base, momentum, part = lax.optimization_barrier((outer_grad, base, momentum, part))
+    outer_grad = outer(total)
+    outer_grad, base, momentum, *part = lax.optimization_barrier((outer_grad, base, momentum, *part))
     gathered = exchange(outer_grad, "zi")
 
     kv = part[0].astype(f32)

time: 159 us -> 161 us (1.013)
  the two profiles are of different devices: /device:TPU:230 before, /device:TPU:296 now
where the time goes in v8:
time: 161 us; the launch traced here: 160 us
  waiting for transfers between devices  69.1 us (43%)
  starting transfers between devices  55.6 us (35%)
  blocking collectives  14.4 us (9%)
  Pallas kernels  8.16 us (5%)
  local copies, waits for them, and re-layouts  6.72 us (4%)
  other arithmetic  5.42 us (3%)
    ppermute x1, waiting for transfers between devices, shards(): there = lax.ppermute(other, 'h', swap)  32.7 us
    all_to_all x3, starting transfers between devices, exchange(): return lax.all_to_all(array, axis, split_axis=0, concat_axis=0, tiled=True)  26.8 us
    all_to_all x3, waiting for transfers between devices, exchange(): return lax.all_to_all(array, axis, split_axis=0, concat_axis=0, tiled=True)  19 us
    all_gather x1, blocking collectives, finish(): outer_grad = lax.all_gather(gathered, 'x', axis=0, tiled=True)  14.4 us
    ppermute x1, waiting for transfers between devices, outer(): across = lax.ppermute(total, 'zo', swap)  12.7 us
    ppermute x1, starting transfers between devices, shards(): there = lax.ppermute(other, 'h', swap)  11.8 us
    ppermute x3, starting transfers between devices, shards(): lax.ppermute(part[step], 'y', shift('y', n_y, step))  10.6 us
    pallas_call x1, Pallas kernels, project(): pl.pallas_call(project_kernel, out_shape=[jax.ShapeDtypeStruct((rows, 2 *...  6.79 us
  transfers between devices with their start and end apart: 10, of which 5 were waited for; matrix products, arithmetic and copies ran while one was open for 4% of the time, Pallas kernels for 5%

profile of v8, /device:TPU:296, one launch (start us, length us, event | category | flops | bytes accessed | tf_op | source)
XLA Modules:
  0.0 160.2 jit_solution(16800000592340315068)
XLA Ops:
  0.6 4.3 %all-to-all-start = ((bf16[4,64,1792]{2,1,0:T(8,128)(2,1)}), bf16[4,64,1792]{2,1,0:T(8,128)(2,1)}, u32[]{:S(2)}, u32[]{:S(2)}) async-start(bf16[4,64,1792]{2,1,0:T(8,128)(2,1)} %bitcast.27), calls=%async_computation | async-start | bytes 1835008 | tf_op jit(solution)/shard_map/all_to_all | solution.py:91
  4.9 1.9 %collective-permute-start = (bf16[1024,512]{1,0:T(8,128)(2,1)}, bf16[1024,512]{1,0:T(8,128)(2,1)}, u32[]{:S(2)}, u32[]{:S(2)}) collective-permute-start(bf16[1024,512]{1,0:T(8,128)(2,1)} %own_ref.1), channel_id=1, source_target_pairs={{0,1},{1,0},{2,3},{3,2},{4,5},{5,4},{6,7},{7,6},{8,9},{9,8},{10,11... | collective-permute-start | bytes 3145736 | tf_op jit(solution)/shard_map/ppermute | solution.py:113
  6.9 0.1 pad_add_fusion.place_ref
  6.9 0.0 copy-start
  6.9 1.6 copy-done
  8.5 0.0 copy-start.1
  8.5 1.4 shard_map.84
  9.9 2.4 %collective-permute-start.1 = (bf16[512,1024]{1,0:T(8,128)(2,1)S(1)}, bf16[512,1024]{1,0:T(8,128)(2,1)}, u32[]{:S(2)}, u32[]{:S(2)}) collective-permute-start(bf16[512,1024]{1,0:T(8,128)(2,1)S(1)} %shard_map.84), channel_id=1, source_target_pairs={{0,1},{1,0},{2,3},{3,2},{4,5},{5,4},{6,7},{7,6},{8,9},{9,8},{10,11... | collective-permute-start | bytes 3145736 | tf_op jit(solution)/shard_map/ppermute | solution.py:114
  12.3 6.6 %all-to-all-done = bf16[4,64,1792]{2,1,0:T(8,128)(2,1)} async-done(((bf16[4,64,1792]{2,1,0:T(8,128)(2,1)}), bf16[4,64,1792]{2,1,0:T(8,128)(2,1)}, u32[]{:S(2)}, u32[]{:S(2)}) %all-to-all-start) | async-done | bytes 917536 | tf_op jit(solution)/shard_map/all_to_all | solution.py:91
  18.9 2.2 %fusion.1 = bf16[64,1792]{1,0:T(8,128)(2,1)} fusion(f32[256,1792]{1,0:T(8,128)} %param.8, s32[]{:T(128)S(6)} %select_n.11, bf16[4,64,1792]{2,1,0:T(8,128)(2,1)} %all-to-all-done), kind=kLoop, calls=%fused_computation.9 | loop fusion | flops 1261568 | bytes 1376260 | tf_op jit(solution)/shard_map/convert_element_type | solution.py:110
  21.1 0.0 collective-permute-done.sibling_ref
  21.1 0.0 collective-permute-done.1.packed_ref
  21.1 12.6 %all-to-all-start.1 = ((bf16[8,8,1792]{2,1,0:T(8,128)(2,1)}), bf16[8,8,1792]{2,1,0:T(8,128)(2,1)S(1)}, u32[]{:S(2)}, u32[]{:S(2)}) async-start(bf16[8,8,1792]{2,1,0:T(8,128)(2,1)} %bitcast.8), calls=%async_computation.1 | async-start | bytes 458752 | tf_op jit(solution)/shard_map/all_to_all | solution.py:91
  33.7 0.0 copy-done.1
  33.7 6.8 %shard_map.85 = (bf16[1024,256]{1,0:T(8,128)(2,1)S(1)}, bf16[1024,256]{1,0:T(8,128)(2,1)}, bf16[1024,256]{1,0:T(8,128)(2,1)}, bf16[1024,256]{1,0:T(8,128)(2,1)S(1)}) custom-call(s32[3]{0:T(128)S(1)} %pad_add_fusion.place_ref, bf16[1024,512]{1,0:T(8,128)(2,1)} %own_ref.1, bf16[1024,512]{1,0:T(8,128)(2,1)} %collective-permute-done.sibling_ref, ...), custom_call_target="tpu_custom_call" | custom-call | flops 2147483648 | bytes 6291456 | tf_op jit(solution)/shard_map/pallas_call | solution.py:60
  40.5 3.5 %collective-permute-start.3 = (bf16[1024,256]{1,0:T(8,128)(2,1)}, bf16[1024,256]{1,0:T(8,128)(2,1)S(1)}, u32[]{:S(2)}, u32[]{:S(2)}) collective-permute-start(bf16[1024,256]{1,0:T(8,128)(2,1)} %get-tuple-element.140), channel_id=1, source_target_pairs={{0,4},{4,8},{8,12},{12,0},{1,5},{5,9},{9,13},{13,1},{2,6},{6,10},{... | collective-permute-start | bytes 1572872 | tf_op jit(solution)/shard_map/ppermute | solution.py:121
  44.0 2.8 %collective-permute-start.4 = (bf16[1024,256]{1,0:T(8,128)(2,1)}, bf16[1024,256]{1,0:T(8,128)(2,1)S(1)}, u32[]{:S(2)}, u32[]{:S(2)}) collective-permute-start(bf16[1024,256]{1,0:T(8,128)(2,1)} %get-tuple-element.141), channel_id=1, source_target_pairs={{0,8},{4,12},{8,0},{12,4},{1,9},{5,13},{9,1},{13,5},{2,10},{6,14},... | collective-permute-start | bytes 1572872 | tf_op jit(solution)/shard_map/ppermute | solution.py:121
  46.9 4.3 %collective-permute-start.5 = (bf16[1024,256]{1,0:T(8,128)(2,1)S(1)}, bf16[1024,256]{1,0:T(8,128)(2,1)S(1)}, u32[]{:S(2)}, u32[]{:S(2)}) collective-permute-start(bf16[1024,256]{1,0:T(8,128)(2,1)S(1)} %get-tuple-element.142), channel_id=1, source_target_pairs={{0,12},{4,0},{8,4},{12,8},{1,13},{5,1},{9,5},{13,9},{2,14},{6,2},{... | collective-permute-start | bytes 1572872 | tf_op jit(solution)/shard_map/ppermute | solution.py:121
  51.2 0.0 all-to-all-done.1
  51.3 1.9 %collective-permute-start.2 = (bf16[8,1792]{1,0:T(8,128)(2,1)S(1)}, bf16[8,1792]{1,0:T(8,128)(2,1)S(1)}, u32[]{:S(2)}, u32[]{:S(2)}) collective-permute-start(bf16[8,1792]{1,0:T(8,128)(2,1)S(1)} %reduce_sum.12), channel_id=1, source_target_pairs={{0,512},{512,0},{1,513},{513,1},{2,514},{514,2},{3,515},{515,3},{4... | collective-permute-start | bytes 86024 | tf_op jit(solution)/shard_map/ppermute | solution.py:130
  53.2 12.7 %collective-permute-done.2 = bf16[8,1792]{1,0:T(8,128)(2,1)S(1)} collective-permute-done((bf16[8,1792]{1,0:T(8,128)(2,1)S(1)}, bf16[8,1792]{1,0:T(8,128)(2,1)S(1)}, u32[]{:S(2)}, u32[]{:S(2)}) %collective-permute-start.2) | collective-permute-done | bytes 28704 | tf_op jit(solution)/shard_map/ppermute | solution.py:130
  65.9 0.0 collective-permute-done.3
  65.9 0.0 collective-permute-done.4
  66.0 4.7 %collective-permute-done.5 = bf16[1024,256]{1,0:T(8,128)(2,1)S(1)} collective-permute-done((bf16[1024,256]{1,0:T(8,128)(2,1)S(1)}, bf16[1024,256]{1,0:T(8,128)(2,1)S(1)}, u32[]{:S(2)}, u32[]{:S(2)}) %collective-permute-start.5) | collective-permute-done | bytes 524320 | tf_op jit(solution)/shard_map/ppermute | solution.py:121
  70.7 0.7 broadcast_in_dim.6
  71.4 9.9 %all-to-all-start.2 = ((bf16[8,8,1792]{2,1,0:T(8,128)(2,1)}), bf16[8,8,1792]{2,1,0:T(8,128)(2,1)S(1)}, u32[]{:S(2)}, u32[]{:S(2)}) async-start(bf16[8,8,1792]{2,1,0:T(8,128)(2,1)} %broadcast_in_dim.6), calls=%async_computation.2 | async-start | bytes 458752 | tf_op jit(solution)/shard_map/all_to_all | solution.py:91
  81.3 0.0 copy-start.3
  81.3 0.0 copy-start.4
  81.3 0.2 convert_add_fusion.1
  81.5 0.0 copy-start.2
  81.5 1.0 copy-done.2
  82.6 0.6 copy-done.3
  83.2 0.6 copy-done.4
  83.7 0.2 multiply_subtract_fusion
  84.0 12.4 %all-to-all-done.2 = bf16[8,8,1792]{2,1,0:T(8,128)(2,1)S(1)} async-done(((bf16[8,8,1792]{2,1,0:T(8,128)(2,1)}), bf16[8,8,1792]{2,1,0:T(8,128)(2,1)S(1)}, u32[]{:S(2)}, u32[]{:S(2)}) %all-to-all-start.2) | async-done | bytes 229408 | tf_op jit(solution)/shard_map/all_to_all | solution.py:91
  96.4 11.8 %collective-permute-start.6 = (bf16[1024,128]{1,0:T(8,128)(2,1)S(1)}, bf16[1024,128]{1,0:T(8,128)(2,1)S(1)}, u32[]{:S(2)}, u32[]{:S(2)}) collective-permute-start(bf16[1024,128]{1,0:T(8,128)(2,1)S(1)} %slice.44), channel_id=1, source_target_pairs={{0,2},{2,0},{1,3},{3,1},{4,6},{6,4},{5,7},{7,5},{8,10},{10,8},{9,1... | collective-permute-start | bytes 786440 | tf_op jit(solution)/shard_map/ppermute | solution.py:144
  108.2 1.0 broadcast_in_dim.7
  109.2 0.6 broadcast.19
  109.8 0.6 broadcast.19.clone
  110.5 0.0 slice-start
  110.5 16.2 %while.18 = (s32[]{:T(128)}, bf16[64,1792]{1,0:T(8,128)(2,1)S(1)}, bf16[256,1792]{1,0:T(8,128)(2,1)}, f32[4,1792]{1,0:T(4,128)}, f32[4,1792]{1,0:T(4,128)}, /*in...) while((s32[]{:T(128)}, bf16[64,1792]{1,0:T(8,128)(2,1)S(1)}, ...), condition=%wide.region_2.0_spmd, body=%wide.region_1.0_spmd.sunk | while | flops 1985538 | bytes 5404785 | solution.py:160
  110.5 14.4 %all_gather.6 = bf16[256,1792]{1,0:T(8,128)(2,1)S(1)} all-gather(bf16[64,1792]{1,0:T(8,128)(2,1)S(1)} %get-tuple-element.254), channel_id=1, replica_groups=mesh['zo'=2,'zi'=8,'x'=4,'y'=4,'h'=2,'c'=2] {'x'}, dimensions={0}, use_global_device_ids=true | all-gather | bytes 1146880 | tf_op jit(solution)/shard_map/while/body/all_gather | solution.py:152
  124.8 0.1 neg.11
  124.9 1.2 subtract_convert_fusion.2
  126.0 0.6 convert_add_fusion.6
  126.7 32.7 %collective-permute-done.6 = bf16[1024,128]{1,0:T(8,128)(2,1)S(1)} collective-permute-done((bf16[1024,128]{1,0:T(8,128)(2,1)S(1)}, bf16[1024,128]{1,0:T(8,128)(2,1)S(1)}, u32[]{:S(2)}, u32[]{:S(2)}) %collective-permute-start.6) | collective-permute-done | bytes 262176 | tf_op jit(solution)/shard_map/ppermute | solution.py:144
  159.4 0.0 slice-done
  159.4 0.8 add_convert_fusion
  (5 shorter events, 0.1 us)
Async XLA Ops:
  0.6 18.3 %all-to-all-start = ((bf16[4,64,1792]{2,1,0:T(8,128)(2,1)}), bf16[4,64,1792]{2,1,0:T(8,128)(2,1)}, u32[]{:S(2)}, u32[]{:S(2)}) async-start(bf16[4,64,1792]{2,1,0:T(8,128)(2,1)} %bitcast.27), calls=%async_computation | async-start | bytes 1835008 | tf_op jit(solution)/shard_map/all_to_all | solution.py:91
  4.9 16.2 %collective-permute-start = (bf16[1024,512]{1,0:T(8,128)(2,1)}, bf16[1024,512]{1,0:T(8,128)(2,1)}, u32[]{:S(2)}, u32[]{:S(2)}) collective-permute-start(bf16[1024,512]{1,0:T(8,128)(2,1)} %own_ref.1), channel_id=1, source_target_pairs={{0,1},{1,0},{2,3},{3,2},{4,5},{5,4},{6,7},{7,6},{8,9},{9,8},{10,11... | collective-permute-start | bytes 3145736 | tf_op jit(solution)/shard_map/ppermute | solution.py:113
  6.9 1.6 copy-start
  8.5 25.2 %copy-start.1 = (bf16[512,2048]{1,0:T(8,128)(2,1)S(1)}, bf16[512,2048]{1,0:T(8,128)(2,1)}, u32[]{:S(2)}) copy-start(bf16[512,2048]{1,0:T(8,128)(2,1)} %far_ref.3) | copy-start | bytes 6291460
  9.9 11.2 %collective-permute-start.1 = (bf16[512,1024]{1,0:T(8,128)(2,1)S(1)}, bf16[512,1024]{1,0:T(8,128)(2,1)}, u32[]{:S(2)}, u32[]{:S(2)}) collective-permute-start(bf16[512,1024]{1,0:T(8,128)(2,1)S(1)} %shard_map.84), channel_id=1, source_target_pairs={{0,1},{1,0},{2,3},{3,2},{4,5},{5,4},{6,7},{7,6},{8,9},{9,8},{10,11... | collective-permute-start | bytes 3145736 | tf_op jit(solution)/shard_map/ppermute | solution.py:114
  21.1 30.1 %all-to-all-start.1 = ((bf16[8,8,1792]{2,1,0:T(8,128)(2,1)}), bf16[8,8,1792]{2,1,0:T(8,128)(2,1)S(1)}, u32[]{:S(2)}, u32[]{:S(2)}) async-start(bf16[8,8,1792]{2,1,0:T(8,128)(2,1)} %bitcast.8), calls=%async_computation.1 | async-start | bytes 458752 | tf_op jit(solution)/shard_map/all_to_all | solution.py:91
  40.5 25.4 %collective-permute-start.3 = (bf16[1024,256]{1,0:T(8,128)(2,1)}, bf16[1024,256]{1,0:T(8,128)(2,1)S(1)}, u32[]{:S(2)}, u32[]{:S(2)}) collective-permute-start(bf16[1024,256]{1,0:T(8,128)(2,1)} %get-tuple-element.140), channel_id=1, source_target_pairs={{0,4},{4,8},{8,12},{12,0},{1,5},{5,9},{9,13},{13,1},{2,6},{6,10},{... | collective-permute-start | bytes 1572872 | tf_op jit(solution)/shard_map/ppermute | solution.py:121
  44.0 21.9 %collective-permute-start.4 = (bf16[1024,256]{1,0:T(8,128)(2,1)}, bf16[1024,256]{1,0:T(8,128)(2,1)S(1)}, u32[]{:S(2)}, u32[]{:S(2)}) collective-permute-start(bf16[1024,256]{1,0:T(8,128)(2,1)} %get-tuple-element.141), channel_id=1, source_target_pairs={{0,8},{4,12},{8,0},{12,4},{1,9},{5,13},{9,1},{13,5},{2,10},{6,14},... | collective-permute-start | bytes 1572872 | tf_op jit(solution)/shard_map/ppermute | solution.py:121
  46.9 23.8 %collective-permute-start.5 = (bf16[1024,256]{1,0:T(8,128)(2,1)S(1)}, bf16[1024,256]{1,0:T(8,128)(2,1)S(1)}, u32[]{:S(2)}, u32[]{:S(2)}) collective-permute-start(bf16[1024,256]{1,0:T(8,128)(2,1)S(1)} %get-tuple-element.142), channel_id=1, source_target_pairs={{0,12},{4,0},{8,4},{12,8},{1,13},{5,1},{9,5},{13,9},{2,14},{6,2},{... | collective-permute-start | bytes 1572872 | tf_op jit(solution)/shard_map/ppermute | solution.py:121
  51.3 14.7 %collective-permute-start.2 = (bf16[8,1792]{1,0:T(8,128)(2,1)S(1)}, bf16[8,1792]{1,0:T(8,128)(2,1)S(1)}, u32[]{:S(2)}, u32[]{:S(2)}) collective-permute-start(bf16[8,1792]{1,0:T(8,128)(2,1)S(1)} %reduce_sum.12), channel_id=1, source_target_pairs={{0,512},{512,0},{1,513},{513,1},{2,514},{514,2},{3,515},{515,3},{4... | collective-permute-start | bytes 86024 | tf_op jit(solution)/shard_map/ppermute | solution.py:130
  71.4 25.0 %all-to-all-start.2 = ((bf16[8,8,1792]{2,1,0:T(8,128)(2,1)}), bf16[8,8,1792]{2,1,0:T(8,128)(2,1)S(1)}, u32[]{:S(2)}, u32[]{:S(2)}) async-start(bf16[8,8,1792]{2,1,0:T(8,128)(2,1)} %broadcast_in_dim.6), calls=%async_computation.2 | async-start | bytes 458752 | tf_op jit(solution)/shard_map/all_to_all | solution.py:91
  81.3 1.9 %copy-start.3 = (f32[256,1792]{1,0:T(8,128)S(1)}, f32[256,1792]{1,0:T(8,128)}, u32[]{:S(2)}) copy-start(f32[256,1792]{1,0:T(8,128)} %param.8) | copy-start | bytes 5505028
  81.3 2.4 %copy-start.4 = (f32[256,1792]{1,0:T(8,128)S(1)}, f32[256,1792]{1,0:T(8,128)}, u32[]{:S(2)}) copy-start(f32[256,1792]{1,0:T(8,128)} %param.9) | copy-start | bytes 5505028
  81.5 1.0 copy-start.2
  96.4 63.0 %collective-permute-start.6 = (bf16[1024,128]{1,0:T(8,128)(2,1)S(1)}, bf16[1024,128]{1,0:T(8,128)(2,1)S(1)}, u32[]{:S(2)}, u32[]{:S(2)}) collective-permute-start(bf16[1024,128]{1,0:T(8,128)(2,1)S(1)} %slice.44), channel_id=1, source_target_pairs={{0,2},{2,0},{1,3},{3,1},{4,6},{6,4},{5,7},{7,5},{8,10},{10,8},{9,1... | collective-permute-start | bytes 786440 | tf_op jit(solution)/shard_map/ppermute | solution.py:144
  110.5 48.9 %slice-start = ((f32[1024,256]{1,0:T(8,128)}), f32[1024,128]{1,0:T(8,128)S(1)}, s32[]{:S(2)}) async-start(f32[1024,256]{1,0:T(8,128)} %copy-done.2), calls=%async_computation.3 | async-start | bytes 1048576 | tf_op jit(solution)/shard_map/slice | solution.py:142

commit v9 on v8

--- a/solution.py
+++ b/solution.py
@@ -132,31 +132,31 @@
         return jnp.broadcast_to(outer_grad, (n_zi, per_zi, width))
 
     outer_grad = outer(total)
-    outer_grad, base, momentum, *part = lax.optimization_barrier((outer_grad, base, momentum, *part))
-    gathered = exchange(outer_grad, "zi")
-
+    outer_grad, *part = lax.optimization_barrier((outer_grad, *part))
     kv = part[0].astype(f32)
     for piece in range(1, n_y):
         kv += part[piece].astype(f32)
-    without = base - 0.567 * momentum
-    mine, other, without = lax.optimization_barrier((kv[:, :LANES], kv[:, LANES:].astype(bf16), without))
-    gathered, other = lax.optimization_barrier((gathered, other))
+    mine, other = lax.optimization_barrier((kv[:, :LANES], kv[:, LANES:].astype(bf16)))
     there = lax.ppermute(other, "h", swap)
-    gathered = gathered.reshape(per_x, width)
     start = ((zo * n_zi + zi) * n_x + x) * own
 
     def own_rows(array):
         return lax.dynamic_slice_in_dim(array, start, own, 0).astype(f32)
 
-    def finish(gathered):
+    def finish(outer_grad):
+        outer_grad, old_base, old_momentum = lax.optimization_barrier((outer_grad, base, momentum))
+        gathered = exchange(outer_grad, "zi").reshape(per_x, width)
+        without = old_base - 0.567 * old_momentum
+        gathered, without = lax.optimization_barrier((gathered, without))
         outer_grad = lax.all_gather(gathered, "x", axis=0, tiled=True)
         synced = (without - 1.33 * outer_grad.astype(f32)).astype(bf16)
         new_base = own_rows(without) - 1.33 * own_rows(outer_grad)
-        new_momentum = 0.9 * own_rows(momentum) + own_rows(outer_grad)
+        new_momentum = 0.9 * own_rows(old_momentum) + own_rows(outer_grad)
         return synced, new_base, new_momentum
 
     empty = (jnp.zeros((rows, width), bf16), jnp.zeros((own, width), f32), jnp.zeros((own, width), f32))
-    carry = (gathered, *empty)
+    outer_grad = after(outer_grad, other)
+    carry = (outer_grad, *empty)
     carry = lax.fori_loop(0, once, lambda _, carry: (-carry[0], *finish(carry[0])), carry)
     synced, new_base, new_momentum = carry[1:]
     there = after(there, synced, new_base)

time: 161 us -> 169 us (1.050)
  the two profiles are of different devices: /device:TPU:296 before, /device:TPU:8 now
where the time goes in v9:
time: 169 us; the launch traced here: 168 us
  starting transfers between devices  78.6 us (47%)
  waiting for transfers between devices  52 us (31%)
  blocking collectives  14.4 us (9%)
  other arithmetic  9.26 us (5%)
  Pallas kernels  8.18 us (5%)
  local copies, waits for them, and re-layouts  4.58 us (3%)
    all_to_all x3, waiting for transfers between devices, exchange(): return lax.all_to_all(array, axis, split_axis=0, concat_axis=0, tiled=True)  48.1 us
    all_to_all x3, starting transfers between devices, exchange(): return lax.all_to_all(array, axis, split_axis=0, concat_axis=0, tiled=True)  26.5 us
    ppermute x1, starting transfers between devices, shards(): there = lax.ppermute(other, 'h', swap)  21.5 us
    ppermute x1, starting transfers between devices, outer(): across = lax.ppermute(total, 'zo', swap)  15.7 us
    all_gather x1, blocking collectives, finish(): outer_grad = lax.all_gather(gathered, 'x', axis=0, tiled=True)  14.4 us
    ppermute x3, starting transfers between devices, shards(): lax.ppermute(part[step], 'y', shift('y', n_y, step))  10.6 us
    pallas_call x1, Pallas kernels, project(): pl.pallas_call(project_kernel, out_shape=[jax.ShapeDtypeStruct((rows, 2 *...  6.81 us
  transfers between devices with their start and end apart: 10, of which 4 were waited for; matrix products, arithmetic and copies ran while one was open for 7% of the time, Pallas kernels for 5%

profile of v9, /device:TPU:8, one launch (start us, length us, event | category | flops | bytes accessed | tf_op | source)
XLA Modules:
  0.0 167.9 jit_solution(7199956115879532447)
XLA Ops:
  0.6 4.3 %all-to-all-start.1 = ((bf16[4,64,1792]{2,1,0:T(8,128)(2,1)}), bf16[4,64,1792]{2,1,0:T(8,128)(2,1)}, u32[]{:S(2)}, u32[]{:S(2)}) async-start(bf16[4,64,1792]{2,1,0:T(8,128)(2,1)} %bitcast.29), calls=%async_computation.1 | async-start | bytes 1835008 | tf_op jit(solution)/shard_map/all_to_all | solution.py:91
  4.9 0.1 pad_add_fusion.place_ref
  5.0 0.0 copy-start
  5.0 1.6 copy-done
  6.6 0.0 copy-start.1
  6.6 1.4 shard_map.84
  8.0 1.9 %collective-permute-start.1 = (bf16[512,1024]{1,0:T(8,128)(2,1)S(1)}, bf16[512,1024]{1,0:T(8,128)(2,1)}, u32[]{:S(2)}, u32[]{:S(2)}) collective-permute-start(bf16[512,1024]{1,0:T(8,128)(2,1)S(1)} %shard_map.84), channel_id=1, source_target_pairs={{0,1},{1,0},{2,3},{3,2},{4,5},{5,4},{6,7},{7,6},{8,9},{9,8},{10,11... | collective-permute-start | bytes 3145736 | tf_op jit(solution)/shard_map/ppermute | solution.py:114
  9.9 2.4 %collective-permute-start = (bf16[1024,512]{1,0:T(8,128)(2,1)}, bf16[1024,512]{1,0:T(8,128)(2,1)}, u32[]{:S(2)}, u32[]{:S(2)}) collective-permute-start(bf16[1024,512]{1,0:T(8,128)(2,1)} %own_ref.1), channel_id=1, source_target_pairs={{0,1},{1,0},{2,3},{3,2},{4,5},{5,4},{6,7},{7,6},{8,9},{9,8},{10,11... | collective-permute-start | bytes 3145736 | tf_op jit(solution)/shard_map/ppermute | solution.py:113
  12.3 6.6 %all-to-all-done.1 = bf16[4,64,1792]{2,1,0:T(8,128)(2,1)} async-done(((bf16[4,64,1792]{2,1,0:T(8,128)(2,1)}), bf16[4,64,1792]{2,1,0:T(8,128)(2,1)}, u32[]{:S(2)}, u32[]{:S(2)}) %all-to-all-start.1) | async-done | bytes 917536 | tf_op jit(solution)/shard_map/all_to_all | solution.py:91
  18.9 2.2 %fusion.1 = bf16[64,1792]{1,0:T(8,128)(2,1)} fusion(f32[256,1792]{1,0:T(8,128)} %param.8, s32[]{:T(128)S(6)} %select_n.11, bf16[4,64,1792]{2,1,0:T(8,128)(2,1)} %all-to-all-done.1), kind=kLoop, calls=%fused_computation.9 | loop fusion | flops 1261568 | bytes 1376260 | tf_op jit(solution)/shard_map/convert_element_type | solution.py:110
  21.1 0.0 collective-permute-done.1.packed_ref
  21.1 0.0 collective-permute-done.sibling_ref
  21.1 12.5 %all-to-all-start.2 = ((bf16[8,8,1792]{2,1,0:T(8,128)(2,1)}), bf16[8,8,1792]{2,1,0:T(8,128)(2,1)S(1)}, u32[]{:S(2)}, u32[]{:S(2)}) async-start(bf16[8,8,1792]{2,1,0:T(8,128)(2,1)} %bitcast.9), calls=%async_computation.2 | async-start | bytes 458752 | tf_op jit(solution)/shard_map/all_to_all | solution.py:91
  33.6 0.0 copy-done.1
  33.7 6.8 %shard_map.85 = (bf16[1024,256]{1,0:T(8,128)(2,1)S(1)}, bf16[1024,256]{1,0:T(8,128)(2,1)}, bf16[1024,256]{1,0:T(8,128)(2,1)}, bf16[1024,256]{1,0:T(8,128)(2,1)S(1)}) custom-call(s32[3]{0:T(128)S(1)} %pad_add_fusion.place_ref, bf16[1024,512]{1,0:T(8,128)(2,1)} %own_ref.1, bf16[1024,512]{1,0:T(8,128)(2,1)} %collective-permute-done.sibling_ref, ...), custom_call_target="tpu_custom_call" | custom-call | flops 2147483648 | bytes 6291456 | tf_op jit(solution)/shard_map/pallas_call | solution.py:60
  40.5 3.5 %collective-permute-start.3 = (bf16[1024,256]{1,0:T(8,128)(2,1)}, bf16[1024,256]{1,0:T(8,128)(2,1)S(1)}, u32[]{:S(2)}, u32[]{:S(2)}) collective-permute-start(bf16[1024,256]{1,0:T(8,128)(2,1)} %get-tuple-element.133), channel_id=1, source_target_pairs={{0,4},{4,8},{8,12},{12,0},{1,5},{5,9},{9,13},{13,1},{2,6},{6,10},{... | collective-permute-start | bytes 1572872 | tf_op jit(solution)/shard_map/ppermute | solution.py:121
  43.9 2.8 %collective-permute-start.4 = (bf16[1024,256]{1,0:T(8,128)(2,1)}, bf16[1024,256]{1,0:T(8,128)(2,1)S(1)}, u32[]{:S(2)}, u32[]{:S(2)}) collective-permute-start(bf16[1024,256]{1,0:T(8,128)(2,1)} %get-tuple-element.134), channel_id=1, source_target_pairs={{0,8},{4,12},{8,0},{12,4},{1,9},{5,13},{9,1},{13,5},{2,10},{6,14},... | collective-permute-start | bytes 1572872 | tf_op jit(solution)/shard_map/ppermute | solution.py:121
  46.8 4.3 %collective-permute-start.5 = (bf16[1024,256]{1,0:T(8,128)(2,1)S(1)}, bf16[1024,256]{1,0:T(8,128)(2,1)S(1)}, u32[]{:S(2)}, u32[]{:S(2)}) collective-permute-start(bf16[1024,256]{1,0:T(8,128)(2,1)S(1)} %get-tuple-element.135), channel_id=1, source_target_pairs={{0,12},{4,0},{8,4},{12,8},{1,13},{5,1},{9,5},{13,9},{2,14},{6,2},{... | collective-permute-start | bytes 1572872 | tf_op jit(solution)/shard_map/ppermute | solution.py:121
  51.1 0.0 all-to-all-done.2
  51.2 15.7 %collective-permute-start.2 = (bf16[8,1792]{1,0:T(8,128)(2,1)S(1)}, bf16[8,1792]{1,0:T(8,128)(2,1)S(1)}, u32[]{:S(2)}, u32[]{:S(2)}) collective-permute-start(bf16[8,1792]{1,0:T(8,128)(2,1)S(1)} %reduce_sum.12), channel_id=1, source_target_pairs={{0,512},{512,0},{1,513},{513,1},{2,514},{514,2},{3,515},{515,3},{4... | collective-permute-start | bytes 86024 | tf_op jit(solution)/shard_map/ppermute | solution.py:130
  66.9 2.1 %collective-permute-done.2 = bf16[8,1792]{1,0:T(8,128)(2,1)S(1)} collective-permute-done((bf16[8,1792]{1,0:T(8,128)(2,1)S(1)}, bf16[8,1792]{1,0:T(8,128)(2,1)S(1)}, u32[]{:S(2)}, u32[]{:S(2)}) %collective-permute-start.2) | collective-permute-done | bytes 28704 | tf_op jit(solution)/shard_map/ppermute | solution.py:130
  69.1 0.0 collective-permute-done.3
  69.1 0.0 collective-permute-done.4
  69.1 1.8 %collective-permute-done.5 = bf16[1024,256]{1,0:T(8,128)(2,1)S(1)} collective-permute-done((bf16[1024,256]{1,0:T(8,128)(2,1)S(1)}, bf16[1024,256]{1,0:T(8,128)(2,1)S(1)}, u32[]{:S(2)}, u32[]{:S(2)}) %collective-permute-start.5) | collective-permute-done | bytes 524320 | tf_op jit(solution)/shard_map/ppermute | solution.py:121
  70.9 0.2 convert_add_fusion.1
  71.2 21.5 %collective-permute-start.6 = (bf16[1024,128]{1,0:T(8,128)(2,1)S(1)}, bf16[1024,128]{1,0:T(8,128)(2,1)S(1)}, u32[]{:S(2)}, u32[]{:S(2)}) collective-permute-start(bf16[1024,128]{1,0:T(8,128)(2,1)S(1)} %slice.44), channel_id=1, source_target_pairs={{0,2},{2,0},{1,3},{3,1},{4,6},{6,4},{5,7},{7,5},{8,10},{10,8},{9,1... | collective-permute-start | bytes 786440 | tf_op jit(solution)/shard_map/ppermute | solution.py:140
  92.7 1.0 broadcast_in_dim.7
  93.7 0.6 broadcast.24
  94.3 0.6 broadcast.24.clone
  94.9 72.2 %while.18 = (s32[]{:T(128)}, bf16[8,8,1792]{2,1,0:T(8,128)(2,1)S(1)}, bf16[256,1792]{1,0:T(8,128)(2,1)}, f32[4,1792]{1,0:T(4,128)}, f32[4,1792]{1,0:T(4,128)}, /...) while((s32[]{:T(128)}, bf16[8,8,1792]{2,1,0:T(8,128)(2,1)S(1)}, ...), condition=%wide.region_2.0_spmd, body=%wide.region_1.0_spmd.sunk | while | flops 2903042 | bytes 12056713 | solution.py:160
  94.9 0.7 copy.15
  95.6 9.6 %all-to-all-start = ((bf16[8,8,1792]{2,1,0:T(8,128)(2,1)}), bf16[8,8,1792]{2,1,0:T(8,128)(2,1)S(1)}, u32[]{:S(2)}, u32[]{:S(2)}) async-start(bf16[8,8,1792]{2,1,0:T(8,128)(2,1)} %copy.15), calls=%async_computation | async-start | bytes 458752 | tf_op jit(solution)/shard_map/while/body/all_to_all | solution.py:91
  105.2 1.0 neg.11
  106.2 2.3 %multiply_subtract_fusion.2 = f32[256,1792]{1,0:T(8,128)S(1)} fusion(f32[256,1792]{1,0:T(8,128)} %get-tuple-element.227, f32[256,1792]{1,0:T(8,128)} %get-tuple-element.228), kind=kLoop, calls=%fused_computation.1.clone.1 | loop fusion | flops 917504 | bytes 5505024 | tf_op jit(solution)/shard_map/while/body/sub | solution.py:149
  108.5 41.5 %all-to-all-done = bf16[8,8,1792]{2,1,0:T(8,128)(2,1)S(1)} async-done(((bf16[8,8,1792]{2,1,0:T(8,128)(2,1)}), bf16[8,8,1792]{2,1,0:T(8,128)(2,1)S(1)}, u32[]{:S(2)}, u32[]{:S(2)}) %all-to-all-start) | async-done | bytes 229408 | tf_op jit(solution)/shard_map/while/body/all_to_all | solution.py:91
  150.1 14.4 %all_gather.6 = bf16[256,1792]{1,0:T(8,128)(2,1)S(1)} all-gather(bf16[64,1792]{1,0:T(8,128)(2,1)S(1)} %bitcast.28), channel_id=1, replica_groups=mesh['zo'=2,'zi'=8,'x'=4,'y'=4,'h'=2,'c'=2] {'x'}, dimensions={0}, use_global_device_ids=true | all-gather | bytes 1146880 | tf_op jit(solution)/shard_map/while/body/all_gather | solution.py:151
  164.5 1.2 subtract_convert_fusion.2
  165.7 1.5 convert_add_fusion.6
  167.1 0.0 collective-permute-done.6
  167.1 0.8 add_convert_fusion
  (5 shorter events, 0.1 us)
Async XLA Ops:
  0.6 18.3 %all-to-all-start.1 = ((bf16[4,64,1792]{2,1,0:T(8,128)(2,1)}), bf16[4,64,1792]{2,1,0:T(8,128)(2,1)}, u32[]{:S(2)}, u32[]{:S(2)}) async-start(bf16[4,64,1792]{2,1,0:T(8,128)(2,1)} %bitcast.29), calls=%async_computation.1 | async-start | bytes 1835008 | tf_op jit(solution)/shard_map/all_to_all | solution.py:91
  5.0 1.6 copy-start
  6.6 27.0 %copy-start.1 = (bf16[512,2048]{1,0:T(8,128)(2,1)S(1)}, bf16[512,2048]{1,0:T(8,128)(2,1)}, u32[]{:S(2)}) copy-start(bf16[512,2048]{1,0:T(8,128)(2,1)} %far_ref.3) | copy-start | bytes 6291460
  8.0 13.1 %collective-permute-start.1 = (bf16[512,1024]{1,0:T(8,128)(2,1)S(1)}, bf16[512,1024]{1,0:T(8,128)(2,1)}, u32[]{:S(2)}, u32[]{:S(2)}) collective-permute-start(bf16[512,1024]{1,0:T(8,128)(2,1)S(1)} %shard_map.84), channel_id=1, source_target_pairs={{0,1},{1,0},{2,3},{3,2},{4,5},{5,4},{6,7},{7,6},{8,9},{9,8},{10,11... | collective-permute-start | bytes 3145736 | tf_op jit(solution)/shard_map/ppermute | solution.py:114
  9.9 11.2 %collective-permute-start = (bf16[1024,512]{1,0:T(8,128)(2,1)}, bf16[1024,512]{1,0:T(8,128)(2,1)}, u32[]{:S(2)}, u32[]{:S(2)}) collective-permute-start(bf16[1024,512]{1,0:T(8,128)(2,1)} %own_ref.1), channel_id=1, source_target_pairs={{0,1},{1,0},{2,3},{3,2},{4,5},{5,4},{6,7},{7,6},{8,9},{9,8},{10,11... | collective-permute-start | bytes 3145736 | tf_op jit(solution)/shard_map/ppermute | solution.py:113
  21.1 30.0 %all-to-all-start.2 = ((bf16[8,8,1792]{2,1,0:T(8,128)(2,1)}), bf16[8,8,1792]{2,1,0:T(8,128)(2,1)S(1)}, u32[]{:S(2)}, u32[]{:S(2)}) async-start(bf16[8,8,1792]{2,1,0:T(8,128)(2,1)} %bitcast.9), calls=%async_computation.2 | async-start | bytes 458752 | tf_op jit(solution)/shard_map/all_to_all | solution.py:91
  40.5 28.6 %collective-permute-start.3 = (bf16[1024,256]{1,0:T(8,128)(2,1)}, bf16[1024,256]{1,0:T(8,128)(2,1)S(1)}, u32[]{:S(2)}, u32[]{:S(2)}) collective-permute-start(bf16[1024,256]{1,0:T(8,128)(2,1)} %get-tuple-element.133), channel_id=1, source_target_pairs={{0,4},{4,8},{8,12},{12,0},{1,5},{5,9},{9,13},{13,1},{2,6},{6,10},{... | collective-permute-start | bytes 1572872 | tf_op jit(solution)/shard_map/ppermute | solution.py:121
  43.9 25.1 %collective-permute-start.4 = (bf16[1024,256]{1,0:T(8,128)(2,1)}, bf16[1024,256]{1,0:T(8,128)(2,1)S(1)}, u32[]{:S(2)}, u32[]{:S(2)}) collective-permute-start(bf16[1024,256]{1,0:T(8,128)(2,1)} %get-tuple-element.134), channel_id=1, source_target_pairs={{0,8},{4,12},{8,0},{12,4},{1,9},{5,13},{9,1},{13,5},{2,10},{6,14},... | collective-permute-start | bytes 1572872 | tf_op jit(solution)/shard_map/ppermute | solution.py:121
  46.8 24.1 %collective-permute-start.5 = (bf16[1024,256]{1,0:T(8,128)(2,1)S(1)}, bf16[1024,256]{1,0:T(8,128)(2,1)S(1)}, u32[]{:S(2)}, u32[]{:S(2)}) collective-permute-start(bf16[1024,256]{1,0:T(8,128)(2,1)S(1)} %get-tuple-element.135), channel_id=1, source_target_pairs={{0,12},{4,0},{8,4},{12,8},{1,13},{5,1},{9,5},{13,9},{2,14},{6,2},{... | collective-permute-start | bytes 1572872 | tf_op jit(solution)/shard_map/ppermute | solution.py:121
  51.2 17.9 %collective-permute-start.2 = (bf16[8,1792]{1,0:T(8,128)(2,1)S(1)}, bf16[8,1792]{1,0:T(8,128)(2,1)S(1)}, u32[]{:S(2)}, u32[]{:S(2)}) collective-permute-start(bf16[8,1792]{1,0:T(8,128)(2,1)S(1)} %reduce_sum.12), channel_id=1, source_target_pairs={{0,512},{512,0},{1,513},{513,1},{2,514},{514,2},{3,515},{515,3},{4... | collective-permute-start | bytes 86024 | tf_op jit(solution)/shard_map/ppermute | solution.py:130
  71.2 95.9 %collective-permute-start.6 = (bf16[1024,128]{1,0:T(8,128)(2,1)S(1)}, bf16[1024,128]{1,0:T(8,128)(2,1)S(1)}, u32[]{:S(2)}, u32[]{:S(2)}) collective-permute-start(bf16[1024,128]{1,0:T(8,128)(2,1)S(1)} %slice.44), channel_id=1, source_target_pairs={{0,2},{2,0},{1,3},{3,1},{4,6},{6,4},{5,7},{7,5},{8,10},{10,8},{9,1... | collective-permute-start | bytes 786440 | tf_op jit(solution)/shard_map/ppermute | solution.py:140
  95.6 54.4 %all-to-all-start = ((bf16[8,8,1792]{2,1,0:T(8,128)(2,1)}), bf16[8,8,1792]{2,1,0:T(8,128)(2,1)S(1)}, u32[]{:S(2)}, u32[]{:S(2)}) async-start(bf16[8,8,1792]{2,1,0:T(8,128)(2,1)} %copy.15), calls=%async_computation | async-start | bytes 458752 | tf_op jit(solution)/shard_map/while/body/all_to_all | solution.py:91

commit v10 on v8

--- a/solution.py
+++ b/solution.py
@@ -44,14 +44,18 @@
 
 def project_kernel(place_ref, own_ref, sibling_ref, near_ref, far_ref, packed_ref, *out_refs):
     mine = jnp.concatenate([near_ref[...], far_ref[...]], axis=1)
-    total = jnp.dot(own_ref[...], mine, preferred_element_type=f32)
-    total += jnp.dot(sibling_ref[...], packed_ref[...], preferred_element_type=f32)
-    total = total.astype(bf16)
+    lacked = packed_ref[...]
+    rows = own_ref.shape[0]
+    tile = min(rows, 256)
     for step, out_ref in enumerate(out_refs):
 
         @pl.when(pl.program_id(0) == step)
         def _(out_ref=out_ref):
-            out_ref[...] = total
+            for start in range(0, rows, tile):
+                at = slice(start, start + tile)
+                total = jnp.dot(own_ref[at, :], mine, preferred_element_type=f32)
+                total += jnp.dot(sibling_ref[at, :], lacked, preferred_element_type=f32)
+                out_ref[at, :] = total.astype(bf16)
 
 
 def project(place, own, sibling, weight, packed, n_y):

time: 161 us -> 161 us (level)
  no operation moved by 1% of the time
where the time goes in v10:
time: 161 us; the launch traced here: 160 us
  waiting for transfers between devices  69.1 us (43%)
  starting transfers between devices  55.6 us (35%)
  blocking collectives  14.4 us (9%)
  Pallas kernels  8.12 us (5%)
  local copies, waits for them, and re-layouts  6.72 us (4%)
  other arithmetic  5.42 us (3%)
    ppermute x1, waiting for transfers between devices, shards(): there = lax.ppermute(other, 'h', swap)  32.7 us
    all_to_all x3, starting transfers between devices, exchange(): return lax.all_to_all(array, axis, split_axis=0, concat_axis=0, tiled=True)  26.8 us
    all_to_all x3, waiting for transfers between devices, exchange(): return lax.all_to_all(array, axis, split_axis=0, concat_axis=0, tiled=True)  19 us
    all_gather x1, blocking collectives, finish(): outer_grad = lax.all_gather(gathered, 'x', axis=0, tiled=True)  14.4 us
    ppermute x1, waiting for transfers between devices, outer(): across = lax.ppermute(total, 'zo', swap)  12.7 us
    ppermute x1, starting transfers between devices, shards(): there = lax.ppermute(other, 'h', swap)  11.8 us
    ppermute x3, starting transfers between devices, shards(): lax.ppermute(part[step], 'y', shift('y', n_y, step))  10.6 us
    pallas_call x1, Pallas kernels, project(): pl.pallas_call(project_kernel, out_shape=[jax.ShapeDtypeStruct((rows, 2 *...  6.76 us
  transfers between devices with their start and end apart: 10, of which 5 were waited for; matrix products, arithmetic and copies ran while one was open for 4% of the time, Pallas kernels for 5%

profile of v10, /device:TPU:296, one launch (start us, length us, event | category | flops | bytes accessed | tf_op | source)
XLA Modules:
  0.0 160.1 jit_solution(1861298994861201952)
XLA Ops:
  0.6 4.3 %all-to-all-start = ((bf16[4,64,1792]{2,1,0:T(8,128)(2,1)}), bf16[4,64,1792]{2,1,0:T(8,128)(2,1)}, u32[]{:S(2)}, u32[]{:S(2)}) async-start(bf16[4,64,1792]{2,1,0:T(8,128)(2,1)} %bitcast.27), calls=%async_computation | async-start | bytes 1835008 | tf_op jit(solution)/shard_map/all_to_all | solution.py:95
  4.9 1.9 %collective-permute-start = (bf16[1024,512]{1,0:T(8,128)(2,1)}, bf16[1024,512]{1,0:T(8,128)(2,1)}, u32[]{:S(2)}, u32[]{:S(2)}) collective-permute-start(bf16[1024,512]{1,0:T(8,128)(2,1)} %own_ref.1), channel_id=1, source_target_pairs={{0,1},{1,0},{2,3},{3,2},{4,5},{5,4},{6,7},{7,6},{8,9},{9,8},{10,11... | collective-permute-start | bytes 3145736 | tf_op jit(solution)/shard_map/ppermute | solution.py:117
  6.9 0.1 pad_add_fusion.place_ref
  6.9 0.0 copy-start
  6.9 1.6 copy-done
  8.5 0.0 copy-start.1
  8.5 1.4 shard_map.84
  9.9 2.4 %collective-permute-start.1 = (bf16[512,1024]{1,0:T(8,128)(2,1)S(1)}, bf16[512,1024]{1,0:T(8,128)(2,1)}, u32[]{:S(2)}, u32[]{:S(2)}) collective-permute-start(bf16[512,1024]{1,0:T(8,128)(2,1)S(1)} %shard_map.84), channel_id=1, source_target_pairs={{0,1},{1,0},{2,3},{3,2},{4,5},{5,4},{6,7},{7,6},{8,9},{9,8},{10,11... | collective-permute-start | bytes 3145736 | tf_op jit(solution)/shard_map/ppermute | solution.py:118
  12.3 6.6 %all-to-all-done = bf16[4,64,1792]{2,1,0:T(8,128)(2,1)} async-done(((bf16[4,64,1792]{2,1,0:T(8,128)(2,1)}), bf16[4,64,1792]{2,1,0:T(8,128)(2,1)}, u32[]{:S(2)}, u32[]{:S(2)}) %all-to-all-start) | async-done | bytes 917536 | tf_op jit(solution)/shard_map/all_to_all | solution.py:95
  18.9 2.2 %fusion.1 = bf16[64,1792]{1,0:T(8,128)(2,1)} fusion(f32[256,1792]{1,0:T(8,128)} %param.8, s32[]{:T(128)S(6)} %select_n.11, bf16[4,64,1792]{2,1,0:T(8,128)(2,1)} %all-to-all-done), kind=kLoop, calls=%fused_computation.9 | loop fusion | flops 1261568 | bytes 1376260 | tf_op jit(solution)/shard_map/convert_element_type | solution.py:114
  21.1 0.0 collective-permute-done.sibling_ref
  21.1 0.0 collective-permute-done.1.packed_ref
  21.1 12.6 %all-to-all-start.1 = ((bf16[8,8,1792]{2,1,0:T(8,128)(2,1)}), bf16[8,8,1792]{2,1,0:T(8,128)(2,1)S(1)}, u32[]{:S(2)}, u32[]{:S(2)}) async-start(bf16[8,8,1792]{2,1,0:T(8,128)(2,1)} %bitcast.8), calls=%async_computation.1 | async-start | bytes 458752 | tf_op jit(solution)/shard_map/all_to_all | solution.py:95
  33.7 0.0 copy-done.1
  33.7 6.8 %shard_map.85 = (bf16[1024,256]{1,0:T(8,128)(2,1)S(1)}, bf16[1024,256]{1,0:T(8,128)(2,1)}, bf16[1024,256]{1,0:T(8,128)(2,1)}, bf16[1024,256]{1,0:T(8,128)(2,1)S(1)}) custom-call(s32[3]{0:T(128)S(1)} %pad_add_fusion.place_ref, bf16[1024,512]{1,0:T(8,128)(2,1)} %own_ref.1, bf16[1024,512]{1,0:T(8,128)(2,1)} %collective-permute-done.sibling_ref, ...), custom_call_target="tpu_custom_call" | custom-call | flops 2147483648 | bytes 6291456 | tf_op jit(solution)/shard_map/pallas_call | solution.py:64
  40.5 3.5 %collective-permute-start.3 = (bf16[1024,256]{1,0:T(8,128)(2,1)}, bf16[1024,256]{1,0:T(8,128)(2,1)S(1)}, u32[]{:S(2)}, u32[]{:S(2)}) collective-permute-start(bf16[1024,256]{1,0:T(8,128)(2,1)} %get-tuple-element.140), channel_id=1, source_target_pairs={{0,4},{4,8},{8,12},{12,0},{1,5},{5,9},{9,13},{13,1},{2,6},{6,10},{... | collective-permute-start | bytes 1572872 | tf_op jit(solution)/shard_map/ppermute | solution.py:125
  44.0 2.8 %collective-permute-start.4 = (bf16[1024,256]{1,0:T(8,128)(2,1)}, bf16[1024,256]{1,0:T(8,128)(2,1)S(1)}, u32[]{:S(2)}, u32[]{:S(2)}) collective-permute-start(bf16[1024,256]{1,0:T(8,128)(2,1)} %get-tuple-element.141), channel_id=1, source_target_pairs={{0,8},{4,12},{8,0},{12,4},{1,9},{5,13},{9,1},{13,5},{2,10},{6,14},... | collective-permute-start | bytes 1572872 | tf_op jit(solution)/shard_map/ppermute | solution.py:125
  46.8 4.3 %collective-permute-start.5 = (bf16[1024,256]{1,0:T(8,128)(2,1)S(1)}, bf16[1024,256]{1,0:T(8,128)(2,1)S(1)}, u32[]{:S(2)}, u32[]{:S(2)}) collective-permute-start(bf16[1024,256]{1,0:T(8,128)(2,1)S(1)} %get-tuple-element.142), channel_id=1, source_target_pairs={{0,12},{4,0},{8,4},{12,8},{1,13},{5,1},{9,5},{13,9},{2,14},{6,2},{... | collective-permute-start | bytes 1572872 | tf_op jit(solution)/shard_map/ppermute | solution.py:125
  51.2 0.0 all-to-all-done.1
  51.2 1.9 %collective-permute-start.2 = (bf16[8,1792]{1,0:T(8,128)(2,1)S(1)}, bf16[8,1792]{1,0:T(8,128)(2,1)S(1)}, u32[]{:S(2)}, u32[]{:S(2)}) collective-permute-start(bf16[8,1792]{1,0:T(8,128)(2,1)S(1)} %reduce_sum.12), channel_id=1, source_target_pairs={{0,512},{512,0},{1,513},{513,1},{2,514},{514,2},{3,515},{515,3},{4... | collective-permute-start | bytes 86024 | tf_op jit(solution)/shard_map/ppermute | solution.py:134
  53.1 12.7 %collective-permute-done.2 = bf16[8,1792]{1,0:T(8,128)(2,1)S(1)} collective-permute-done((bf16[8,1792]{1,0:T(8,128)(2,1)S(1)}, bf16[8,1792]{1,0:T(8,128)(2,1)S(1)}, u32[]{:S(2)}, u32[]{:S(2)}) %collective-permute-start.2) | collective-permute-done | bytes 28704 | tf_op jit(solution)/shard_map/ppermute | solution.py:134
  65.9 0.0 collective-permute-done.3
  65.9 0.0 collective-permute-done.4
  65.9 4.7 %collective-permute-done.5 = bf16[1024,256]{1,0:T(8,128)(2,1)S(1)} collective-permute-done((bf16[1024,256]{1,0:T(8,128)(2,1)S(1)}, bf16[1024,256]{1,0:T(8,128)(2,1)S(1)}, u32[]{:S(2)}, u32[]{:S(2)}) %collective-permute-start.5) | collective-permute-done | bytes 524320 | tf_op jit(solution)/shard_map/ppermute | solution.py:125
  70.6 0.7 broadcast_in_dim.6
  71.3 9.9 %all-to-all-start.2 = ((bf16[8,8,1792]{2,1,0:T(8,128)(2,1)}), bf16[8,8,1792]{2,1,0:T(8,128)(2,1)S(1)}, u32[]{:S(2)}, u32[]{:S(2)}) async-start(bf16[8,8,1792]{2,1,0:T(8,128)(2,1)} %broadcast_in_dim.6), calls=%async_computation.2 | async-start | bytes 458752 | tf_op jit(solution)/shard_map/all_to_all | solution.py:95
  81.3 0.0 copy-start.3
  81.3 0.0 copy-start.4
  81.3 0.2 convert_add_fusion.1
  81.5 0.0 copy-start.2
  81.5 1.0 copy-done.2
  82.5 0.6 copy-done.3
  83.1 0.6 copy-done.4
  83.7 0.2 multiply_subtract_fusion
  84.0 12.4 %all-to-all-done.2 = bf16[8,8,1792]{2,1,0:T(8,128)(2,1)S(1)} async-done(((bf16[8,8,1792]{2,1,0:T(8,128)(2,1)}), bf16[8,8,1792]{2,1,0:T(8,128)(2,1)S(1)}, u32[]{:S(2)}, u32[]{:S(2)}) %all-to-all-start.2) | async-done | bytes 229408 | tf_op jit(solution)/shard_map/all_to_all | solution.py:95
  96.4 11.8 %collective-permute-start.6 = (bf16[1024,128]{1,0:T(8,128)(2,1)S(1)}, bf16[1024,128]{1,0:T(8,128)(2,1)S(1)}, u32[]{:S(2)}, u32[]{:S(2)}) collective-permute-start(bf16[1024,128]{1,0:T(8,128)(2,1)S(1)} %slice.44), channel_id=1, source_target_pairs={{0,2},{2,0},{1,3},{3,1},{4,6},{6,4},{5,7},{7,5},{8,10},{10,8},{9,1... | collective-permute-start | bytes 786440 | tf_op jit(solution)/shard_map/ppermute | solution.py:148
  108.2 1.0 broadcast_in_dim.7
  109.2 0.6 broadcast.19
  109.8 0.6 broadcast.19.clone
  110.4 0.0 slice-start
  110.4 16.2 %while.18 = (s32[]{:T(128)}, bf16[64,1792]{1,0:T(8,128)(2,1)S(1)}, bf16[256,1792]{1,0:T(8,128)(2,1)}, f32[4,1792]{1,0:T(4,128)}, f32[4,1792]{1,0:T(4,128)}, /*in...) while((s32[]{:T(128)}, bf16[64,1792]{1,0:T(8,128)(2,1)S(1)}, ...), condition=%wide.region_2.0_spmd, body=%wide.region_1.0_spmd.sunk | while | flops 1985538 | bytes 5404785 | solution.py:164
  110.4 14.4 %all_gather.6 = bf16[256,1792]{1,0:T(8,128)(2,1)S(1)} all-gather(bf16[64,1792]{1,0:T(8,128)(2,1)S(1)} %get-tuple-element.254), channel_id=1, replica_groups=mesh['zo'=2,'zi'=8,'x'=4,'y'=4,'h'=2,'c'=2] {'x'}, dimensions={0}, use_global_device_ids=true | all-gather | bytes 1146880 | tf_op jit(solution)/shard_map/while/body/all_gather | solution.py:156
  124.8 0.1 neg.11
  124.8 1.2 subtract_convert_fusion.2
  126.0 0.6 convert_add_fusion.6
  126.7 32.7 %collective-permute-done.6 = bf16[1024,128]{1,0:T(8,128)(2,1)S(1)} collective-permute-done((bf16[1024,128]{1,0:T(8,128)(2,1)S(1)}, bf16[1024,128]{1,0:T(8,128)(2,1)S(1)}, u32[]{:S(2)}, u32[]{:S(2)}) %collective-permute-start.6) | collective-permute-done | bytes 262176 | tf_op jit(solution)/shard_map/ppermute | solution.py:148
  159.4 0.0 slice-done
  159.4 0.8 add_convert_fusion
  (5 shorter events, 0.1 us)
Async XLA Ops:
  0.6 18.3 %all-to-all-start = ((bf16[4,64,1792]{2,1,0:T(8,128)(2,1)}), bf16[4,64,1792]{2,1,0:T(8,128)(2,1)}, u32[]{:S(2)}, u32[]{:S(2)}) async-start(bf16[4,64,1792]{2,1,0:T(8,128)(2,1)} %bitcast.27), calls=%async_computation | async-start | bytes 1835008 | tf_op jit(solution)/shard_map/all_to_all | solution.py:95
  4.9 16.2 %collective-permute-start = (bf16[1024,512]{1,0:T(8,128)(2,1)}, bf16[1024,512]{1,0:T(8,128)(2,1)}, u32[]{:S(2)}, u32[]{:S(2)}) collective-permute-start(bf16[1024,512]{1,0:T(8,128)(2,1)} %own_ref.1), channel_id=1, source_target_pairs={{0,1},{1,0},{2,3},{3,2},{4,5},{5,4},{6,7},{7,6},{8,9},{9,8},{10,11... | collective-permute-start | bytes 3145736 | tf_op jit(solution)/shard_map/ppermute | solution.py:117
  6.9 1.6 copy-start
  8.5 25.2 %copy-start.1 = (bf16[512,2048]{1,0:T(8,128)(2,1)S(1)}, bf16[512,2048]{1,0:T(8,128)(2,1)}, u32[]{:S(2)}) copy-start(bf16[512,2048]{1,0:T(8,128)(2,1)} %far_ref.3) | copy-start | bytes 6291460
  9.9 11.2 %collective-permute-start.1 = (bf16[512,1024]{1,0:T(8,128)(2,1)S(1)}, bf16[512,1024]{1,0:T(8,128)(2,1)}, u32[]{:S(2)}, u32[]{:S(2)}) collective-permute-start(bf16[512,1024]{1,0:T(8,128)(2,1)S(1)} %shard_map.84), channel_id=1, source_target_pairs={{0,1},{1,0},{2,3},{3,2},{4,5},{5,4},{6,7},{7,6},{8,9},{9,8},{10,11... | collective-permute-start | bytes 3145736 | tf_op jit(solution)/shard_map/ppermute | solution.py:118
  21.1 30.1 %all-to-all-start.1 = ((bf16[8,8,1792]{2,1,0:T(8,128)(2,1)}), bf16[8,8,1792]{2,1,0:T(8,128)(2,1)S(1)}, u32[]{:S(2)}, u32[]{:S(2)}) async-start(bf16[8,8,1792]{2,1,0:T(8,128)(2,1)} %bitcast.8), calls=%async_computation.1 | async-start | bytes 458752 | tf_op jit(solution)/shard_map/all_to_all | solution.py:95
  40.5 25.4 %collective-permute-start.3 = (bf16[1024,256]{1,0:T(8,128)(2,1)}, bf16[1024,256]{1,0:T(8,128)(2,1)S(1)}, u32[]{:S(2)}, u32[]{:S(2)}) collective-permute-start(bf16[1024,256]{1,0:T(8,128)(2,1)} %get-tuple-element.140), channel_id=1, source_target_pairs={{0,4},{4,8},{8,12},{12,0},{1,5},{5,9},{9,13},{13,1},{2,6},{6,10},{... | collective-permute-start | bytes 1572872 | tf_op jit(solution)/shard_map/ppermute | solution.py:125
  44.0 21.9 %collective-permute-start.4 = (bf16[1024,256]{1,0:T(8,128)(2,1)}, bf16[1024,256]{1,0:T(8,128)(2,1)S(1)}, u32[]{:S(2)}, u32[]{:S(2)}) collective-permute-start(bf16[1024,256]{1,0:T(8,128)(2,1)} %get-tuple-element.141), channel_id=1, source_target_pairs={{0,8},{4,12},{8,0},{12,4},{1,9},{5,13},{9,1},{13,5},{2,10},{6,14},... | collective-permute-start | bytes 1572872 | tf_op jit(solution)/shard_map/ppermute | solution.py:125
  46.8 23.8 %collective-permute-start.5 = (bf16[1024,256]{1,0:T(8,128)(2,1)S(1)}, bf16[1024,256]{1,0:T(8,128)(2,1)S(1)}, u32[]{:S(2)}, u32[]{:S(2)}) collective-permute-start(bf16[1024,256]{1,0:T(8,128)(2,1)S(1)} %get-tuple-element.142), channel_id=1, source_target_pairs={{0,12},{4,0},{8,4},{12,8},{1,13},{5,1},{9,5},{13,9},{2,14},{6,2},{... | collective-permute-start | bytes 1572872 | tf_op jit(solution)/shard_map/ppermute | solution.py:125
  51.2 14.7 %collective-permute-start.2 = (bf16[8,1792]{1,0:T(8,128)(2,1)S(1)}, bf16[8,1792]{1,0:T(8,128)(2,1)S(1)}, u32[]{:S(2)}, u32[]{:S(2)}) collective-permute-start(bf16[8,1792]{1,0:T(8,128)(2,1)S(1)} %reduce_sum.12), channel_id=1, source_target_pairs={{0,512},{512,0},{1,513},{513,1},{2,514},{514,2},{3,515},{515,3},{4... | collective-permute-start | bytes 86024 | tf_op jit(solution)/shard_map/ppermute | solution.py:134
  71.3 25.0 %all-to-all-start.2 = ((bf16[8,8,1792]{2,1,0:T(8,128)(2,1)}), bf16[8,8,1792]{2,1,0:T(8,128)(2,1)S(1)}, u32[]{:S(2)}, u32[]{:S(2)}) async-start(bf16[8,8,1792]{2,1,0:T(8,128)(2,1)} %broadcast_in_dim.6), calls=%async_computation.2 | async-start | bytes 458752 | tf_op jit(solution)/shard_map/all_to_all | solution.py:95
  81.3 1.9 %copy-start.3 = (f32[256,1792]{1,0:T(8,128)S(1)}, f32[256,1792]{1,0:T(8,128)}, u32[]{:S(2)}) copy-start(f32[256,1792]{1,0:T(8,128)} %param.8) | copy-start | bytes 5505028
  81.3 2.4 %copy-start.4 = (f32[256,1792]{1,0:T(8,128)S(1)}, f32[256,1792]{1,0:T(8,128)}, u32[]{:S(2)}) copy-start(f32[256,1792]{1,0:T(8,128)} %param.9) | copy-start | bytes 5505028
  81.5 1.0 copy-start.2
  96.4 63.0 %collective-permute-start.6 = (bf16[1024,128]{1,0:T(8,128)(2,1)S(1)}, bf16[1024,128]{1,0:T(8,128)(2,1)S(1)}, u32[]{:S(2)}, u32[]{:S(2)}) collective-permute-start(bf16[1024,128]{1,0:T(8,128)(2,1)S(1)} %slice.44), channel_id=1, source_target_pairs={{0,2},{2,0},{1,3},{3,1},{4,6},{6,4},{5,7},{7,5},{8,10},{10,8},{9,1... | collective-permute-start | bytes 786440 | tf_op jit(solution)/shard_map/ppermute | solution.py:148
  110.4 48.9 %slice-start = ((f32[1024,256]{1,0:T(8,128)}), f32[1024,128]{1,0:T(8,128)S(1)}, s32[]{:S(2)}) async-start(f32[1024,256]{1,0:T(8,128)} %copy-done.2), calls=%async_computation.3 | async-start | bytes 1048576 | tf_op jit(solution)/shard_map/slice | solution.py:146

commit v11 on v8

--- a/solution.py
+++ b/solution.py
@@ -140,9 +140,8 @@
         kv += part[piece].astype(f32)
     without = base - 0.567 * momentum
     mine, other, without = lax.optimization_barrier((kv[:, :LANES], kv[:, LANES:].astype(bf16), without))
-    gathered, other = lax.optimization_barrier((gathered, other))
     there = lax.ppermute(other, "h", swap)
-    gathered = gathered.reshape(per_x, width)
+    gathered = after(gathered, other).reshape(per_x, width)
     start = ((zo * n_zi + zi) * n_x + x) * own
 
     def own_rows(array):

time: 161 us -> 153 us (0.950)
  waiting for transfers between devices: 69.1 us -> 61.7 us
    ppermute x1, waiting for transfers between devices: 32.7 us -> 0.01 us  [shards(): there = lax.ppermute(other, 'h', swap)]
    all_to_all x3, waiting for transfers between devices: 19 us -> 44.2 us  [exchange(): return lax.all_to_all(array, axis, split_axis=0, concat_axis=0, tiled=True)]
  transfers between devices with their start and end apart: 10 -> 10, of which waited for: 5 -> 4; matrix products, arithmetic and copies ran while one was open for 4% -> 5% of each run, Pallas kernels for 5% -> 5%
where the time goes in v11:
time: 153 us; the launch traced here: 152 us
  waiting for transfers between devices  61.7 us (40%)
  starting transfers between devices  55.6 us (36%)
  blocking collectives  13.7 us (9%)
  Pallas kernels  8.16 us (5%)
  local copies, waits for them, and re-layouts  6.72 us (4%)
  other arithmetic  5.42 us (4%)
    all_to_all x3, waiting for transfers between devices, exchange(): return lax.all_to_all(array, axis, split_axis=0, concat_axis=0, tiled=True)  44.2 us
    all_to_all x3, starting transfers between devices, exchange(): return lax.all_to_all(array, axis, split_axis=0, concat_axis=0, tiled=True)  26.8 us
    all_gather x1, blocking collectives, finish(): outer_grad = lax.all_gather(gathered, 'x', axis=0, tiled=True)  13.7 us
    ppermute x1, waiting for transfers between devices, outer(): across = lax.ppermute(total, 'zo', swap)  12.7 us
    ppermute x1, starting transfers between devices, shards(): there = lax.ppermute(other, 'h', swap)  11.9 us
    ppermute x3, starting transfers between devices, shards(): lax.ppermute(part[step], 'y', shift('y', n_y, step))  10.6 us
    pallas_call x1, Pallas kernels, project(): pl.pallas_call(project_kernel, out_shape=[jax.ShapeDtypeStruct((rows, 2 *...  6.79 us
    ppermute x3, waiting for transfers between devices, shards(): lax.ppermute(part[step], 'y', shift('y', n_y, step))  4.73 us
  transfers between devices with their start and end apart: 10, of which 4 were waited for; matrix products, arithmetic and copies ran while one was open for 5% of the time, Pallas kernels for 5%

profile of v11, /device:TPU:296, one launch (start us, length us, event | category | flops | bytes accessed | tf_op | source)
XLA Modules:
  0.0 152.0 jit_solution(10540303518411544001)
XLA Ops:
  0.6 4.3 %all-to-all-start = ((bf16[4,64,1792]{2,1,0:T(8,128)(2,1)}), bf16[4,64,1792]{2,1,0:T(8,128)(2,1)}, u32[]{:S(2)}, u32[]{:S(2)}) async-start(bf16[4,64,1792]{2,1,0:T(8,128)(2,1)} %bitcast.27), calls=%async_computation | async-start | bytes 1835008 | tf_op jit(solution)/shard_map/all_to_all | solution.py:91
  4.9 1.9 %collective-permute-start = (bf16[1024,512]{1,0:T(8,128)(2,1)}, bf16[1024,512]{1,0:T(8,128)(2,1)}, u32[]{:S(2)}, u32[]{:S(2)}) collective-permute-start(bf16[1024,512]{1,0:T(8,128)(2,1)} %own_ref.1), channel_id=1, source_target_pairs={{0,1},{1,0},{2,3},{3,2},{4,5},{5,4},{6,7},{7,6},{8,9},{9,8},{10,11... | collective-permute-start | bytes 3145736 | tf_op jit(solution)/shard_map/ppermute | solution.py:113
  6.9 0.1 pad_add_fusion.place_ref
  6.9 0.0 copy-start
  6.9 1.6 %copy-done = bf16[512,2048]{1,0:T(8,128)(2,1)S(1)} copy-done((bf16[512,2048]{1,0:T(8,128)(2,1)S(1)}, bf16[512,2048]{1,0:T(8,128)(2,1)}, u32[]{:S(2)}) %copy-start) | copy-done | bytes 2097176
  8.5 0.0 copy-start.1
  8.5 1.4 shard_map.84
  9.9 2.4 %collective-permute-start.1 = (bf16[512,1024]{1,0:T(8,128)(2,1)S(1)}, bf16[512,1024]{1,0:T(8,128)(2,1)}, u32[]{:S(2)}, u32[]{:S(2)}) collective-permute-start(bf16[512,1024]{1,0:T(8,128)(2,1)S(1)} %shard_map.84), channel_id=1, source_target_pairs={{0,1},{1,0},{2,3},{3,2},{4,5},{5,4},{6,7},{7,6},{8,9},{9,8},{10,11... | collective-permute-start | bytes 3145736 | tf_op jit(solution)/shard_map/ppermute | solution.py:114
  12.3 6.6 %all-to-all-done = bf16[4,64,1792]{2,1,0:T(8,128)(2,1)} async-done(((bf16[4,64,1792]{2,1,0:T(8,128)(2,1)}), bf16[4,64,1792]{2,1,0:T(8,128)(2,1)}, u32[]{:S(2)}, u32[]{:S(2)}) %all-to-all-start) | async-done | bytes 917536 | tf_op jit(solution)/shard_map/all_to_all | solution.py:91
  18.9 2.2 %fusion.1 = bf16[64,1792]{1,0:T(8,128)(2,1)} fusion(f32[256,1792]{1,0:T(8,128)} %param.8, s32[]{:T(128)S(6)} %select_n.11, bf16[4,64,1792]{2,1,0:T(8,128)(2,1)} %all-to-all-done), kind=kLoop, calls=%fused_computation.9 | loop fusion | flops 1261568 | bytes 1376260 | tf_op jit(solution)/shard_map/convert_element_type | solution.py:110
  21.1 0.0 collective-permute-done.sibling_ref
  21.1 0.0 collective-permute-done.1.packed_ref
  21.1 12.6 %all-to-all-start.1 = ((bf16[8,8,1792]{2,1,0:T(8,128)(2,1)}), bf16[8,8,1792]{2,1,0:T(8,128)(2,1)S(1)}, u32[]{:S(2)}, u32[]{:S(2)}) async-start(bf16[8,8,1792]{2,1,0:T(8,128)(2,1)} %bitcast.8), calls=%async_computation.1 | async-start | bytes 458752 | tf_op jit(solution)/shard_map/all_to_all | solution.py:91
  33.7 0.0 copy-done.1
  33.7 6.8 %shard_map.85 = (bf16[1024,256]{1,0:T(8,128)(2,1)S(1)}, bf16[1024,256]{1,0:T(8,128)(2,1)}, bf16[1024,256]{1,0:T(8,128)(2,1)}, bf16[1024,256]{1,0:T(8,128)(2,1)S(1)}) custom-call(s32[3]{0:T(128)S(1)} %pad_add_fusion.place_ref, bf16[1024,512]{1,0:T(8,128)(2,1)} %own_ref.1, bf16[1024,512]{1,0:T(8,128)(2,1)} %collective-permute-done.sibling_ref, ...), custom_call_target="tpu_custom_call" | custom-call | flops 2147483648 | bytes 6291456 | tf_op jit(solution)/shard_map/pallas_call | solution.py:60
  40.5 3.5 %collective-permute-start.3 = (bf16[1024,256]{1,0:T(8,128)(2,1)}, bf16[1024,256]{1,0:T(8,128)(2,1)S(1)}, u32[]{:S(2)}, u32[]{:S(2)}) collective-permute-start(bf16[1024,256]{1,0:T(8,128)(2,1)} %get-tuple-element.139), channel_id=1, source_target_pairs={{0,4},{4,8},{8,12},{12,0},{1,5},{5,9},{9,13},{13,1},{2,6},{6,10},{... | collective-permute-start | bytes 1572872 | tf_op jit(solution)/shard_map/ppermute | solution.py:121
  44.0 2.8 %collective-permute-start.4 = (bf16[1024,256]{1,0:T(8,128)(2,1)}, bf16[1024,256]{1,0:T(8,128)(2,1)S(1)}, u32[]{:S(2)}, u32[]{:S(2)}) collective-permute-start(bf16[1024,256]{1,0:T(8,128)(2,1)} %get-tuple-element.140), channel_id=1, source_target_pairs={{0,8},{4,12},{8,0},{12,4},{1,9},{5,13},{9,1},{13,5},{2,10},{6,14},... | collective-permute-start | bytes 1572872 | tf_op jit(solution)/shard_map/ppermute | solution.py:121
  46.9 4.3 %collective-permute-start.5 = (bf16[1024,256]{1,0:T(8,128)(2,1)S(1)}, bf16[1024,256]{1,0:T(8,128)(2,1)S(1)}, u32[]{:S(2)}, u32[]{:S(2)}) collective-permute-start(bf16[1024,256]{1,0:T(8,128)(2,1)S(1)} %get-tuple-element.141), channel_id=1, source_target_pairs={{0,12},{4,0},{8,4},{12,8},{1,13},{5,1},{9,5},{13,9},{2,14},{6,2},{... | collective-permute-start | bytes 1572872 | tf_op jit(solution)/shard_map/ppermute | solution.py:121
  51.2 0.0 all-to-all-done.1
  51.3 1.9 %collective-permute-start.2 = (bf16[8,1792]{1,0:T(8,128)(2,1)S(1)}, bf16[8,1792]{1,0:T(8,128)(2,1)S(1)}, u32[]{:S(2)}, u32[]{:S(2)}) collective-permute-start(bf16[8,1792]{1,0:T(8,128)(2,1)S(1)} %reduce_sum.12), channel_id=1, source_target_pairs={{0,512},{512,0},{1,513},{513,1},{2,514},{514,2},{3,515},{515,3},{4... | collective-permute-start | bytes 86024 | tf_op jit(solution)/shard_map/ppermute | solution.py:130
  53.2 12.7 %collective-permute-done.2 = bf16[8,1792]{1,0:T(8,128)(2,1)S(1)} collective-permute-done((bf16[8,1792]{1,0:T(8,128)(2,1)S(1)}, bf16[8,1792]{1,0:T(8,128)(2,1)S(1)}, u32[]{:S(2)}, u32[]{:S(2)}) %collective-permute-start.2) | collective-permute-done | bytes 28704 | tf_op jit(solution)/shard_map/ppermute | solution.py:130
  65.9 0.0 collective-permute-done.3
  65.9 0.0 collective-permute-done.4
  66.0 4.7 %collective-permute-done.5 = bf16[1024,256]{1,0:T(8,128)(2,1)S(1)} collective-permute-done((bf16[1024,256]{1,0:T(8,128)(2,1)S(1)}, bf16[1024,256]{1,0:T(8,128)(2,1)S(1)}, u32[]{:S(2)}, u32[]{:S(2)}) %collective-permute-start.5) | collective-permute-done | bytes 524320 | tf_op jit(solution)/shard_map/ppermute | solution.py:121
  70.7 0.7 broadcast_in_dim.6
  71.4 9.9 %all-to-all-start.2 = ((bf16[8,8,1792]{2,1,0:T(8,128)(2,1)}), bf16[8,8,1792]{2,1,0:T(8,128)(2,1)S(1)}, u32[]{:S(2)}, u32[]{:S(2)}) async-start(bf16[8,8,1792]{2,1,0:T(8,128)(2,1)} %broadcast_in_dim.6), calls=%async_computation.2 | async-start | bytes 458752 | tf_op jit(solution)/shard_map/all_to_all | solution.py:91
  81.3 0.0 copy-start.3
  81.3 0.0 copy-start.4
  81.3 0.2 convert_add_fusion.1
  81.5 0.0 copy-start.2
  81.5 1.0 copy-done.2
  82.6 0.6 copy-done.3
  83.2 0.6 copy-done.4
  83.7 0.2 multiply_subtract_fusion
  83.9 11.9 %collective-permute-start.6 = (bf16[1024,128]{1,0:T(8,128)(2,1)S(1)}, bf16[1024,128]{1,0:T(8,128)(2,1)S(1)}, u32[]{:S(2)}, u32[]{:S(2)}) collective-permute-start(bf16[1024,128]{1,0:T(8,128)(2,1)S(1)} %slice.44), channel_id=1, source_target_pairs={{0,2},{2,0},{1,3},{3,1},{4,6},{6,4},{5,7},{7,5},{8,10},{10,8},{9,1... | collective-permute-start | bytes 786440 | tf_op jit(solution)/shard_map/ppermute | solution.py:143
  95.9 37.6 %all-to-all-done.2 = bf16[8,8,1792]{2,1,0:T(8,128)(2,1)S(1)} async-done(((bf16[8,8,1792]{2,1,0:T(8,128)(2,1)}), bf16[8,8,1792]{2,1,0:T(8,128)(2,1)S(1)}, u32[]{:S(2)}, u32[]{:S(2)}) %all-to-all-start.2) | async-done | bytes 229408 | tf_op jit(solution)/shard_map/all_to_all | solution.py:91
  133.5 1.0 broadcast_in_dim.7
  134.5 0.6 broadcast.19
  135.1 0.6 broadcast.19.clone
  135.7 0.0 slice-start
  135.7 15.6 %while.18 = (s32[]{:T(128)}, bf16[64,1792]{1,0:T(8,128)(2,1)S(1)}, bf16[256,1792]{1,0:T(8,128)(2,1)}, f32[4,1792]{1,0:T(4,128)}, f32[4,1792]{1,0:T(4,128)}, /*in...) while((s32[]{:T(128)}, bf16[64,1792]{1,0:T(8,128)(2,1)S(1)}, ...), condition=%wide.region_2.0_spmd, body=%wide.region_1.0_spmd.sunk | while | flops 1985538 | bytes 5404785 | solution.py:159
  135.7 13.7 %all_gather.6 = bf16[256,1792]{1,0:T(8,128)(2,1)S(1)} all-gather(bf16[64,1792]{1,0:T(8,128)(2,1)S(1)} %get-tuple-element.252), channel_id=1, replica_groups=mesh['zo'=2,'zi'=8,'x'=4,'y'=4,'h'=2,'c'=2] {'x'}, dimensions={0}, use_global_device_ids=true | all-gather | bytes 1146880 | tf_op jit(solution)/shard_map/while/body/all_gather | solution.py:151
  149.4 0.1 neg.11
  149.4 1.2 subtract_convert_fusion.2
  150.6 0.6 convert_add_fusion.6
  151.3 0.0 collective-permute-done.6
  151.3 0.0 slice-done
  151.3 0.8 add_convert_fusion
  (5 shorter events, 0.1 us)
Async XLA Ops:
  0.6 18.3 %all-to-all-start = ((bf16[4,64,1792]{2,1,0:T(8,128)(2,1)}), bf16[4,64,1792]{2,1,0:T(8,128)(2,1)}, u32[]{:S(2)}, u32[]{:S(2)}) async-start(bf16[4,64,1792]{2,1,0:T(8,128)(2,1)} %bitcast.27), calls=%async_computation | async-start | bytes 1835008 | tf_op jit(solution)/shard_map/all_to_all | solution.py:91
  4.9 16.2 %collective-permute-start = (bf16[1024,512]{1,0:T(8,128)(2,1)}, bf16[1024,512]{1,0:T(8,128)(2,1)}, u32[]{:S(2)}, u32[]{:S(2)}) collective-permute-start(bf16[1024,512]{1,0:T(8,128)(2,1)} %own_ref.1), channel_id=1, source_target_pairs={{0,1},{1,0},{2,3},{3,2},{4,5},{5,4},{6,7},{7,6},{8,9},{9,8},{10,11... | collective-permute-start | bytes 3145736 | tf_op jit(solution)/shard_map/ppermute | solution.py:113
  6.9 1.6 %copy-start = (bf16[512,2048]{1,0:T(8,128)(2,1)S(1)}, bf16[512,2048]{1,0:T(8,128)(2,1)}, u32[]{:S(2)}) copy-start(bf16[512,2048]{1,0:T(8,128)(2,1)} %far_ref.3) | copy-start | bytes 6291460
  8.5 25.2 %copy-start.1 = (bf16[512,2048]{1,0:T(8,128)(2,1)S(1)}, bf16[512,2048]{1,0:T(8,128)(2,1)}, u32[]{:S(2)}) copy-start(bf16[512,2048]{1,0:T(8,128)(2,1)} %far_ref.3) | copy-start | bytes 6291460
  9.9 11.2 %collective-permute-start.1 = (bf16[512,1024]{1,0:T(8,128)(2,1)S(1)}, bf16[512,1024]{1,0:T(8,128)(2,1)}, u32[]{:S(2)}, u32[]{:S(2)}) collective-permute-start(bf16[512,1024]{1,0:T(8,128)(2,1)S(1)} %shard_map.84), channel_id=1, source_target_pairs={{0,1},{1,0},{2,3},{3,2},{4,5},{5,4},{6,7},{7,6},{8,9},{9,8},{10,11... | collective-permute-start | bytes 3145736 | tf_op jit(solution)/shard_map/ppermute | solution.py:114
  21.1 30.1 %all-to-all-start.1 = ((bf16[8,8,1792]{2,1,0:T(8,128)(2,1)}), bf16[8,8,1792]{2,1,0:T(8,128)(2,1)S(1)}, u32[]{:S(2)}, u32[]{:S(2)}) async-start(bf16[8,8,1792]{2,1,0:T(8,128)(2,1)} %bitcast.8), calls=%async_computation.1 | async-start | bytes 458752 | tf_op jit(solution)/shard_map/all_to_all | solution.py:91
  40.5 25.4 %collective-permute-start.3 = (bf16[1024,256]{1,0:T(8,128)(2,1)}, bf16[1024,256]{1,0:T(8,128)(2,1)S(1)}, u32[]{:S(2)}, u32[]{:S(2)}) collective-permute-start(bf16[1024,256]{1,0:T(8,128)(2,1)} %get-tuple-element.139), channel_id=1, source_target_pairs={{0,4},{4,8},{8,12},{12,0},{1,5},{5,9},{9,13},{13,1},{2,6},{6,10},{... | collective-permute-start | bytes 1572872 | tf_op jit(solution)/shard_map/ppermute | solution.py:121
  44.0 21.9 %collective-permute-start.4 = (bf16[1024,256]{1,0:T(8,128)(2,1)}, bf16[1024,256]{1,0:T(8,128)(2,1)S(1)}, u32[]{:S(2)}, u32[]{:S(2)}) collective-permute-start(bf16[1024,256]{1,0:T(8,128)(2,1)} %get-tuple-element.140), channel_id=1, source_target_pairs={{0,8},{4,12},{8,0},{12,4},{1,9},{5,13},{9,1},{13,5},{2,10},{6,14},... | collective-permute-start | bytes 1572872 | tf_op jit(solution)/shard_map/ppermute | solution.py:121
  46.9 23.8 %collective-permute-start.5 = (bf16[1024,256]{1,0:T(8,128)(2,1)S(1)}, bf16[1024,256]{1,0:T(8,128)(2,1)S(1)}, u32[]{:S(2)}, u32[]{:S(2)}) collective-permute-start(bf16[1024,256]{1,0:T(8,128)(2,1)S(1)} %get-tuple-element.141), channel_id=1, source_target_pairs={{0,12},{4,0},{8,4},{12,8},{1,13},{5,1},{9,5},{13,9},{2,14},{6,2},{... | collective-permute-start | bytes 1572872 | tf_op jit(solution)/shard_map/ppermute | solution.py:121
  51.3 14.7 %collective-permute-start.2 = (bf16[8,1792]{1,0:T(8,128)(2,1)S(1)}, bf16[8,1792]{1,0:T(8,128)(2,1)S(1)}, u32[]{:S(2)}, u32[]{:S(2)}) collective-permute-start(bf16[8,1792]{1,0:T(8,128)(2,1)S(1)} %reduce_sum.12), channel_id=1, source_target_pairs={{0,512},{512,0},{1,513},{513,1},{2,514},{514,2},{3,515},{515,3},{4... | collective-permute-start | bytes 86024 | tf_op jit(solution)/shard_map/ppermute | solution.py:130
  71.4 62.1 %all-to-all-start.2 = ((bf16[8,8,1792]{2,1,0:T(8,128)(2,1)}), bf16[8,8,1792]{2,1,0:T(8,128)(2,1)S(1)}, u32[]{:S(2)}, u32[]{:S(2)}) async-start(bf16[8,8,1792]{2,1,0:T(8,128)(2,1)} %broadcast_in_dim.6), calls=%async_computation.2 | async-start | bytes 458752 | tf_op jit(solution)/shard_map/all_to_all | solution.py:91
  81.3 1.9 %copy-start.3 = (f32[256,1792]{1,0:T(8,128)S(1)}, f32[256,1792]{1,0:T(8,128)}, u32[]{:S(2)}) copy-start(f32[256,1792]{1,0:T(8,128)} %param.8) | copy-start | bytes 5505028
  81.3 2.4 %copy-start.4 = (f32[256,1792]{1,0:T(8,128)S(1)}, f32[256,1792]{1,0:T(8,128)}, u32[]{:S(2)}) copy-start(f32[256,1792]{1,0:T(8,128)} %param.9) | copy-start | bytes 5505028
  81.5 1.0 copy-start.2
  83.9 67.3 %collective-permute-start.6 = (bf16[1024,128]{1,0:T(8,128)(2,1)S(1)}, bf16[1024,128]{1,0:T(8,128)(2,1)S(1)}, u32[]{:S(2)}, u32[]{:S(2)}) collective-permute-start(bf16[1024,128]{1,0:T(8,128)(2,1)S(1)} %slice.44), channel_id=1, source_target_pairs={{0,2},{2,0},{1,3},{3,1},{4,6},{6,4},{5,7},{7,5},{8,10},{10,8},{9,1... | collective-permute-start | bytes 786440 | tf_op jit(solution)/shard_map/ppermute | solution.py:143
  135.7 15.6 %slice-start = ((f32[1024,256]{1,0:T(8,128)}), f32[1024,128]{1,0:T(8,128)S(1)}, s32[]{:S(2)}) async-start(f32[1024,256]{1,0:T(8,128)} %copy-done.2), calls=%async_computation.3 | async-start | bytes 1048576 | tf_op jit(solution)/shard_map/slice | solution.py:142
